TPU v7x, 32 devices: a whole 2x2x4 slice. The times are simulated.
32 devices in a mesh: fsdp: 4 (over y, x), ctx: 8 (over z, core).
Axes of the slice: x: 2, y: 2, z: 4, core: 2. Of those that a mesh axis runs over, the one named last changes fastest.
Arguments:
- tokens: bfloat16 [4096, 2048], P(('fsdp', 'ctx')), may hold values from -6 to 6
- cotangent: bfloat16 [4096, 2048], P(('fsdp', 'ctx')), may hold values from -6 to 6
- doc_lengths: int32 [4, 4], P('fsdp'), may hold values from 1 to 1021, as said below
- gain_attn: bfloat16 [2048], P(('fsdp', 'ctx')), may hold values from 0.5 to 1.5
- w_query: bfloat16 [2048, 2048], P(('fsdp', 'ctx')), may hold values from -0.125 to 0.125
- w_key: bfloat16 [2048, 2048], P(('fsdp', 'ctx')), may hold values from -0.125 to 0.125
- w_value: bfloat16 [2048, 2048], P(('fsdp', 'ctx')), may hold values from -0.125 to 0.125
- w_out: bfloat16 [2048, 2048], P(('fsdp', 'ctx')), may hold values from -1 to 1
- gain_mlp: bfloat16 [2048], P(('fsdp', 'ctx')), may hold values from 0.5 to 1.5
- w_gate: bfloat16 [2048, 8192], P(('fsdp', 'ctx')), may hold values from -0.125 to 0.125
- w_up: bfloat16 [2048, 8192], P(('fsdp', 'ctx')), may hold values from -0.125 to 0.125
- w_down: bfloat16 [2048, 8192], P(('fsdp', 'ctx')), may hold values from -0.0625 to 0.0625
Outputs:
- layer_out: bfloat16 [4096, 2048], P(('fsdp', 'ctx'))
- grad_tokens: float32 [4096, 2048], P(('fsdp', 'ctx'))
- grad_gain_attn: float32 [2048], P(('fsdp', 'ctx'))
- grad_query: float32 [2048, 2048], P(('fsdp', 'ctx'))
- grad_key: float32 [2048, 2048], P(('fsdp', 'ctx'))
- grad_value: float32 [2048, 2048], P(('fsdp', 'ctx'))
- grad_out: float32 [2048, 2048], P(('fsdp', 'ctx'))
- grad_gain_mlp: float32 [2048], P(('fsdp', 'ctx'))
- grad_gate: float32 [2048, 8192], P(('fsdp', 'ctx'))
- grad_up: float32 [2048, 8192], P(('fsdp', 'ctx'))
- grad_down: float32 [2048, 8192], P(('fsdp', 'ctx'))
Inputs may be any that keep to these rules, and one draw needn't show every extreme that they name: `doc_lengths`: row g holds the lengths of the 4 documents packed in order into the g-th group of 1024 rows of tokens; each row sums to 1024.
All inputs are finite; a program needn't handle non-finite values.
Results may differ from a plain program's by a relative error of at most 0.014.
Values may be sent and summed in bfloat16 or wider, within the bound.
No kernel may reach another device: no remote copies, remote signals or barrier semaphores. Data moves between devices by JAX's collectives and lax.ppermute only.
A program may use at most 320 MiB of HBM per device.

v0:
```python
import math

import jax
import jax.numpy as jnp
from jax import lax
from jax.sharding import PartitionSpec as P

H = 32
HD = 64


EPSILON = 1e-05
ROPE_BASE = 130000.0


def doc_layout(doc_sizes, position):
    doc_ends = jnp.cumsum(doc_sizes)
    doc_starts = doc_ends - doc_sizes
    doc_index = jnp.sum((position[:, None] >= doc_ends[None, :]).astype(jnp.int32), axis=1)
    numbers = jnp.arange(doc_sizes.shape[0], dtype=jnp.int32)
    doc_match = (doc_index[:, None] == numbers[None, :]).astype(jnp.int32)
    begins = jnp.sum(doc_match * doc_starts[None, :], axis=1)
    return (doc_index, position - begins)


def rotate(values, places, direction, head_size):
    half_size = head_size // 2
    inv_freq = ROPE_BASE ** (-2.0 * jnp.arange(half_size).astype(values.dtype) / head_size)
    angles = places.astype(values.dtype)[:, None] * inv_freq[None, :]
    cosine = jnp.cos(angles)[:, None, :]
    sine_part = direction * jnp.sin(angles)[:, None, :]
    shaped = values.reshape(values.shape[0], -1, head_size)
    lower_half = shaped[..., :half_size]
    upper_half = shaped[..., half_size:]
    turned = jnp.concatenate(
        [
            lower_half * cosine - upper_half * sine_part,
            upper_half * cosine + lower_half * sine_part,
        ],
        axis=-1,
    )
    return turned.reshape(values.shape)


def contract_back(left_rows, right_rows):
    return lax.dot_general(
        left_rows, right_rows, (((1,), (1,)), ((), ())), preferred_element_type=jnp.float32
    )


def tokens_first(left_rows, right_rows):
    return lax.dot_general(
        left_rows, right_rows, (((0,), (0,)), ((), ())), preferred_element_type=jnp.float32
    )


def norm_back(d_normed, unit_rows, inverse, gain_f):
    d_unit = d_normed * gain_f
    return inverse * (d_unit - unit_rows * jnp.mean(d_unit * unit_rows, axis=-1, keepdims=True))


def reorder_blocks(matrix, outer, inner):
    columns = matrix.shape[1]
    shaped = matrix.reshape(outer, inner, -1, columns)
    return jnp.swapaxes(shaped, 0, 1).reshape(-1, columns)


def swiglu_parts(normed_rows, gate_cols, up_cols):
    gate = jnp.dot(normed_rows, gate_cols, preferred_element_type=jnp.float32)
    up_proj = jnp.dot(normed_rows, up_cols, preferred_element_type=jnp.float32)
    sigmoid_gate = jax.nn.sigmoid(gate)
    silu_gate = gate * sigmoid_gate
    hidden = (silu_gate * up_proj).astype(jnp.bfloat16)
    return (gate, up_proj, sigmoid_gate, silu_gate, hidden)


def swiglu_back(back_rows, down_cols, gate, up_proj, sigmoid_gate, silu_gate):
    d_hidden = jnp.dot(back_rows, down_cols, preferred_element_type=jnp.float32)
    d_gate = (d_hidden * up_proj * sigmoid_gate * (1.0 + gate * (1.0 - sigmoid_gate))).astype(
        jnp.bfloat16
    )
    d_up = (d_hidden * silu_gate).astype(jnp.bfloat16)
    return (d_gate, d_up)


def local(
    tokens,
    cotangent,
    doc_lengths,
    gain_attn,
    w_query,
    w_key,
    w_value,
    w_out,
    gain_mlp,
    w_gate,
    w_up,
    w_down,
):
    row_count = tokens.shape[0]
    feature_count = tokens.shape[1]
    shard_count = lax.axis_size("ctx")
    fsdp_count = lax.axis_size("fsdp")
    group_count = row_count * shard_count
    factor = HD ** (-0.5)
    first_row = lax.axis_index("ctx") * row_count
    doc_sizes = doc_lengths[0]
    position = first_row + jnp.arange(row_count, dtype=jnp.int32)
    query_doc, places = doc_layout(doc_sizes, position)
    gain_a, gain_m, full_query, full_key, full_value, full_out = (
        lax.all_gather(gain_attn, ("fsdp", "ctx"), axis=0, tiled=True),
        lax.all_gather(gain_mlp, ("fsdp", "ctx"), axis=0, tiled=True),
        lax.all_gather(w_query, ("fsdp", "ctx"), axis=0, tiled=True),
        lax.all_gather(w_key, ("fsdp", "ctx"), axis=0, tiled=True),
        lax.all_gather(w_value, ("fsdp", "ctx"), axis=0, tiled=True),
        lax.all_gather(w_out, ("fsdp", "ctx"), axis=0, tiled=True),
    )
    values_f = tokens.astype(jnp.float32)
    inverse = lax.rsqrt(jnp.mean(values_f * values_f, axis=-1, keepdims=True) + EPSILON)
    unit_rows = values_f * inverse
    normed = (unit_rows * gain_a.astype(jnp.float32)).astype(jnp.bfloat16)
    query_proj = jnp.dot(normed, full_query, preferred_element_type=jnp.float32)
    key_proj = jnp.dot(normed, full_key, preferred_element_type=jnp.float32)
    value_proj = jnp.dot(normed, full_value, preferred_element_type=jnp.float32)
    query_rot = rotate(query_proj, places, 1.0, HD).astype(jnp.bfloat16)
    key_rot = rotate(key_proj, places, 1.0, HD).astype(jnp.bfloat16)
    value_low = value_proj.astype(jnp.bfloat16)
    query_heads = query_rot.reshape(row_count, H, HD)

    def attend(running, key_block, value_block, key_position):
        row_max, row_sum, weighted = running
        key_doc, unused = doc_layout(doc_sizes, key_position)
        raw_scores = (
            jnp.einsum(
                "qhd,khd->hqk",
                query_heads,
                key_block.reshape(-1, H, HD),
                preferred_element_type=jnp.float32,
            )
            * factor
        )
        allowed = (query_doc[:, None] == key_doc[None, :]) & (
            key_position[None, :] <= position[:, None]
        )
        scores = jnp.where(allowed[None], raw_scores, -jnp.inf)
        new_max = jnp.maximum(row_max, jnp.max(scores, axis=-1))
        shrink = jnp.exp(row_max - new_max)
        weights = jnp.exp(scores - new_max[:, :, None])
        row_sum = row_sum * shrink + jnp.sum(weights, axis=-1)
        weighted = weighted * shrink.T[:, :, None] + jnp.einsum(
            "hqk,khd->qhd",
            weights,
            value_block.reshape(-1, H, HD).astype(jnp.float32),
            precision=lax.Precision.HIGHEST,
        )
        return (new_max, row_sum, weighted)

    start_state = (
        jnp.full((H, row_count), -1e30, jnp.float32),
        jnp.zeros((H, row_count), jnp.float32),
        jnp.zeros((row_count, H, HD), jnp.float32),
    )
    running = start_state
    key_piece = lax.all_gather(key_rot, "ctx", axis=0, tiled=True)
    value_piece = lax.all_gather(value_low, "ctx", axis=0, tiled=True)
    amount = key_piece.shape[0]
    fold_block_rows = row_count * math.gcd(amount // row_count, max(1, 512 // row_count))
    splits = amount // fold_block_rows
    key_position = jnp.arange(amount, dtype=jnp.int32)

    def advance(carried, pieces_in):
        return (attend(carried, pieces_in[0], pieces_in[1], pieces_in[2]), None)

    running, unused = lax.scan(
        advance,
        running,
        (
            key_piece.reshape(splits, fold_block_rows, -1),
            value_piece.reshape(splits, fold_block_rows, -1),
            key_position.reshape(splits, fold_block_rows),
        ),
    )
    row_max, row_sum, weighted = running
    log_total = row_max + jnp.log(row_sum)
    attended = (weighted / row_sum.T[:, :, None]).reshape(row_count, feature_count)
    attended_low = attended.astype(jnp.bfloat16)
    mixed = values_f + contract_back(attended_low, full_out)
    inverse_mlp = lax.rsqrt(jnp.mean(mixed * mixed, axis=-1, keepdims=True) + EPSILON)
    unit_mlp = mixed * inverse_mlp
    normed_mlp = (unit_mlp * gain_m.astype(jnp.float32)).astype(jnp.bfloat16)
    slab_gate, slab_up, slab_down = (
        lax.all_gather(w_gate, "fsdp", axis=0, tiled=True),
        lax.all_gather(w_up, "fsdp", axis=0, tiled=True),
        lax.all_gather(w_down, "fsdp", axis=0, tiled=True),
    )
    turned_gate, turned_up, turned_down = (
        lax.all_to_all(slab_gate, "ctx", split_axis=1, concat_axis=0, tiled=True),
        lax.all_to_all(slab_up, "ctx", split_axis=1, concat_axis=0, tiled=True),
        lax.all_to_all(slab_down, "ctx", split_axis=1, concat_axis=0, tiled=True),
    )
    col_gate = reorder_blocks(turned_gate, shard_count, fsdp_count)
    col_up = reorder_blocks(turned_up, shard_count, fsdp_count)
    col_down = reorder_blocks(turned_down, shard_count, fsdp_count)
    normed_group, back_group = (
        lax.all_gather(normed_mlp, "ctx", axis=0, tiled=True),
        lax.all_gather(cotangent, "ctx", axis=0, tiled=True),
    )
    gate, up_proj, sigmoid_gate, silu_gate, hidden = swiglu_parts(normed_group, col_gate, col_up)
    branch_out = lax.psum_scatter(
        contract_back(hidden, col_down).astype(jnp.bfloat16), "ctx", scatter_dimension=0, tiled=True
    ).astype(jnp.float32)
    layer_out = (mixed + branch_out).astype(jnp.bfloat16)
    d_gate, d_up = swiglu_back(back_group, col_down, gate, up_proj, sigmoid_gate, silu_gate)
    d_normed_mlp = lax.psum_scatter(
        contract_back(d_gate, col_gate) + contract_back(d_up, col_up),
        "ctx",
        scatter_dimension=0,
        tiled=True,
    )
    part_gate = reorder_blocks(tokens_first(normed_group, d_gate), fsdp_count, shard_count)
    part_up = reorder_blocks(tokens_first(normed_group, d_up), fsdp_count, shard_count)
    part_down = reorder_blocks(tokens_first(back_group, hidden), fsdp_count, shard_count)
    moved_gate, moved_up, moved_down = (
        lax.all_to_all(
            part_gate.astype(jnp.bfloat16), "ctx", split_axis=0, concat_axis=1, tiled=True
        ).astype(part_gate.dtype),
        lax.all_to_all(
            part_up.astype(jnp.bfloat16), "ctx", split_axis=0, concat_axis=1, tiled=True
        ).astype(part_up.dtype),
        lax.all_to_all(
            part_down.astype(jnp.bfloat16), "ctx", split_axis=0, concat_axis=1, tiled=True
        ).astype(part_down.dtype),
    )
    grad_gate, grad_up, grad_down = (
        lax.psum_scatter(
            moved_gate.astype(jnp.bfloat16), "fsdp", scatter_dimension=0, tiled=True
        ).astype(jnp.float32),
        lax.psum_scatter(
            moved_up.astype(jnp.bfloat16), "fsdp", scatter_dimension=0, tiled=True
        ).astype(jnp.float32),
        lax.psum_scatter(
            moved_down.astype(jnp.bfloat16), "fsdp", scatter_dimension=0, tiled=True
        ).astype(jnp.float32),
    )
    gain_mlp_term = jnp.sum(d_normed_mlp * unit_mlp, axis=0)
    d_mixed = cotangent.astype(jnp.float32) + norm_back(
        d_normed_mlp, unit_mlp, inverse_mlp, gain_m.astype(jnp.float32)
    )
    d_mixed_low = d_mixed.astype(jnp.bfloat16)
    d_out_low = jnp.dot(d_mixed_low, full_out, preferred_element_type=jnp.float32).astype(
        jnp.bfloat16
    )
    d_out_heads = d_out_low.reshape(row_count, H, HD)
    d_out_f = d_out_heads.astype(jnp.float32)
    delta = jnp.sum(d_out_f * attended.reshape(row_count, H, HD), axis=-1).T
    key_all, value_all = (
        lax.all_gather(key_rot, "ctx", axis=0, tiled=True),
        lax.all_gather(value_low, "ctx", axis=0, tiled=True),
    )
    block_rows = min(512, group_count)
    lowest = position[0] - places[0]
    begin_block = lowest // block_rows
    end_block = (first_row + row_count - 1) // block_rows + 1

    def back_block(block_index, running):
        d_query, d_keys, d_values = running
        offset = block_index * block_rows
        key_block = lax.dynamic_slice_in_dim(key_all, offset, block_rows, 0)
        value_block = lax.dynamic_slice_in_dim(value_all, offset, block_rows, 0)
        key_position = offset + jnp.arange(block_rows, dtype=jnp.int32)
        key_doc, unused = doc_layout(doc_sizes, key_position)
        key_heads = key_block.reshape(block_rows, H, HD)
        raw_scores = (
            jnp.einsum("qhd,khd->hqk", query_heads, key_heads, preferred_element_type=jnp.float32)
            * factor
        )
        allowed = (query_doc[:, None] == key_doc[None, :]) & (
            key_position[None, :] <= position[:, None]
        )
        weights = jnp.where(allowed[None], jnp.exp(raw_scores - log_total[:, :, None]), 0.0)
        d_weights = jnp.einsum(
            "qhd,khd->hqk",
            d_out_heads,
            value_block.reshape(block_rows, H, HD),
            preferred_element_type=jnp.float32,
        )
        d_scores = (weights * (d_weights - delta[:, :, None])).astype(jnp.bfloat16)
        d_query = d_query + jnp.einsum(
            "hqk,khd->qhd", d_scores, key_heads, preferred_element_type=jnp.float32
        )
        key_part = (
            jnp.einsum("hqk,qhd->khd", d_scores, query_heads, preferred_element_type=jnp.float32)
            * factor
        ).reshape(block_rows, feature_count)
        value_part = jnp.einsum(
            "hqk,qhd->khd", weights, d_out_f, precision=lax.Precision.HIGHEST
        ).reshape(block_rows, feature_count)
        d_keys = lax.dynamic_update_slice_in_dim(
            d_keys, lax.dynamic_slice_in_dim(d_keys, offset, block_rows, 0) + key_part, offset, 0
        )
        d_values = lax.dynamic_update_slice_in_dim(
            d_values,
            lax.dynamic_slice_in_dim(d_values, offset, block_rows, 0) + value_part,
            offset,
            0,
        )
        return (d_query, d_keys, d_values)

    zero_group = jnp.zeros((group_count, feature_count), jnp.float32)
    d_query, d_keys, d_values = lax.fori_loop(
        begin_block,
        end_block,
        back_block,
        (jnp.zeros((row_count, H, HD), jnp.float32), zero_group, zero_group),
    )
    key_grad, value_grad = (
        lax.psum_scatter(d_keys, "ctx", scatter_dimension=0, tiled=True),
        lax.psum_scatter(d_values, "ctx", scatter_dimension=0, tiled=True),
    )
    d_query_low = rotate(
        (d_query * factor).reshape(row_count, feature_count), places, -1.0, HD
    ).astype(jnp.bfloat16)
    d_key_low = rotate(key_grad, places, -1.0, HD).astype(jnp.bfloat16)
    d_value_low = value_grad.astype(jnp.bfloat16)
    d_normed = (
        contract_back(d_query_low, full_query)
        + contract_back(d_key_low, full_key)
        + contract_back(d_value_low, full_value)
    )
    gain_attn_term = jnp.sum(d_normed * unit_rows, axis=0)
    grad_tokens = d_mixed + norm_back(d_normed, unit_rows, inverse, gain_a.astype(jnp.float32))
    grad_gain_attn, grad_query, grad_key, grad_value, grad_out, grad_gain_mlp = (
        lax.psum_scatter(gain_attn_term, ("fsdp", "ctx"), scatter_dimension=0, tiled=True),
        lax.psum_scatter(
            tokens_first(normed, d_query_low), ("fsdp", "ctx"), scatter_dimension=0, tiled=True
        ),
        lax.psum_scatter(
            tokens_first(normed, d_key_low), ("fsdp", "ctx"), scatter_dimension=0, tiled=True
        ),
        lax.psum_scatter(
            tokens_first(normed, d_value_low), ("fsdp", "ctx"), scatter_dimension=0, tiled=True
        ),
        lax.psum_scatter(
            tokens_first(d_mixed_low, attended_low),
            ("fsdp", "ctx"),
            scatter_dimension=0,
            tiled=True,
        ),
        lax.psum_scatter(gain_mlp_term, ("fsdp", "ctx"), scatter_dimension=0, tiled=True),
    )
    return (
        layer_out,
        grad_tokens,
        grad_gain_attn,
        grad_query,
        grad_key,
        grad_value,
        grad_out,
        grad_gain_mlp,
        grad_gate,
        grad_up,
        grad_down,
    )


def solution(mesh):
    in_specs = (
        P(("fsdp", "ctx"), None),
        P(("fsdp", "ctx"), None),
        P("fsdp", None),
        P(("fsdp", "ctx")),
        P(("fsdp", "ctx"), None),
        P(("fsdp", "ctx"), None),
        P(("fsdp", "ctx"), None),
        P(("fsdp", "ctx"), None),
        P(("fsdp", "ctx")),
        P(("fsdp", "ctx"), None),
        P(("fsdp", "ctx"), None),
        P(("fsdp", "ctx"), None),
    )
    out_specs = (
        P(("fsdp", "ctx"), None),
        P(("fsdp", "ctx"), None),
        P(("fsdp", "ctx")),
        P(("fsdp", "ctx"), None),
        P(("fsdp", "ctx"), None),
        P(("fsdp", "ctx"), None),
        P(("fsdp", "ctx"), None),
        P(("fsdp", "ctx")),
        P(("fsdp", "ctx"), None),
        P(("fsdp", "ctx"), None),
        P(("fsdp", "ctx"), None),
    )
    return jax.shard_map(local, mesh=mesh, in_specs=in_specs, out_specs=out_specs, check_vma=False)
```

profile of v0, /device:TPU:0, one launch (start us, length us, event | category | flops | bytes accessed | tf_op | source)
XLA Modules:
  0.0 2427.6 jit_solution(8481391783653051645)
XLA Ops:
  12.3 42.6 %all-reduce.5 = (bf16[2048]{0:T(1024)(128)(2,1)S(1)}, bf16[2048]{0:T(1024)(128)(2,1)S(1)}) all-reduce(bf16[2048]{0:T(1024)(128)(2,1)S(1)} %dynamic-update-slice, bf16[2048]{0:T(1024)(128)(2,1)S(1)} %dynamic-update-slice.1), channel_id=1, replica_groups=mesh['fsdp'=4,'ctx'=8] {'fsdp','ctx'}, use_global_device_ids=true, to_apply=%add | all-reduce | flops 4096 | bytes 16384
  56.2 35.3 %all-gather.18.cloned.1.call-done = bf16[2048,2048]{1,0:T(8,128)(2,1)} async-done(((bf16[64,2048]{1,0:T(8,128)(2,1)}), bf16[2048,2048]{1,0:T(8,128)(2,1)}) %all-gather.18.cloned.1.call-update) | async-done | bytes 8388624 | tf_op jit(solution)/shard_map/all_gather | solution.py:115
  99.4 71.0 %all-gather.16.cloned.1.call-done = bf16[2048,2048]{1,0:T(8,128)(2,1)} async-done(((bf16[64,2048]{1,0:T(8,128)(2,1)}), bf16[2048,2048]{1,0:T(8,128)(2,1)}) %all-gather.16.cloned.1.call-update) | async-done | bytes 8388624 | tf_op jit(solution)/shard_map/all_gather | solution.py:113
  177.2 72.2 %all-gather.12.cloned.1.call-done = bf16[2048,2048]{1,0:T(8,128)(2,1)} async-done(((bf16[64,2048]{1,0:T(8,128)(2,1)}), bf16[2048,2048]{1,0:T(8,128)(2,1)}) %all-gather.12.cloned.1.call-update) | async-done | bytes 8388624 | tf_op jit(solution)/shard_map/all_gather | solution.py:114
  259.1 43.4 %all-gather.30.cloned.1.call-done = bf16[256,8192]{1,0:T(8,128)(2,1)} async-done(((bf16[64,8192]{1,0:T(8,128)(2,1)}), bf16[256,8192]{1,0:T(8,128)(2,1)}) %all-gather.30.cloned.1.call-update) | async-done | bytes 4194320 | tf_op jit(solution)/shard_map/all_gather | solution.py:194
  314.4 42.4 %all-gather.28.cloned.1.call-done = bf16[256,8192]{1,0:T(8,128)(2,1)} async-done(((bf16[64,8192]{1,0:T(8,128)(2,1)}), bf16[256,8192]{1,0:T(8,128)(2,1)}) %all-gather.28.cloned.1.call-update) | async-done | bytes 4194320 | tf_op jit(solution)/shard_map/all_gather | solution.py:193
  363.3 78.0 %all-to-all-done.2 = bf16[256,8,1024]{0,2,1:T(8,128)(2,1)} async-done(((bf16[256,8,1024]{0,2,1:T(8,128)(2,1)}), bf16[256,8,1024]{0,2,1:T(8,128)(2,1)}, u32[]{:S(2)}, u32[]{:S(2)}) %all-to-all-start.2) | async-done | bytes 4194336 | tf_op jit(solution)/shard_map/all_to_all | solution.py:199
  446.2 71.6 %all-gather.14.cloned.1.call-done = bf16[1024,2048]{1,0:T(8,128)(2,1)} async-done(((bf16[128,2048]{1,0:T(8,128)(2,1)}), bf16[1024,2048]{1,0:T(8,128)(2,1)}) %all-gather.14.cloned.1.call-update) | async-done | bytes 4194320 | tf_op jit(solution)/shard_map/all_gather | solution.py:164
  517.8 42.3 %while.35 = (s32[]{:T(128)}, f32[32,128]{1,0:T(8,128)S(1)}, f32[32,128]{1,0:T(8,128)S(1)}, f32[128,32,64]{0,2,1:T(8,128)}, s32[128]{0:T(128)S(1)}, /*index=5*/s3...) while((s32[]{:T(128)}, f32[32,128]{1,0:T(8,128)S(1)}, ...), condition=%wide.region_9.10_spmd.clone, body=%wide.region_5.0_spmd.clone.sunk | while | flops 1901033088 | bytes 66074364 | solution.py:174
  561.5 60.8 %all-gather.22.cloned.1.call-done = bf16[2048,2048]{1,0:T(8,128)(2,1)} async-done(((bf16[64,2048]{1,0:T(8,128)(2,1)}), bf16[2048,2048]{1,0:T(8,128)(2,1)}) %all-gather.22.cloned.1.call-update) | async-done | bytes 8388624 | tf_op jit(solution)/shard_map/all_gather | solution.py:116
  629.7 45.8 %all-gather.26.cloned.1.call-done = bf16[256,8192]{1,0:T(8,128)(2,1)} async-done(((bf16[64,8192]{1,0:T(8,128)(2,1)}), bf16[256,8192]{1,0:T(8,128)(2,1)}) %all-gather.26.cloned.1.call-update) | async-done | bytes 4194320 | tf_op jit(solution)/shard_map/all_gather | solution.py:192
  710.3 136.3 %all-to-all-done = bf16[256,8,1024]{0,2,1:T(8,128)(2,1)} async-done(((bf16[256,8,1024]{0,2,1:T(8,128)(2,1)}), bf16[256,8,1024]{0,2,1:T(8,128)(2,1)}, u32[]{:S(2)}, u32[]{:S(2)}) %all-to-all-start) | async-done | bytes 4194336 | tf_op jit(solution)/shard_map/all_to_all | solution.py:197
  874.5 13.3 multiply_convert_fusion
  909.8 77.9 %reduce-scatter.20.cloned.1.call-done = f32[128,2048]{1,0:T(8,128)} async-done(((f32[1024,2048]{1,0:T(8,128)}), f32[128,2048]{1,0:T(8,128)}) %reduce-scatter.20.cloned.1.call-update) | async-done | bytes 1048592 | tf_op jit(solution)/shard_map/reduce_scatter | solution.py:214
  989.8 48.5 %reduce-scatter.18.cloned.1.call-done = bf16[128,2048]{1,0:T(8,128)(2,1)} async-done(((bf16[1024,2048]{1,0:T(8,128)(2,1)}), bf16[128,2048]{1,0:T(8,128)(2,1)}) %reduce-scatter.18.cloned.1.call-update) | async-done | bytes 524304 | tf_op jit(solution)/shard_map/reduce_scatter | solution.py:209
  1058.0 40.7 %while.34 = (s32[]{:T(128)}, f32[128,32,64]{0,2,1:T(8,128)}, f32[1024,2048]{0,1:T(8,128)}, f32[1024,2048]{0,1:T(8,128)}, s32[]{:T(128)}, /*index=5*/bf16[1024,20...) while((s32[]{:T(128)}, f32[128,32,64]{0,2,1:T(8,128)}, ...), condition=%wide.region_17.18_spmd.clone, body=%wide.region_15.17_spmd.clone.sunk | while | flops 2706839552 | bytes 120319856 | solution.py:310
  1117.7 189.8 %all_to_all.96 = bf16[8,256,1024]{2,1,0:T(8,128)(2,1)} all-to-all(bf16[8,256,1024]{2,1,0:T(8,128)(2,1)S(1)} %bitcast.230), channel_id=1, replica_groups=mesh['fsdp'=4,'ctx'=8] {'ctx'}, dimensions={0} | all-to-all | bytes 8388608 | tf_op jit(solution)/shard_map/all_to_all | solution.py:230
  1330.0 153.6 %all_to_all.97 = bf16[8,256,1024]{2,1,0:T(8,128)(2,1)} all-to-all(bf16[8,256,1024]{2,1,0:T(8,128)(2,1)S(1)} %bitcast.233), channel_id=1, replica_groups=mesh['fsdp'=4,'ctx'=8] {'ctx'}, dimensions={0} | all-to-all | bytes 8388608 | tf_op jit(solution)/shard_map/all_to_all | solution.py:224
  1505.7 97.3 %all_to_all.98 = bf16[8,256,1024]{2,1,0:T(8,128)(2,1)} all-to-all(bf16[8,256,1024]{2,1,0:T(8,128)(2,1)S(1)} %bitcast.236), channel_id=1, replica_groups=mesh['fsdp'=4,'ctx'=8] {'ctx'}, dimensions={0} | all-to-all | bytes 8388608 | tf_op jit(solution)/shard_map/all_to_all | solution.py:227
  1691.5 40.7 %all-reduce.4 = (f32[2048]{0:T(1024)S(1)}, f32[2048]{0:T(1024)S(1)}) all-reduce(f32[2048]{0:T(1024)S(1)} %get-tuple-element.597, f32[2048]{0:T(1024)S(1)} %copy-done.28), channel_id=6, replica_groups=mesh['fsdp'=4,'ctx'=8] {'fsdp','ctx'}, use_global_device_ids=true, to_apply=%region_22.23.clone | all-reduce | flops 4096 | bytes 32768
  1734.8 123.6 %reduce-scatter.32.cloned.1.call-done = f32[64,2048]{1,0:T(8,128)} async-done(((f32[2048,2048]{1,0:T(8,128)}), f32[64,2048]{1,0:T(8,128)}) %reduce-scatter.32.cloned.1.call-update) | async-done | bytes 524304 | tf_op jit(solution)/shard_map/reduce_scatter | solution.py:343
  1858.3 187.2 %reduce-scatter.30.cloned.1.call-done = f32[64,2048]{1,0:T(8,128)} async-done(((f32[2048,2048]{1,0:T(8,128)}), f32[64,2048]{1,0:T(8,128)}) %reduce-scatter.30.cloned.1.call-update) | async-done | bytes 524304 | tf_op jit(solution)/shard_map/reduce_scatter | solution.py:340
  2045.6 187.4 %reduce-scatter.28.cloned.1.call-done = f32[64,2048]{1,0:T(8,128)} async-done(((f32[2048,2048]{1,0:T(8,128)}), f32[64,2048]{1,0:T(8,128)}) %reduce-scatter.28.cloned.1.call-update) | async-done | bytes 524304 | tf_op jit(solution)/shard_map/reduce_scatter | solution.py:337
  2232.9 187.4 %reduce-scatter.26.cloned.1.call-done = f32[64,2048]{1,0:T(8,128)} async-done(((f32[2048,2048]{1,0:T(8,128)}), f32[64,2048]{1,0:T(8,128)}) %reduce-scatter.26.cloned.1.call-update) | async-done | bytes 524304 | tf_op jit(solution)/shard_map/reduce_scatter | solution.py:334
  (275 shorter events, 405.2 us)
Async XLA Ops:
  7.9 162.5 %all-gather.16.cloned.1.call-start = ((), (), s32[]{:S(2)}) async-start(), calls=%async_computation.19 | async-start | bytes 8650752 | tf_op jit(solution)/shard_map/all_gather | solution.py:113
  8.7 240.8 %all-gather.12.cloned.1.call-start = ((), (), s32[]{:S(2)}) async-start(), calls=%async_computation.17 | async-start | bytes 8650752 | tf_op jit(solution)/shard_map/all_gather | solution.py:114
  9.4 293.1 %all-gather.30.cloned.1.call-start = ((), (), s32[]{:S(2)}) async-start(), calls=%async_computation.26 | async-start | bytes 5242880 | tf_op jit(solution)/shard_map/all_gather | solution.py:194
  10.0 346.9 %all-gather.28.cloned.1.call-start = ((), (), s32[]{:S(2)}) async-start(), calls=%async_computation.25 | async-start | bytes 5242880 | tf_op jit(solution)/shard_map/all_gather | solution.py:193
  10.6 435.6 %all-gather.20.cloned.1.call-start = ((), (), s32[]{:S(2)}) async-start(), calls=%async_computation.21 | async-start | bytes 4718592 | tf_op jit(solution)/shard_map/all_gather | solution.py:165
  97.2 420.6 %all-gather.14.cloned.1.call-start = ((), (), s32[]{:S(2)}) async-start(), calls=%async_computation.18 | async-start | bytes 4718592 | tf_op jit(solution)/shard_map/all_gather | solution.py:164
  258.3 364.0 %all-gather.22.cloned.1.call-start = ((), (), s32[]{:S(2)}) async-start(), calls=%async_computation.22 | async-start | bytes 8650752 | tf_op jit(solution)/shard_map/all_gather | solution.py:116
  308.9 132.4 %all-to-all-start.2 = ((bf16[256,8,1024]{0,2,1:T(8,128)(2,1)}), bf16[256,8,1024]{0,2,1:T(8,128)(2,1)}, u32[]{:S(2)}, u32[]{:S(2)}) async-start(bf16[256,8,1024]{0,2,1:T(8,128)(2,1)} %bitcast.224), calls=%async_computation.2 | async-start | bytes 8388608 | tf_op jit(solution)/shard_map/all_to_all | solution.py:199
  313.5 362.0 %all-gather.26.cloned.1.call-start = ((), (), s32[]{:S(2)}) async-start(), calls=%async_computation.24 | async-start | bytes 5242880 | tf_op jit(solution)/shard_map/all_gather | solution.py:192
  441.3 240.7 %all-to-all-start.1 = ((bf16[256,8,1024]{0,2,1:T(8,128)(2,1)}), bf16[256,8,1024]{0,2,1:T(8,128)(2,1)}, u32[]{:S(2)}, u32[]{:S(2)}) async-start(bf16[256,8,1024]{0,2,1:T(8,128)(2,1)} %bitcast.223), calls=%async_computation.1 | async-start | bytes 8388608 | tf_op jit(solution)/shard_map/all_to_all | solution.py:198
  446.1 411.9 %all-gather.24.cloned.1.call-start = ((), (), s32[]{:S(2)}) async-start(), calls=%async_computation.23 | async-start | bytes 4718592 | tf_op jit(solution)/shard_map/all_gather | solution.py:205
  682.0 164.7 %all-to-all-start = ((bf16[256,8,1024]{0,2,1:T(8,128)(2,1)}), bf16[256,8,1024]{0,2,1:T(8,128)(2,1)}, u32[]{:S(2)}, u32[]{:S(2)}) async-start(bf16[256,8,1024]{0,2,1:T(8,128)(2,1)} %bitcast.225), calls=%async_computation | async-start | bytes 8388608 | tf_op jit(solution)/shard_map/all_to_all | solution.py:197
  686.6 187.9 %all-gather.32.cloned.1.call-start = ((), (), s32[]{:S(2)}) async-start(), calls=%async_computation.28 | async-start | bytes 4718592 | tf_op jit(solution)/shard_map/all_gather | solution.py:206
  687.3 300.3 %reduce-scatter.20.cloned.1.call-start = ((), (), s32[]{:S(2)}) async-start(), calls=%async_computation.29 | async-start | bytes 9437184 | tf_op jit(solution)/shard_map/reduce_scatter | solution.py:214
  899.2 139.1 %reduce-scatter.18.cloned.1.call-start = ((), (), s32[]{:S(2)}) async-start(), calls=%async_computation.27 | async-start | bytes 4718592 | tf_op jit(solution)/shard_map/reduce_scatter | solution.py:209
  909.1 716.9 %reduce-scatter.24.cloned.1.call-start = ((), (), s32[]{:S(2)}) async-start(), calls=%async_computation.31 | async-start | bytes 9437184 | tf_op jit(solution)/shard_map/reduce_scatter | solution.py:318
  1098.7 540.3 %reduce-scatter.22.cloned.1.call-start = ((), (), s32[]{:S(2)}) async-start(), calls=%async_computation.30 | async-start | bytes 9437184 | tf_op jit(solution)/shard_map/reduce_scatter | solution.py:317
  1099.3 558.9 %reduce-scatter.38.cloned.1.call-start = ((), (), s32[]{:S(2)}) async-start(), calls=%async_computation.38 | async-start | bytes 5242880
  1320.4 343.4 %reduce-scatter.34.cloned.1.call-start = ((), (), s32[]{:S(2)}) async-start(), calls=%async_computation.36 | async-start | bytes 5242880
  1496.5 173.0 %reduce-scatter.36.cloned.1.call-start = ((), (), s32[]{:S(2)}) async-start(), calls=%async_computation.37 | async-start | bytes 5242880
  1615.9 242.4 %reduce-scatter.32.cloned.1.call-start = ((), (), s32[]{:S(2)}) async-start(), calls=%async_computation.35 | async-start | bytes 17301504 | tf_op jit(solution)/shard_map/reduce_scatter | solution.py:343
  1625.9 419.7 %reduce-scatter.30.cloned.1.call-start = ((), (), s32[]{:S(2)}) async-start(), calls=%async_computation.34 | async-start | bytes 17301504 | tf_op jit(solution)/shard_map/reduce_scatter | solution.py:340
  1636.8 596.1 %reduce-scatter.28.cloned.1.call-start = ((), (), s32[]{:S(2)}) async-start(), calls=%async_computation.33 | async-start | bytes 17301504 | tf_op jit(solution)/shard_map/reduce_scatter | solution.py:337
  1649.2 771.1 %reduce-scatter.26.cloned.1.call-start = ((), (), s32[]{:S(2)}) async-start(), calls=%async_computation.32 | async-start | bytes 17301504 | tf_op jit(solution)/shard_map/reduce_scatter | solution.py:334
  (45 other events, 1159.4 us)
Sparse Core Ops, SparseCore 0:
  11.0 80.5 all-gather.17
  94.5 75.8 all-gather.15
  173.4 75.9 all-gather.11
  251.1 51.2 all-gather.29
  304.2 52.6 all-gather.27
  358.9 79.3 all-gather.19
  440.5 77.3 all-gather.13
  520.8 101.5 all-gather.21
  624.2 51.2 all-gather.25
  677.6 79.5 all-gather.23
  758.7 84.4 all-gather.31
  899.3 88.3 reduce-scatter.19
  990.0 48.3 reduce-scatter.17
  1098.8 185.5 reduce-scatter.23
  1286.5 183.8 reduce-scatter.21
  1473.3 75.4 reduce-scatter.37
  1551.9 52.6 reduce-scatter.33
  1616.0 51.5 reduce-scatter.35
  1670.6 187.6 reduce-scatter.31
  1861.2 184.3 reduce-scatter.29
  2048.5 184.3 reduce-scatter.27
  2235.9 184.3 reduce-scatter.25
where the time goes:
time: 2440 us; the launch traced here: 2430 us
  waiting for transfers between devices  1470 us (60%)
  blocking collectives  524 us (21%)
  matrix products  188 us (8%)
  local copies, waits for them, and re-layouts  178 us (7%)
  other arithmetic  30.8 us (1%)
    all_to_all x1, blocking collectives, local(): lax.all_to_all(part_down.astype(jnp.bfloat16), 'ctx', split_axis=0, conca...  190 us
    reduce_scatter x1, waiting for transfers between devices, local(): lax.psum_scatter(tokens_first(normed, d_key_low), ('fsdp', 'ctx'), scatte...  187 us
    reduce_scatter x1, waiting for transfers between devices, local(): lax.psum_scatter(tokens_first(normed, d_query_low), ('fsdp', 'ctx'), scat...  187 us
    reduce_scatter x1, waiting for transfers between devices, local(): lax.psum_scatter(tokens_first(normed, d_value_low), ('fsdp', 'ctx'), scat...  187 us
    all_to_all x1, blocking collectives, local(): lax.all_to_all(part_gate.astype(jnp.bfloat16), 'ctx', split_axis=0, conca...  154 us
    all_to_all x1, waiting for transfers between devices, local(): lax.all_to_all(slab_gate, 'ctx', split_axis=1, concat_axis=0, tiled=True)  136 us
    reduce_scatter x1, waiting for transfers between devices, local(): lax.psum_scatter(tokens_first(d_mixed_low, attended_low), ('fsdp', 'ctx')...  124 us
    all_to_all x1, blocking collectives, local(): lax.all_to_all(part_up.astype(jnp.bfloat16), 'ctx', split_axis=0, concat_...  97.3 us
  transfers between devices with their start and end apart: 25, of which 16 were waited for; matrix products, arithmetic and copies ran while one was open for 13% of the time, Pallas kernels for 0%

commit v1 on v0

v1 whole, which is shorter than its diff:
```python
import functools

import jax
import jax.numpy as jnp
from jax import lax
from jax.experimental import pallas as pl
from jax.experimental.pallas import tpu as pltpu
from jax.sharding import PartitionSpec as P

H = 32
HD = 64
EPSILON = 1e-05
ROPE_BASE = 130000.0
BLOCK = 256
VMEM_LIMIT = 56 * 1024 * 1024
LOW = jnp.bfloat16
F32 = jnp.float32


def dot(left, right, left_dim, right_dim):
    return lax.dot_general(
        left, right, (((left_dim,), (right_dim,)), ((), ())), preferred_element_type=F32
    )


def flip(axis, size, bit):
    return [(i, i ^ bit) for i in range(size)]


def same_core_groups(size):
    return [[2 * i + core for i in range(size // 2)] for core in (0, 1)]


def gather_fsdp(block):
    size = lax.axis_size("fsdp")
    if size != 4:
        return lax.all_gather(block, "fsdp", axis=0, tiled=True)
    me = lax.axis_index("fsdp")
    rows = block.shape[0]
    half = rows // 2
    from_x = lax.ppermute(block, "fsdp", flip("fsdp", 4, 1))
    from_y = lax.ppermute(block, "fsdp", flip("fsdp", 4, 2))
    far_top = lax.ppermute(from_x[:half], "fsdp", flip("fsdp", 4, 2))
    far_low = lax.ppermute(from_y[half:], "fsdp", flip("fsdp", 4, 1))
    out = jnp.zeros((4 * rows, block.shape[1]), block.dtype)
    for piece, place in (
        (block, me * rows),
        (from_x, (me ^ 1) * rows),
        (from_y, (me ^ 2) * rows),
        (far_top, (me ^ 3) * rows),
        (far_low, (me ^ 3) * rows + half),
    ):
        out = lax.dynamic_update_slice_in_dim(out, piece, place, 0)
    return out


def scatter_fsdp(part):
    size = lax.axis_size("fsdp")
    if size != 4:
        return lax.psum_scatter(part, "fsdp", scatter_dimension=0, tiled=True).astype(F32)
    me = lax.axis_index("fsdp")
    rows = part.shape[0] // 4
    half = rows // 2

    def piece(bits, low):
        return lax.dynamic_slice_in_dim(part, (me ^ bits) * rows + low * half, half, 0)

    over_x = lax.ppermute(
        jnp.concatenate([piece(3, 0), piece(1, 0)]), "fsdp", flip("fsdp", 4, 1)
    )
    over_y = lax.ppermute(
        jnp.concatenate([piece(3, 1), piece(2, 1)]), "fsdp", flip("fsdp", 4, 2)
    )
    send_y = (piece(2, 0).astype(F32) + over_x[:half].astype(F32)).astype(part.dtype)
    send_x = (piece(1, 1).astype(F32) + over_y[:half].astype(F32)).astype(part.dtype)
    last_y = lax.ppermute(send_y, "fsdp", flip("fsdp", 4, 2))
    last_x = lax.ppermute(send_x, "fsdp", flip("fsdp", 4, 1))
    top = piece(0, 0).astype(F32) + over_x[half:].astype(F32) + last_y.astype(F32)
    low = piece(0, 1).astype(F32) + over_y[half:].astype(F32) + last_x.astype(F32)
    return jnp.concatenate([top, low])


def gather_ctx(block):
    size = lax.axis_size("ctx")
    pairs = size // 2
    core = lax.axis_index("ctx") % 2
    mine = lax.all_to_all(
        jnp.broadcast_to(block[None], (pairs,) + block.shape),
        "ctx",
        0,
        0,
        axis_index_groups=same_core_groups(size),
        tiled=True,
    )
    other = lax.ppermute(mine, "ctx", flip("ctx", size, 1))
    first = jnp.where(core == 0, mine, other)
    second = jnp.where(core == 0, other, mine)
    return jnp.stack([first, second], axis=1).reshape((size,) + block.shape)


def scatter_ctx(part):
    size = lax.axis_size("ctx")
    pairs = size // 2
    core = lax.axis_index("ctx") % 2
    shaped = part.reshape(pairs, 2, part.shape[0] // size, part.shape[1])
    mine = lax.dynamic_index_in_dim(shaped, core, 1, keepdims=False)
    theirs = lax.dynamic_index_in_dim(shaped, 1 - core, 1, keepdims=False)
    got = lax.ppermute(theirs, "ctx", flip("ctx", size, 1))
    pair_sum = (mine.astype(F32) + got.astype(F32)).astype(part.dtype)
    landed = lax.all_to_all(
        pair_sum, "ctx", 0, 0, axis_index_groups=same_core_groups(size), tiled=True
    )
    return jnp.sum(landed.astype(F32), axis=0)


def to_columns(rows_block):
    return lax.all_to_all(rows_block, "ctx", split_axis=1, concat_axis=0, tiled=True)


def swap_halves(values):
    width = values.shape[1]
    lane = lax.broadcasted_iota(jnp.int32, values.shape, 1)
    down = pltpu.roll(values, width - HD // 2, 1)
    up = pltpu.roll(values, HD // 2, 1)
    return jnp.where(lane % HD < HD // 2, down, up)


def project_kernel(width, x_ref, w_ref, cos_ref, sin_ref, unit_ref, out_ref):
    x = x_ref[...].astype(F32)
    inverse = lax.rsqrt(jnp.mean(x * x, axis=-1, keepdims=True) + EPSILON)
    unit = (x * inverse).astype(LOW)
    unit_ref[...] = unit
    cos, sin = cos_ref[...], sin_ref[...]
    for part in range(3):
        columns = slice(part * width, (part + 1) * width)
        value = dot(unit, w_ref[:, columns], 1, 0)
        if part < 2:
            value = value * cos + swap_halves(value) * sin
        out_ref[:, columns] = value.astype(LOW)


def project(x_all, w_qkv, cos, sin):
    count, features = x_all.shape
    width = w_qkv.shape[1] // 3
    return pl.pallas_call(
        functools.partial(project_kernel, width),
        grid=(count // BLOCK,),
        in_specs=[
            pl.BlockSpec((BLOCK, features), lambda i: (i, 0)),
            pl.BlockSpec((features, 3 * width), lambda i: (0, 0)),
            pl.BlockSpec((BLOCK, width), lambda i: (i, 0)),
            pl.BlockSpec((BLOCK, width), lambda i: (i, 0)),
        ],
        out_specs=[
            pl.BlockSpec((BLOCK, features), lambda i: (i, 0)),
            pl.BlockSpec((BLOCK, 3 * width), lambda i: (i, 0)),
        ],
        out_shape=[
            jax.ShapeDtypeStruct((count, features), LOW),
            jax.ShapeDtypeStruct((count, 3 * width), LOW),
        ],
        compiler_params=pltpu.CompilerParams(vmem_limit_bytes=VMEM_LIMIT),
        name="project",
    )(x_all, w_qkv, cos, sin)


def masked_scores(key, query, key_block, query_block, starts):
    scores = dot(key, query, 1, 1) * (HD**-0.5)
    at_key = key_block * BLOCK + lax.broadcasted_iota(jnp.int32, scores.shape, 0)
    at_query = query_block * BLOCK + lax.broadcasted_iota(jnp.int32, scores.shape, 1)
    return jnp.where((at_key <= at_query) & (at_key >= starts), scores, -1e30)


def attend_kernel(heads, lo_ref, start_ref, q_ref, k_ref, v_ref, out_ref, score_ref):
    block = pl.program_id(0)
    starts = start_ref[...]
    lanes = [slice(h * HD, (h + 1) * HD) for h in range(heads)]
    queries = [q_ref[:, lane] for lane in lanes]

    def score(key_block, tops):
        rows = pl.ds(pl.multiple_of(key_block * BLOCK, BLOCK), BLOCK)
        fresh = []
        for h in range(heads):
            s = masked_scores(k_ref[rows, lanes[h]], queries[h], key_block, block, starts)
            score_ref[h, rows, :] = s
            fresh.append(jnp.maximum(tops[h], jnp.max(s, axis=0, keepdims=True)))
        return tuple(fresh)

    lo = lo_ref[block]
    tops = lax.fori_loop(lo, block + 1, score, (jnp.full((1, BLOCK), -1e30, F32),) * heads)

    def weigh(key_block, carried):
        sums, totals = carried
        rows = pl.ds(pl.multiple_of(key_block * BLOCK, BLOCK), BLOCK)
        new_sums, new_totals = [], []
        for h in range(heads):
            p = jnp.exp(score_ref[h, rows, :] - tops[h])
            new_sums.append(sums[h] + jnp.sum(p, axis=0, keepdims=True))
            new_totals.append(totals[h] + dot(v_ref[rows, lanes[h]], p.astype(LOW), 0, 0))
        return tuple(new_sums), tuple(new_totals)

    sums, totals = lax.fori_loop(
        lo,
        block + 1,
        weigh,
        ((jnp.zeros((1, BLOCK), F32),) * heads, (jnp.zeros((HD, BLOCK), F32),) * heads),
    )
    turned = jnp.concatenate([totals[h] / sums[h] for h in range(heads)], axis=0)
    out_ref[...] = turned.T.astype(LOW)


def attend(lows, starts, qkv):
    count = qkv.shape[0]
    width = qkv.shape[1] // 3
    heads = width // HD
    return pl.pallas_call(
        functools.partial(attend_kernel, heads),
        grid_spec=pltpu.PrefetchScalarGridSpec(
            num_scalar_prefetch=1,
            grid=(count // BLOCK,),
            in_specs=[
                pl.BlockSpec((1, BLOCK), lambda i, lo: (0, i)),
                pl.BlockSpec((BLOCK, width), lambda i, lo: (i, 0)),
                pl.BlockSpec((count, width), lambda i, lo: (0, 1)),
                pl.BlockSpec((count, width), lambda i, lo: (0, 2)),
            ],
            out_specs=pl.BlockSpec((BLOCK, width), lambda i, lo: (i, 0)),
            scratch_shapes=[pltpu.VMEM((heads, count, BLOCK), F32)],
        ),
        out_shape=jax.ShapeDtypeStruct((count, width), LOW),
        compiler_params=pltpu.CompilerParams(vmem_limit_bytes=VMEM_LIMIT),
        name="attend",
    )(lows, starts, qkv, qkv, qkv)


def attend_back_kernel(
    heads,
    lo_ref,
    start_ref,
    q_ref,
    k_ref,
    v_ref,
    back_ref,
    cos_ref,
    sin_ref,
    out_ref,
    weight_ref,
    slope_ref,
    dk_ref,
    dv_ref,
):
    block = pl.program_id(0)
    width = heads * HD
    starts = start_ref[...]
    lanes = [slice(h * HD, (h + 1) * HD) for h in range(heads)]
    queries = [q_ref[:, lane] for lane in lanes]
    backs = [back_ref[:, lane] for lane in lanes]

    @pl.when(block == 0)
    def _():
        dk_ref[...] = jnp.zeros_like(dk_ref)
        dv_ref[...] = jnp.zeros_like(dv_ref)

    def score(key_block, tops):
        rows = pl.ds(pl.multiple_of(key_block * BLOCK, BLOCK), BLOCK)
        fresh = []
        for h in range(heads):
            s = masked_scores(k_ref[rows, lanes[h]], queries[h], key_block, block, starts)
            weight_ref[h, rows, :] = s
            slope_ref[h, rows, :] = dot(v_ref[rows, lanes[h]], backs[h], 1, 1)
            fresh.append(jnp.maximum(tops[h], jnp.max(s, axis=0, keepdims=True)))
        return tuple(fresh)

    lo = lo_ref[block]
    tops = lax.fori_loop(lo, block + 1, score, (jnp.full((1, BLOCK), -1e30, F32),) * heads)

    def weigh(key_block, carried):
        sums, deltas = carried
        rows = pl.ds(pl.multiple_of(key_block * BLOCK, BLOCK), BLOCK)
        new_sums, new_deltas = [], []
        for h in range(heads):
            p = jnp.exp(weight_ref[h, rows, :] - tops[h])
            weight_ref[h, rows, :] = p
            new_sums.append(sums[h] + jnp.sum(p, axis=0, keepdims=True))
            new_deltas.append(
                deltas[h] + jnp.sum(p * slope_ref[h, rows, :], axis=0, keepdims=True)
            )
        return tuple(new_sums), tuple(new_deltas)

    zero_row = (jnp.zeros((1, BLOCK), F32),) * heads
    sums, deltas = lax.fori_loop(lo, block + 1, weigh, (zero_row, zero_row))
    inverses = [1.0 / sums[h] for h in range(heads)]
    deltas = [deltas[h] * inverses[h] for h in range(heads)]

    def spread(key_block, totals):
        rows = pl.ds(pl.multiple_of(key_block * BLOCK, BLOCK), BLOCK)
        fresh, dks, dvs = [], [], []
        for h in range(heads):
            p = weight_ref[h, rows, :] * inverses[h]
            ds = (p * (slope_ref[h, rows, :] - deltas[h])).astype(LOW)
            dvs.append(dot(p.astype(LOW), backs[h], 1, 0))
            dks.append(dot(ds, queries[h], 1, 0))
            fresh.append(totals[h] + dot(k_ref[rows, lanes[h]], ds, 0, 0))
        dk_ref[rows, :] += jnp.concatenate(dks, axis=1)
        dv_ref[rows, :] += jnp.concatenate(dvs, axis=1)
        return tuple(fresh)

    totals = lax.fori_loop(lo, block + 1, spread, (jnp.zeros((HD, BLOCK), F32),) * heads)
    here = pl.ds(pl.multiple_of(block * BLOCK, BLOCK), BLOCK)
    dq = jnp.concatenate(totals, axis=0).T * (HD**-0.5)
    dq = dq * cos_ref[here, :] - swap_halves(dq) * sin_ref[here, :]
    out_ref[here, 0:width] = dq.astype(LOW)

    @pl.when(block == pl.num_programs(0) - 1)
    def _():
        def finish(index, carried):
            rows = pl.ds(pl.multiple_of(index * BLOCK, BLOCK), BLOCK)
            dk = dk_ref[rows, :] * (HD**-0.5)
            dk = dk * cos_ref[rows, :] - swap_halves(dk) * sin_ref[rows, :]
            out_ref[rows, width : 2 * width] = dk.astype(LOW)
            out_ref[rows, 2 * width : 3 * width] = dv_ref[rows, :].astype(LOW)
            return carried

        lax.fori_loop(0, dk_ref.shape[0] // BLOCK, finish, 0)


def attend_back(lows, starts, qkv, back, cos, sin):
    count = qkv.shape[0]
    width = qkv.shape[1] // 3
    heads = width // HD
    return pl.pallas_call(
        functools.partial(attend_back_kernel, heads),
        grid_spec=pltpu.PrefetchScalarGridSpec(
            num_scalar_prefetch=1,
            grid=(count // BLOCK,),
            in_specs=[
                pl.BlockSpec((1, BLOCK), lambda i, lo: (0, i)),
                pl.BlockSpec((BLOCK, width), lambda i, lo: (i, 0)),
                pl.BlockSpec((count, width), lambda i, lo: (0, 1)),
                pl.BlockSpec((count, width), lambda i, lo: (0, 2)),
                pl.BlockSpec((BLOCK, width), lambda i, lo: (i, 0)),
                pl.BlockSpec((count, width), lambda i, lo: (0, 0)),
                pl.BlockSpec((count, width), lambda i, lo: (0, 0)),
            ],
            out_specs=pl.BlockSpec((count, 3 * width), lambda i, lo: (0, 0)),
            scratch_shapes=[
                pltpu.VMEM((heads, count, BLOCK), F32),
                pltpu.VMEM((heads, count, BLOCK), F32),
                pltpu.VMEM((count, width), F32),
                pltpu.VMEM((count, width), F32),
            ],
        ),
        out_shape=jax.ShapeDtypeStruct((count, 3 * width), LOW),
        compiler_params=pltpu.CompilerParams(vmem_limit_bytes=VMEM_LIMIT),
        name="attend_back",
    )(lows, starts, qkv, qkv, qkv, back, cos, sin)


def local(
    tokens,
    cotangent,
    doc_lengths,
    gain_attn,
    w_query,
    w_key,
    w_value,
    w_out,
    gain_mlp,
    w_gate,
    w_up,
    w_down,
):
    rows, features = tokens.shape
    n_c = lax.axis_size("ctx")
    group = rows * n_c
    width = features // n_c
    here = lax.axis_index("ctx") * rows
    share = w_query.shape[0]

    gain_a = gain_attn.astype(F32)[:, None]
    gain_m = gain_mlp.astype(F32)[:, None]

    def scaled(weight, gain):
        return (weight.astype(F32) * gain).astype(LOW)

    x_all = lax.all_gather(tokens, "ctx", axis=0, tiled=True)
    out_all = lax.all_gather(w_out, ("fsdp", "ctx"), axis=0, tiled=True)
    back_all = lax.all_gather(cotangent, "ctx", axis=0, tiled=True)

    stacked = jnp.concatenate(
        [
            scaled(w, gain_a).reshape(share, n_c, width)
            for w in (w_query, w_key, w_value)
        ],
        axis=2,
    ).reshape(share, 3 * features)
    w_qkv = gather_fsdp(to_columns(stacked))
    col_gate = gather_fsdp(to_columns(scaled(w_gate, gain_m)))
    col_up = gather_fsdp(to_columns(scaled(w_up, gain_m)))
    col_down = gather_fsdp(to_columns(w_down))

    position = jnp.arange(group, dtype=jnp.int32)
    doc_ends = jnp.cumsum(doc_lengths[0])
    doc_starts = doc_ends - doc_lengths[0]
    starts = jnp.max(
        jnp.where(position[:, None] >= doc_starts[None, :], doc_starts[None, :], 0), axis=1
    ).astype(jnp.int32)
    places = (position - starts).astype(F32)
    half = HD // 2
    lane = jnp.arange(128, dtype=jnp.int32)
    inv_freq = ROPE_BASE ** (-2.0 * (lane % half).astype(F32) / HD)
    angles = places[:, None] * inv_freq[None, :]
    sign = jnp.where(lane % HD < half, -1.0, 1.0).astype(F32)
    cos = jnp.tile(jnp.cos(angles), (1, width // 128))
    sin = jnp.tile(jnp.sin(angles) * sign[None, :], (1, width // 128))
    lows = starts[::BLOCK] // BLOCK
    starts_row = starts[None, :]

    unit, qkv = project(x_all, w_qkv, cos, sin)
    attended = attend(lows, starts_row, qkv)
    attended_all = (
        jnp.swapaxes(gather_ctx(attended), 0, 1).reshape(group, features)
    )
    mixed = x_all.astype(F32) + dot(attended_all, out_all, 1, 1)
    inverse_mlp = lax.rsqrt(jnp.mean(mixed * mixed, axis=-1, keepdims=True) + EPSILON)
    unit_mlp = (mixed * inverse_mlp).astype(LOW)

    gate = dot(unit_mlp, col_gate, 1, 0)
    up = dot(unit_mlp, col_up, 1, 0)
    sigmoid = jax.nn.sigmoid(gate)
    silu = gate * sigmoid
    hidden = (silu * up).astype(LOW)
    d_hidden = dot(back_all, col_down, 1, 0)
    d_gate = (d_hidden * up * sigmoid * (1.0 + gate * (1.0 - sigmoid))).astype(LOW)
    d_up = (d_hidden * silu).astype(LOW)
    branch = dot(hidden, col_down, 1, 1).astype(LOW)
    d_unit_part = (dot(d_gate, col_gate, 1, 1) + dot(d_up, col_up, 1, 1)).astype(LOW)
    d_unit = scatter_ctx(d_unit_part)
    branch_own = lax.psum_scatter(branch, "ctx", scatter_dimension=0, tiled=True).astype(F32)
    mixed_own = lax.dynamic_slice_in_dim(mixed, here, rows, 0)
    layer_out = (mixed_own + branch_own).astype(LOW)

    inverse_own = lax.dynamic_slice_in_dim(inverse_mlp, here, rows, 0)
    unit_own = mixed_own * inverse_own
    d_mixed = cotangent.astype(F32) + inverse_own * (
        d_unit - unit_own * jnp.mean(d_unit * unit_own, axis=-1, keepdims=True)
    )
    d_mixed_low = d_mixed.astype(LOW)
    d_att = dot(d_mixed_low, out_all, 1, 0).astype(LOW)
    d_att_own = lax.all_to_all(d_att, "ctx", split_axis=1, concat_axis=0, tiled=True)
    d_qkv = attend_back(lows, starts_row, qkv, d_att_own, cos, sin)

    d_first = scatter_ctx(dot(d_qkv, w_qkv, 1, 1).astype(LOW))
    x_own = tokens.astype(F32)
    inverse = lax.rsqrt(jnp.mean(x_own * x_own, axis=-1, keepdims=True) + EPSILON)
    first_own = x_own * inverse
    grad_tokens = d_mixed + inverse * (
        d_first - first_own * jnp.mean(d_first * first_own, axis=-1, keepdims=True)
    )

    def weight_grad(left, right):
        part = dot(left, right, 0, 0).astype(LOW)
        mine = scatter_fsdp(part).astype(LOW)
        return lax.all_to_all(mine, "ctx", split_axis=0, concat_axis=1, tiled=True).astype(F32)

    raw_gate = weight_grad(unit_mlp, d_gate)
    raw_up = weight_grad(unit_mlp, d_up)
    grad_down = weight_grad(back_all, hidden)
    attended_own = lax.dynamic_slice_in_dim(attended_all, here, rows, 0)
    grad_out = lax.psum_scatter(
        dot(d_mixed_low, attended_own, 0, 0).astype(LOW),
        ("fsdp", "ctx"),
        scatter_dimension=0,
        tiled=True,
    ).astype(F32)
    raw_qkv = weight_grad(unit, d_qkv).reshape(share, n_c, 3, width)
    raw_query, raw_key, raw_value = (
        raw_qkv[:, :, part].reshape(share, features) for part in range(3)
    )
    grad_gain_attn = jnp.sum(
        raw_query * w_query.astype(F32)
        + raw_key * w_key.astype(F32)
        + raw_value * w_value.astype(F32),
        axis=1,
    )
    grad_gain_mlp = jnp.sum(
        raw_gate * w_gate.astype(F32) + raw_up * w_up.astype(F32), axis=1
    )
    return (
        layer_out,
        grad_tokens,
        grad_gain_attn,
        raw_query * gain_a,
        raw_key * gain_a,
        raw_value * gain_a,
        grad_out,
        grad_gain_mlp,
        raw_gate * gain_m,
        raw_up * gain_m,
        grad_down,
    )


def solution(mesh):
    split = P(("fsdp", "ctx"))
    rows = P(("fsdp", "ctx"), None)
    in_specs = (rows, rows, P("fsdp", None), split, rows, rows, rows, rows, split, rows, rows, rows)
    out_specs = (rows, rows, split, rows, rows, rows, rows, split, rows, rows, rows)
    return jax.shard_map(local, mesh=mesh, in_specs=in_specs, out_specs=out_specs, check_vma=False)
```

time: 2440 us -> 861 us (0.35)
  waiting for transfers between devices: 1470 us -> 438 us
  blocking collectives: 524 us -> 0 us
  matrix products: 188 us -> 104 us
  local copies, waits for them, and re-layouts: 178 us -> 101 us
  starting transfers between devices: 15.8 us -> 87.1 us
  Pallas kernels: 0 us -> 40 us
  other arithmetic: 30.8 us -> 67.4 us
    reduce_scatter x8 -> x2, waiting for transfers between devices: 812 us -> 0.02 us  [the longest x1 0.02 us: local(): lax.psum_scatter(branch, 'ctx', scatter_dimension=0, tiled=True).astype(F32)]
    all_gather x11 -> x3, waiting for transfers between devices: 443 us -> 0.02 us  [the longest x1 0.02 us: local(): x_all = lax.all_gather(tokens, 'ctx', axis=0, tiled=True)]
    all_to_all x3 -> x0, blocking collectives: 441 us -> none  [the longest x1 190 us: local(): lax.all_to_all(part_down.astype(jnp.bfloat16), 'ctx', split_axis=0, conca...]
    ppermute x0 -> x35, waiting for transfers between devices: none -> 224 us  [the longest x4 80 us: scatter_fsdp(): lax.ppermute(jnp.concatenate([piece(3, 0), piece(1, 0)]), 'fsdp', flip('f...]
    dot_general x30 -> x14, matrix products: 188 us -> 104 us  [dot(): lax.dot_general(left, right, (((left_dim,), (right_dim,)), ((), ())), pre...]
    unnamed x2 -> x0, blocking collectives: 83.4 us -> none
    pallas_call x0 -> x3, Pallas kernels: none -> 40 us  [the longest x1 20.1 us: attend_back(): pl.pallas_call(functools.partial(attend_back_kernel, heads), grid_spec=pl...]
    all_to_all x3 -> x12, starting transfers between devices: 14.1 us -> 52.1 us  [the longest x4 18.6 us: to_columns(): lax.all_to_all(rows_block, 'ctx', split_axis=1, concat_axis=0, tiled=True)]
  transfers between devices with their start and end apart: 25 -> 52, of which waited for: 16 -> 25; matrix products, arithmetic and copies ran while one was open for 13% -> 24% of each run, Pallas kernels for 0% -> 5%
where the time goes in v1:
time: 861 us; the launch traced here: 852 us
  waiting for transfers between devices  438 us (51%)
  matrix products  104 us (12%)
  local copies, waits for them, and re-layouts  101 us (12%)
  starting transfers between devices  87.1 us (10%)
  other arithmetic  67.4 us (8%)
  Pallas kernels  40 us (5%)
  between operations  14.9 us (2%)
    all_to_all x4, waiting for transfers between devices, to_columns(): lax.all_to_all(rows_block, 'ctx', split_axis=1, concat_axis=0, tiled=True)  121 us
    dot_general x14, matrix products, dot(): lax.dot_general(left, right, (((left_dim,), (right_dim,)), ((), ())), pre...  104 us
    ppermute x4, waiting for transfers between devices, scatter_fsdp(): lax.ppermute(jnp.concatenate([piece(3, 0), piece(1, 0)]), 'fsdp', flip('f...  80 us
    all_to_all x2, waiting for transfers between devices, scatter_ctx(): lax.all_to_all(pair_sum, 'ctx', 0, 0, axis_index_groups=same_core_groups(...  74.4 us
    ppermute x4, waiting for transfers between devices, gather_fsdp(): from_y = lax.ppermute(block, 'fsdp', flip('fsdp', 4, 2))  55.4 us
    dynamic_update_slice x20, local copies, waits for them, and re-layouts, gather_fsdp(): out = lax.dynamic_update_slice_in_dim(out, piece, place, 0)  29.8 us
    ppermute x4, waiting for transfers between devices, scatter_fsdp(): last_y = lax.ppermute(send_y, 'fsdp', flip('fsdp', 4, 2))  24.6 us
    ppermute x4, waiting for transfers between devices, scatter_fsdp(): last_x = lax.ppermute(send_x, 'fsdp', flip('fsdp', 4, 1))  23.9 us
  transfers between devices with their start and end apart: 52, of which 25 were waited for; matrix products, arithmetic and copies ran while one was open for 24% of the time, Pallas kernels for 5%

profile of v1, /device:TPU:0, one launch (start us, length us, event | category | flops | bytes accessed | tf_op | source)
XLA Modules:
  0.0 852.3 jit_solution(15886008500779972480)
XLA Ops:
  19.9 39.2 %all-to-all-done = bf16[64,8,768]{2,0,1:T(8,128)(2,1)S(1)} async-done(((bf16[64,8,768]{2,0,1:T(8,128)(2,1)}), bf16[64,8,768]{2,0,1:T(8,128)(2,1)S(1)}, u32[]{:S(2)}, u32[]{:S(2)}) %all-to-all-start) | async-done | bytes 786464 | tf_op jit(solution)/shard_map/all_to_all | solution.py:117
  67.1 29.0 %all-to-all-done.4 = bf16[64,8,1024]{2,0,1:T(8,128)(2,1)S(1)} async-done(((bf16[64,8,1024]{2,0,1:T(8,128)(2,1)}), bf16[64,8,1024]{2,0,1:T(8,128)(2,1)S(1)}, u32[]{:S(2)}, u32[]{:S(2)}) %all-to-all-start.4) | async-done | bytes 1048608 | tf_op jit(solution)/shard_map/all_to_all | solution.py:117
  101.7 52.5 %all-to-all-done.3 = bf16[64,8,1024]{2,0,1:T(8,128)(2,1)S(1)} async-done(((bf16[64,8,1024]{2,0,1:T(8,128)(2,1)}), bf16[64,8,1024]{2,0,1:T(8,128)(2,1)S(1)}, u32[]{:S(2)}, u32[]{:S(2)}) %all-to-all-start.3) | async-done | bytes 1048608 | tf_op jit(solution)/shard_map/all_to_all | solution.py:117
  167.2 13.3 %collective-permute-done.1 = bf16[512,768]{1,0:T(8,128)(2,1)S(1)} collective-permute-done((bf16[512,768]{1,0:T(8,128)(2,1)S(1)}, bf16[512,768]{1,0:T(8,128)(2,1)S(1)}, u32[]{:S(2)}, u32[]{:S(2)}) %collective-permute-start.1) | collective-permute-done | bytes 786464 | tf_op jit(solution)/shard_map/ppermute | solution.py:42
  195.4 9.5 %project.1 = (bf16[1024,2048]{1,0:T(8,128)(2,1)}, bf16[1024,768]{1,0:T(8,128)(2,1)}) custom-call(bf16[1024,2048]{1,0:T(8,128)(2,1)} %all-gather.4.cloned.1.call-done.x_ref, bf16[2048,768]{1,0:T(8,128)(2,1)} %copy-done.1, f32[1024,256]{1,0:T(8,128)} %bitcast.165, f32[1024,256]{1,0:T(8,128)} %bitcast.163), custom_call_target="tpu_custom_call" | custom-call | tf_op jit(solution)/shard_map/project/pallas_call | solution.py:145
  204.9 10.4 %attend.1 = bf16[1024,256]{1,0:T(8,128)(2,1)} custom-call(s32[4]{0:T(128)} %and_select_fusion.2.lo_ref, s32[1,1024]{1,0:T(1,128)} %bitcast.203, bf16[1024,768]{1,0:T(8,128)(2,1)} %get-tuple-element.13.q_ref.k_ref.v_ref, bf16[1024,768]{1,0:T(8,128)(2,1)} %get-tuple-element.13.q_ref.k_ref.v_ref, bf16[1024,768]{1,0:T(8,128)(2,1)} %get-tuple-element.13.q_ref.k_ref.v_ref), custom_call_target="tpu_custom_call" | custom-call | tf_op jit(solution)/shard_map/attend/pallas_call | solution.py:216
  228.3 29.6 %collective-permute-done.14 = bf16[512,1024]{1,0:T(8,128)(2,1)} collective-permute-done((bf16[512,1024]{1,0:T(8,128)(2,1)}, bf16[512,1024]{1,0:T(8,128)(2,1)}, u32[]{:S(2)}, u32[]{:S(2)}) %collective-permute-start.14) | collective-permute-done | bytes 1048608 | tf_op jit(solution)/shard_map/ppermute | solution.py:42
  306.6 17.7 %collective-permute-done.8 = bf16[256,1024]{1,0:T(8,128)(2,1)} collective-permute-done((bf16[256,1024]{1,0:T(8,128)(2,1)}, bf16[256,1024]{1,0:T(8,128)(2,1)}, u32[]{:S(2)}, u32[]{:S(2)}) %collective-permute-start.8) | collective-permute-done | bytes 524320 | tf_op jit(solution)/shard_map/ppermute | solution.py:44
  342.4 9.9 %fusion.40 = f32[1024,1024]{0,1:T(8,128)} fusion(bf16[1024,2048]{1,0:T(8,128)(2,1)} %all-gather.8.cloned.1.call-done, bf16[2048,1024]{1,0:T(8,128)(2,1)} %constant_dynamic-update-slice_fusion), kind=kOutput, calls=%fused_computation.183 | convolution fusion | flops 4294967296 | bytes 12582912 | tf_op jit(solution)/shard_map/dot_general | solution.py:21
  363.1 13.5 %multiply_reduce_fusion = (f32[1024]{0:T(1024)S(1)}, f32[1024,2048]{1,0:T(8,128)S(1)}) fusion(bf16[1024,2048]{0,1:T(8,128)(2,1)} %bitcast.169, bf16[2048,2048]{1,0:T(8,128)(2,1)} %all-gather.6.cloned.1.call-done, bf16[1024,2048]{1,0:T(8,128)(2,1)} %all-gather.4.cloned.1.call-done.x_ref), kind=kOutput, calls=%fused_computation.2 | convolution fusion | flops 8598322176 | bytes 25169920 | tf_op jit(solution)/shard_map/dot_general | solution.py:21
  379.9 7.8 fusion.38
  387.8 9.7 %fusion.4 = (bf16[1024,1024]{1,0:T(8,128)(2,1)}, bf16[1024,1024]{1,0:T(8,128)(2,1)}, bf16[1024,1024]{1,0:T(8,128)(2,1)S(1)}) fusion(f32[1024,1024]{0,1:T(8,128)S(1)} %copy-done.46, f32[1024,1024]{1,0:T(8,128)S(1)} %fusion.38, bf16[1024,2048]{1,0:T(8,128)(2,1)S(1)} %multiply_convert_fusion, bf16[2048,1024]{1,0:T(8,128)(2,1)} %constant_dynamic-update-slice_fusion.5), kind=kOutput, calls=%fused_computation.14 | convolution fusion | flops 4310695936 | bytes 23068672 | tf_op jit(solution)/shard_map/dot_general | solution.py:21
  398.8 8.2 convolution_convert_fusion.5
  439.1 8.4 convolution_convert_fusion.2
  447.5 52.4 %all-to-all-done.5 = bf16[4,128,2048]{2,1,0:T(8,128)(2,1)} async-done(((bf16[4,128,2048]{2,1,0:T(8,128)(2,1)}), bf16[4,128,2048]{2,1,0:T(8,128)(2,1)}, u32[]{:S(2)}, u32[]{:S(2)}) %all-to-all-start.5) | async-done | bytes 2097184 | tf_op jit(solution)/shard_map/all_to_all | solution.py:110
  522.8 25.8 %collective-permute-done.31 = bf16[512,1024]{0,1:T(8,128)(2,1)S(1)} collective-permute-done((bf16[512,1024]{0,1:T(8,128)(2,1)S(1)}, bf16[512,1024]{0,1:T(8,128)(2,1)S(1)}, u32[]{:S(2)}, u32[]{:S(2)}) %collective-permute-start.31) | collective-permute-done | bytes 1048608 | tf_op jit(solution)/shard_map/ppermute | solution.py:68
  555.7 11.4 %collective-permute-done.32 = bf16[256,1024]{0,1:T(8,128)(2,1)S(1)} collective-permute-done((bf16[256,1024]{0,1:T(8,128)(2,1)S(1)}, bf16[256,1024]{0,1:T(8,128)(2,1)S(1)}, u32[]{:S(2)}, u32[]{:S(2)}) %collective-permute-start.32) | collective-permute-done | bytes 524320 | tf_op jit(solution)/shard_map/ppermute | solution.py:76
  574.0 13.0 %collective-permute-done.34 = bf16[256,1024]{0,1:T(8,128)(2,1)S(1)} collective-permute-done((bf16[256,1024]{0,1:T(8,128)(2,1)S(1)}, bf16[256,1024]{0,1:T(8,128)(2,1)S(1)}, u32[]{:S(2)}, u32[]{:S(2)}) %collective-permute-start.34) | collective-permute-done | bytes 524320 | tf_op jit(solution)/shard_map/ppermute | solution.py:77
  592.2 25.8 %collective-permute-done.27 = bf16[512,1024]{1,0:T(8,128)(2,1)} collective-permute-done((bf16[512,1024]{1,0:T(8,128)(2,1)}, bf16[512,1024]{1,0:T(8,128)(2,1)}, u32[]{:S(2)}, u32[]{:S(2)}) %collective-permute-start.27) | collective-permute-done | bytes 1048608 | tf_op jit(solution)/shard_map/ppermute | solution.py:68
  622.5 24.1 %collective-permute-done.23 = bf16[512,1024]{1,0:T(8,128)(2,1)} collective-permute-done((bf16[512,1024]{1,0:T(8,128)(2,1)}, bf16[512,1024]{1,0:T(8,128)(2,1)}, u32[]{:S(2)}, u32[]{:S(2)}) %collective-permute-start.23) | collective-permute-done | bytes 1048608 | tf_op jit(solution)/shard_map/ppermute | solution.py:68
  662.7 8.3 collective-permute-done.25
  694.1 20.1 %attend_back.1 = bf16[1024,768]{1,0:T(8,128)(2,1)} custom-call(s32[4]{0:T(128)} %and_select_fusion.2.lo_ref, s32[1,1024]{1,0:T(1,128)} %bitcast.204, bf16[1024,768]{1,0:T(8,128)(2,1)} %get-tuple-element.13.q_ref.k_ref.v_ref, bf16[1024,768]{1,0:T(8,128)(2,1)} %get-tuple-element.13.q_ref.k_ref.v_ref, bf16[1024,768]{1,0:T(8,128)(2,1)} %get-tuple-element.13.q_ref.k_ref.v_ref, ...), custom_call_target="tpu_custom_call" | custom-call | tf_op jit(solution)/shard_map/attend_back/pallas_call | solution.py:331
  771.3 16.5 %all-to-all-done.8 = bf16[8,64,768]{2,1,0:T(8,128)(2,1)S(1)} async-done(((bf16[8,64,768]{2,1,0:T(8,128)(2,1)}), bf16[8,64,768]{2,1,0:T(8,128)(2,1)S(1)}, u32[]{:S(2)}, u32[]{:S(2)}) %all-to-all-start.8) | async-done | bytes 786464 | tf_op jit(solution)/shard_map/all_to_all | solution.py:464
  818.7 22.0 %all-to-all-done.7 = bf16[4,128,2048]{2,1,0:T(8,128)(2,1)S(1)} async-done(((bf16[4,128,2048]{2,1,0:T(8,128)(2,1)}), bf16[4,128,2048]{2,1,0:T(8,128)(2,1)S(1)}, u32[]{:S(2)}, u32[]{:S(2)}) %all-to-all-start.7) | async-done | bytes 2097184 | tf_op jit(solution)/shard_map/all_to_all | solution.py:110
  (325 shorter events, 359.3 us)
Async XLA Ops:
  7.2 186.6 %all-gather.4.cloned.1.call-start = ((), (), s32[]{:S(2)}) async-start(), calls=%async_computation.14 | async-start | bytes 4718592 | tf_op jit(solution)/shard_map/all_gather | solution.py:386
  7.9 334.5 %all-gather.8.cloned.1.call-start = ((), (), s32[]{:S(2)}) async-start(), calls=%async_computation.17 | async-start | bytes 4718592 | tf_op jit(solution)/shard_map/all_gather | solution.py:388
  8.7 354.4 %all-gather.6.cloned.1.call-start = ((), (), s32[]{:S(2)}) async-start(), calls=%async_computation.15 | async-start | bytes 8650752 | tf_op jit(solution)/shard_map/all_gather | solution.py:387
  12.4 46.6 %all-to-all-start = ((bf16[64,8,768]{2,0,1:T(8,128)(2,1)}), bf16[64,8,768]{2,0,1:T(8,128)(2,1)S(1)}, u32[]{:S(2)}, u32[]{:S(2)}) async-start(bf16[64,8,768]{2,0,1:T(8,128)(2,1)} %pad_maximum_fusion.10), calls=%async_computation | async-start | bytes 1572864 | tf_op jit(solution)/shard_map/all_to_all | solution.py:117
  97.1 57.1 %all-to-all-start.3 = ((bf16[64,8,1024]{2,0,1:T(8,128)(2,1)}), bf16[64,8,1024]{2,0,1:T(8,128)(2,1)S(1)}, u32[]{:S(2)}, u32[]{:S(2)}) async-start(bf16[64,8,1024]{2,0,1:T(8,128)(2,1)} %bitcast.158), calls=%async_computation.3 | async-start | bytes 2097152 | tf_op jit(solution)/shard_map/all_to_all | solution.py:117
  154.2 61.1 %all-to-all-start.2 = ((bf16[64,8,1024]{2,0,1:T(8,128)(2,1)}), bf16[64,8,1024]{2,0,1:T(8,128)(2,1)}, u32[]{:S(2)}, u32[]{:S(2)}) async-start(bf16[64,8,1024]{2,0,1:T(8,128)(2,1)} %bitcast.159), calls=%async_computation.2 | async-start | bytes 2097152 | tf_op jit(solution)/shard_map/all_to_all | solution.py:117
  218.0 85.2 %all-to-all-start.1 = ((bf16[4,1024,256]{2,1,0:T(8,128)(2,1)}), bf16[4,1024,256]{2,1,0:T(8,128)(2,1)S(1)}, u32[]{:S(2)}, u32[]{:S(2)}) async-start(bf16[4,1024,256]{2,1,0:T(8,128)(2,1)} %broadcast_in_dim.29), calls=%async_computation.1 | async-start | bytes 4194304 | tf_op jit(solution)/shard_map/all_to_all | solution.py:87
  222.5 280.9 %reduce-scatter.3.cloned.1.call-start = ((), (), s32[]{:S(2)}) async-start(), calls=%async_computation.16 | async-start | bytes 4718592 | tf_op jit(solution)/shard_map/reduce_scatter | solution.py:439
  224.3 56.2 %collective-permute-start.6 = (bf16[512,1024]{1,0:T(8,128)(2,1)}, bf16[512,1024]{1,0:T(8,128)(2,1)}, u32[]{:S(2)}, u32[]{:S(2)}) collective-permute-start(bf16[512,1024]{1,0:T(8,128)(2,1)} %bitcast.12), channel_id=1, source_target_pairs={{0,16},{8,24},{16,0},{24,8},{1,17},{9,25},{17,1},{25,9},{2,18},{10... | collective-permute-start | bytes 3145736 | tf_op jit(solution)/shard_map/ppermute | solution.py:42
  224.8 59.0 %collective-permute-start.5 = (bf16[512,1024]{1,0:T(8,128)(2,1)}, bf16[512,1024]{1,0:T(8,128)(2,1)}, u32[]{:S(2)}, u32[]{:S(2)}) collective-permute-start(bf16[512,1024]{1,0:T(8,128)(2,1)} %bitcast.12), channel_id=1, source_target_pairs={{0,8},{8,0},{16,24},{24,16},{1,9},{9,1},{17,25},{25,17},{2,10},{10... | collective-permute-start | bytes 3145736 | tf_op jit(solution)/shard_map/ppermute | solution.py:41
  225.9 60.3 %collective-permute-start.13 = (bf16[512,1024]{1,0:T(8,128)(2,1)}, bf16[512,1024]{1,0:T(8,128)(2,1)}, u32[]{:S(2)}, u32[]{:S(2)}) collective-permute-start(bf16[512,1024]{1,0:T(8,128)(2,1)} %bitcast.181), channel_id=1, source_target_pairs={{0,8},{8,0},{16,24},{24,16},{1,9},{9,1},{17,25},{25,17},{2,10},{10... | collective-permute-start | bytes 3145736 | tf_op jit(solution)/shard_map/ppermute | solution.py:41
  226.8 76.1 %collective-permute-start.10 = (bf16[512,1024]{1,0:T(8,128)(2,1)S(1)}, bf16[512,1024]{1,0:T(8,128)(2,1)}, u32[]{:S(2)}, u32[]{:S(2)}) collective-permute-start(bf16[512,1024]{1,0:T(8,128)(2,1)S(1)} %bitcast.177), channel_id=1, source_target_pairs={{0,16},{8,24},{16,0},{24,8},{1,17},{9,25},{17,1},{25,9},{2,18},{10... | collective-permute-start | bytes 3145736 | tf_op jit(solution)/shard_map/ppermute | solution.py:42
  258.0 45.2 %collective-permute-start.9 = (bf16[512,1024]{1,0:T(8,128)(2,1)S(1)}, bf16[512,1024]{1,0:T(8,128)(2,1)}, u32[]{:S(2)}, u32[]{:S(2)}) collective-permute-start(bf16[512,1024]{1,0:T(8,128)(2,1)S(1)} %bitcast.178), channel_id=1, source_target_pairs={{0,8},{8,0},{16,24},{24,16},{1,9},{9,1},{17,25},{25,17},{2,10},{10... | collective-permute-start | bytes 3145736 | tf_op jit(solution)/shard_map/ppermute | solution.py:41
  280.4 54.9 %collective-permute-start.16 = (bf16[256,1024]{1,0:T(8,128)(2,1)}, bf16[256,1024]{1,0:T(8,128)(2,1)}, u32[]{:S(2)}, u32[]{:S(2)}) collective-permute-start(bf16[256,1024]{1,0:T(8,128)(2,1)} %slice.119), channel_id=1, source_target_pairs={{0,8},{8,0},{16,24},{24,16},{1,9},{9,1},{17,25},{25,17},{2,10},{10... | collective-permute-start | bytes 1572872 | tf_op jit(solution)/shard_map/ppermute | solution.py:44
  286.2 42.9 %collective-permute-start.7 = (bf16[256,1024]{1,0:T(8,128)(2,1)}, bf16[256,1024]{1,0:T(8,128)(2,1)}, u32[]{:S(2)}, u32[]{:S(2)}) collective-permute-start(bf16[256,1024]{1,0:T(8,128)(2,1)} %slice.114), channel_id=1, source_target_pairs={{0,16},{8,24},{16,0},{24,8},{1,17},{9,25},{17,1},{25,9},{2,18},{10... | collective-permute-start | bytes 1572872 | tf_op jit(solution)/shard_map/ppermute | solution.py:43
  303.2 49.1 %collective-permute-start.4 = (bf16[4,1024,256]{2,1,0:T(8,128)(2,1)S(1)}, bf16[4,1024,256]{2,1,0:T(8,128)(2,1)}, u32[]{:S(2)}, u32[]{:S(2)}) collective-permute-start(bf16[4,1024,256]{2,1,0:T(8,128)(2,1)S(1)} %all-to-all-done.1), channel_id=1, source_target_pairs={{0,1},{1,0},{2,3},{3,2},{4,5},{5,4},{6,7},{7,6},{8,9},{9,8},{10,11... | collective-permute-start | bytes 6291464 | tf_op jit(solution)/shard_map/ppermute | solution.py:95
  434.3 65.6 %all-to-all-start.5 = ((bf16[4,128,2048]{2,1,0:T(8,128)(2,1)}), bf16[4,128,2048]{2,1,0:T(8,128)(2,1)}, u32[]{:S(2)}, u32[]{:S(2)}) async-start(bf16[4,128,2048]{2,1,0:T(8,128)(2,1)} %fusion.1), calls=%async_computation.6 | async-start | bytes 4194304 | tf_op jit(solution)/shard_map/all_to_all | solution.py:110
  439.0 404.8 %reduce-scatter.5.cloned.1.call-start = ((), (), s32[]{:S(2)}) async-start(), calls=%async_computation.18 | async-start | bytes 8650752 | tf_op jit(solution)/shard_map/reduce_scatter | solution.py:470
  568.6 49.4 %collective-permute-start.27 = (bf16[512,1024]{1,0:T(8,128)(2,1)}, bf16[512,1024]{1,0:T(8,128)(2,1)}, u32[]{:S(2)}, u32[]{:S(2)}) collective-permute-start(bf16[512,1024]{1,0:T(8,128)(2,1)} %pad_maximum_fusion.4), channel_id=1, source_target_pairs={{0,8},{8,0},{16,24},{24,16},{1,9},{9,1},{17,25},{25,17},{2,10},{10... | collective-permute-start | bytes 3145736 | tf_op jit(solution)/shard_map/ppermute | solution.py:68
  571.7 78.6 %collective-permute-start.29 = (bf16[512,1024]{1,0:T(8,128)(2,1)}, bf16[512,1024]{1,0:T(8,128)(2,1)}, u32[]{:S(2)}, u32[]{:S(2)}) collective-permute-start(bf16[512,1024]{1,0:T(8,128)(2,1)} %pad_maximum_fusion.5), channel_id=1, source_target_pairs={{0,16},{8,24},{16,0},{24,8},{1,17},{9,25},{17,1},{25,9},{2,18},{10... | collective-permute-start | bytes 3145736 | tf_op jit(solution)/shard_map/ppermute | solution.py:71
  574.0 72.6 %collective-permute-start.23 = (bf16[512,1024]{1,0:T(8,128)(2,1)}, bf16[512,1024]{1,0:T(8,128)(2,1)}, u32[]{:S(2)}, u32[]{:S(2)}) collective-permute-start(bf16[512,1024]{1,0:T(8,128)(2,1)} %pad_maximum_fusion.1), channel_id=1, source_target_pairs={{0,8},{8,0},{16,24},{24,16},{1,9},{9,1},{17,25},{25,17},{2,10},{10... | collective-permute-start | bytes 3145736 | tf_op jit(solution)/shard_map/ppermute | solution.py:68
  588.6 70.6 %all-to-all-start.11 = ((bf16[8,64,1024]{2,1,0:T(8,128)(2,1)}), bf16[8,64,1024]{2,1,0:T(8,128)(2,1)S(1)}, u32[]{:S(2)}, u32[]{:S(2)}) async-start(bf16[8,64,1024]{2,1,0:T(8,128)(2,1)} %bitcast.43), calls=%async_computation.13 | async-start | bytes 2097152 | tf_op jit(solution)/shard_map/all_to_all | solution.py:464
  621.7 49.2 %collective-permute-start.25 = (bf16[512,1024]{1,0:T(8,128)(2,1)}, bf16[512,1024]{1,0:T(8,128)(2,1)}, u32[]{:S(2)}, u32[]{:S(2)}) collective-permute-start(bf16[512,1024]{1,0:T(8,128)(2,1)} %pad_maximum_fusion.2), channel_id=1, source_target_pairs={{0,16},{8,24},{16,0},{24,8},{1,17},{9,25},{17,1},{25,9},{2,18},{10... | collective-permute-start | bytes 3145736 | tf_op jit(solution)/shard_map/ppermute | solution.py:71
  788.8 51.9 %all-to-all-start.7 = ((bf16[4,128,2048]{2,1,0:T(8,128)(2,1)}), bf16[4,128,2048]{2,1,0:T(8,128)(2,1)S(1)}, u32[]{:S(2)}, u32[]{:S(2)}) async-start(bf16[4,128,2048]{2,1,0:T(8,128)(2,1)} %fusion), calls=%async_computation.8 | async-start | bytes 4194304 | tf_op jit(solution)/shard_map/all_to_all | solution.py:110
  (79 other events, 1429.1 us)
Sparse Core Ops, SparseCore 0:
  9.6 81.1 all-gather.3
  92.4 67.6 all-gather.7
  163.1 102.2 all-gather.5
  407.2 62.2 reduce-scatter.2
  512.9 158.7 reduce-scatter.4

commit v2 on v1

--- a/solution.py
+++ b/solution.py
@@ -12,7 +12,9 @@
 EPSILON = 1e-05
 ROPE_BASE = 130000.0
 BLOCK = 256
+UNIT = 256
 VMEM_LIMIT = 56 * 1024 * 1024
+GIGA = 1000 * 1000 * 1000
 LOW = jnp.bfloat16
 F32 = jnp.float32
 
@@ -31,60 +33,56 @@
     return [[2 * i + core for i in range(size // 2)] for core in (0, 1)]
 
 
-def gather_fsdp(block):
-    size = lax.axis_size("fsdp")
-    if size != 4:
-        return lax.all_gather(block, "fsdp", axis=0, tiled=True)
-    me = lax.axis_index("fsdp")
-    rows = block.shape[0]
-    half = rows // 2
-    from_x = lax.ppermute(block, "fsdp", flip("fsdp", 4, 1))
-    from_y = lax.ppermute(block, "fsdp", flip("fsdp", 4, 2))
-    far_top = lax.ppermute(from_x[:half], "fsdp", flip("fsdp", 4, 2))
-    far_low = lax.ppermute(from_y[half:], "fsdp", flip("fsdp", 4, 1))
-    out = jnp.zeros((4 * rows, block.shape[1]), block.dtype)
-    for piece, place in (
-        (block, me * rows),
-        (from_x, (me ^ 1) * rows),
-        (from_y, (me ^ 2) * rows),
-        (far_top, (me ^ 3) * rows),
-        (far_low, (me ^ 3) * rows + half),
-    ):
-        out = lax.dynamic_update_slice_in_dim(out, piece, place, 0)
-    return out
-
-
-def scatter_fsdp(part):
-    size = lax.axis_size("fsdp")
-    if size != 4:
-        return lax.psum_scatter(part, "fsdp", scatter_dimension=0, tiled=True).astype(F32)
-    me = lax.axis_index("fsdp")
-    rows = part.shape[0] // 4
-    half = rows // 2
-
-    def piece(bits, low):
-        return lax.dynamic_slice_in_dim(part, (me ^ bits) * rows + low * half, half, 0)
-
-    over_x = lax.ppermute(
-        jnp.concatenate([piece(3, 0), piece(1, 0)]), "fsdp", flip("fsdp", 4, 1)
-    )
-    over_y = lax.ppermute(
-        jnp.concatenate([piece(3, 1), piece(2, 1)]), "fsdp", flip("fsdp", 4, 2)
-    )
-    send_y = (piece(2, 0).astype(F32) + over_x[:half].astype(F32)).astype(part.dtype)
-    send_x = (piece(1, 1).astype(F32) + over_y[:half].astype(F32)).astype(part.dtype)
-    last_y = lax.ppermute(send_y, "fsdp", flip("fsdp", 4, 2))
-    last_x = lax.ppermute(send_x, "fsdp", flip("fsdp", 4, 1))
-    top = piece(0, 0).astype(F32) + over_x[half:].astype(F32) + last_y.astype(F32)
-    low = piece(0, 1).astype(F32) + over_y[half:].astype(F32) + last_x.astype(F32)
-    return jnp.concatenate([top, low])
-
-
-def gather_ctx(block):
+def after(value, *others):
+    return lax.optimization_barrier((value,) + others)[0]
+
+
+def near(block):
+    return (
+        lax.ppermute(block, "fsdp", flip("fsdp", 4, 1)),
+        lax.ppermute(block, "fsdp", flip("fsdp", 4, 2)),
+    )
+
+
+def far(pieces):
+    from_x, from_y = pieces
+    half = from_x.shape[0] // 2
+    return (
+        lax.ppermute(from_x[:half], "fsdp", flip("fsdp", 4, 2)),
+        lax.ppermute(from_y[half:], "fsdp", flip("fsdp", 4, 1)),
+    )
+
+
+def reduce_near(part):
+    return (
+        lax.ppermute(part[0], "fsdp", flip("fsdp", 4, 1)),
+        lax.ppermute(part[1], "fsdp", flip("fsdp", 4, 2)),
+    )
+
+
+def reduce_far(part, landed):
+    over_x, over_y = landed
+    unit = over_x.shape[0] // 2
+    send_y = (part[2][:unit].astype(F32) + over_x[:unit].astype(F32)).astype(LOW)
+    send_x = (part[2][unit : 2 * unit].astype(F32) + over_y[:unit].astype(F32)).astype(LOW)
+    return (
+        lax.ppermute(send_y, "fsdp", flip("fsdp", 4, 2)),
+        lax.ppermute(send_x, "fsdp", flip("fsdp", 4, 1)),
+    )
+
+
+def reduce_own(part, landed, last):
+    over_x, over_y = landed
+    unit = over_x.shape[0] // 2
+    top = part[2][2 * unit : 3 * unit].astype(F32) + over_x[unit:].astype(F32)
+    low = part[2][3 * unit :].astype(F32) + over_y[unit:].astype(F32)
+    return jnp.concatenate([top + last[0].astype(F32), low + last[1].astype(F32)])
+
+
+def spread_cores(block):
     size = lax.axis_size("ctx")
     pairs = size // 2
-    core = lax.axis_index("ctx") % 2
-    mine = lax.all_to_all(
+    return lax.all_to_all(
         jnp.broadcast_to(block[None], (pairs,) + block.shape),
         "ctx",
         0,
@@ -92,24 +90,34 @@
         axis_index_groups=same_core_groups(size),
         tiled=True,
     )
-    other = lax.ppermute(mine, "ctx", flip("ctx", size, 1))
-    first = jnp.where(core == 0, mine, other)
-    second = jnp.where(core == 0, other, mine)
-    return jnp.stack([first, second], axis=1).reshape((size,) + block.shape)
-
-
-def scatter_ctx(part):
+
+
+def other_core(value):
+    return lax.ppermute(value, "ctx", flip("ctx", lax.axis_size("ctx"), 1))
+
+
+def pair_sums(part):
     size = lax.axis_size("ctx")
-    pairs = size // 2
     core = lax.axis_index("ctx") % 2
-    shaped = part.reshape(pairs, 2, part.shape[0] // size, part.shape[1])
+    shaped = part.reshape(size // 2, 2, part.shape[0] // size, part.shape[1])
     mine = lax.dynamic_index_in_dim(shaped, core, 1, keepdims=False)
     theirs = lax.dynamic_index_in_dim(shaped, 1 - core, 1, keepdims=False)
-    got = lax.ppermute(theirs, "ctx", flip("ctx", size, 1))
-    pair_sum = (mine.astype(F32) + got.astype(F32)).astype(part.dtype)
-    landed = lax.all_to_all(
-        pair_sum, "ctx", 0, 0, axis_index_groups=same_core_groups(size), tiled=True
-    )
+    got = other_core(theirs)
+    return (mine.astype(F32) + got.astype(F32)).astype(part.dtype)
+
+
+def swap_chips(sums):
+    return lax.all_to_all(
+        sums,
+        "ctx",
+        0,
+        0,
+        axis_index_groups=same_core_groups(lax.axis_size("ctx")),
+        tiled=True,
+    )
+
+
+def total(landed):
     return jnp.sum(landed.astype(F32), axis=0)
 
 
@@ -125,7 +133,29 @@
     return jnp.where(lane % HD < HD // 2, down, up)
 
 
-def project_kernel(width, x_ref, w_ref, cos_ref, sin_ref, unit_ref, out_ref):
+def units_of(pieces):
+    return [
+        (index, unit)
+        for index, piece in enumerate(pieces)
+        for unit in range(piece.shape[0] // UNIT)
+    ]
+
+
+def gather_units(places_ref, pieces, out_ref):
+    for step, (index, unit) in enumerate(units_of(pieces)):
+        rows = pl.ds(pl.multiple_of(places_ref[step] * UNIT, UNIT), UNIT)
+        out_ref[rows, :] = pieces[index][unit * UNIT : (unit + 1) * UNIT, :]
+
+
+def project_kernel(count, places_ref, x_ref, cos_ref, sin_ref, *refs):
+    pieces = refs[:count]
+    unit_ref, out_ref, w_ref = refs[count:]
+    width = out_ref.shape[1] // 3
+
+    @pl.when(pl.program_id(0) == 0)
+    def _():
+        gather_units(places_ref, pieces, w_ref)
+
     x = x_ref[...].astype(F32)
     inverse = lax.rsqrt(jnp.mean(x * x, axis=-1, keepdims=True) + EPSILON)
     unit = (x * inverse).astype(LOW)
@@ -139,29 +169,201 @@
         out_ref[:, columns] = value.astype(LOW)
 
 
-def project(x_all, w_qkv, cos, sin):
+def project(places, x_all, pieces, cos, sin):
     count, features = x_all.shape
-    width = w_qkv.shape[1] // 3
+    wide = pieces[0].shape[1]
+    width = wide // 3
     return pl.pallas_call(
-        functools.partial(project_kernel, width),
-        grid=(count // BLOCK,),
-        in_specs=[
-            pl.BlockSpec((BLOCK, features), lambda i: (i, 0)),
-            pl.BlockSpec((features, 3 * width), lambda i: (0, 0)),
-            pl.BlockSpec((BLOCK, width), lambda i: (i, 0)),
-            pl.BlockSpec((BLOCK, width), lambda i: (i, 0)),
-        ],
-        out_specs=[
-            pl.BlockSpec((BLOCK, features), lambda i: (i, 0)),
-            pl.BlockSpec((BLOCK, 3 * width), lambda i: (i, 0)),
-        ],
+        functools.partial(project_kernel, len(pieces)),
+        grid_spec=pltpu.PrefetchScalarGridSpec(
+            num_scalar_prefetch=1,
+            grid=(count // BLOCK,),
+            in_specs=[
+                pl.BlockSpec((BLOCK, features), lambda i, p: (i, 0)),
+                pl.BlockSpec((BLOCK, width), lambda i, p: (i, 0)),
+                pl.BlockSpec((BLOCK, width), lambda i, p: (i, 0)),
+            ]
+            + [pl.BlockSpec(piece.shape, lambda i, p: (0, 0)) for piece in pieces],
+            out_specs=[
+                pl.BlockSpec((BLOCK, features), lambda i, p: (i, 0)),
+                pl.BlockSpec((BLOCK, wide), lambda i, p: (i, 0)),
+            ],
+            scratch_shapes=[pltpu.VMEM((features, wide), LOW)],
+        ),
         out_shape=[
             jax.ShapeDtypeStruct((count, features), LOW),
-            jax.ShapeDtypeStruct((count, 3 * width), LOW),
+            jax.ShapeDtypeStruct((count, wide), LOW),
         ],
         compiler_params=pltpu.CompilerParams(vmem_limit_bytes=VMEM_LIMIT),
+        cost_estimate=pl.CostEstimate(flops=9 * GIGA, bytes_accessed=0, transcendentals=0),
         name="project",
-    )(x_all, w_qkv, cos, sin)
+    )(places, x_all, cos, sin, *pieces)
+
+
+def open_kernel(count, places_ref, left_ref, *refs):
+    gate_pieces, up_pieces = refs[:count], refs[count : 2 * count]
+    gate_ref, up_ref, hidden_ref, w_gate_ref, w_up_ref = refs[2 * count :]
+    gather_units(places_ref, gate_pieces, w_gate_ref)
+    gather_units(places_ref, up_pieces, w_up_ref)
+    left = left_ref[...]
+    gate = dot(left, w_gate_ref[...], 1, 0)
+    gate_ref[...] = gate
+    up = dot(left, w_up_ref[...], 1, 0)
+    up_ref[...] = up
+    hidden_ref[...] = (gate * jax.nn.sigmoid(gate) * up).astype(LOW)
+
+
+def open_units(places, left, pieces):
+    count, features = left.shape
+    hidden = pieces[0].shape[1] // 2
+    blocks = hidden // UNIT
+    column = pl.BlockSpec((count, UNIT), lambda j, p: (0, j))
+    return pl.pallas_call(
+        functools.partial(open_kernel, len(pieces)),
+        grid_spec=pltpu.PrefetchScalarGridSpec(
+            num_scalar_prefetch=1,
+            grid=(blocks,),
+            in_specs=[pl.BlockSpec((count, features), lambda j, p: (0, 0))]
+            + [pl.BlockSpec((w.shape[0], UNIT), lambda j, p: (0, j)) for w in pieces]
+            + [pl.BlockSpec((w.shape[0], UNIT), lambda j, p: (0, j + blocks)) for w in pieces],
+            out_specs=[column] * 3,
+            scratch_shapes=[pltpu.VMEM((features, UNIT), LOW)] * 2,
+        ),
+        out_shape=[
+            jax.ShapeDtypeStruct((count, hidden), F32),
+            jax.ShapeDtypeStruct((count, hidden), F32),
+            jax.ShapeDtypeStruct((count, hidden), LOW),
+        ],
+        compiler_params=pltpu.CompilerParams(vmem_limit_bytes=VMEM_LIMIT),
+        cost_estimate=pl.CostEstimate(flops=12 * GIGA, bytes_accessed=0, transcendentals=0),
+        name="open_units",
+    )(places, left, *pieces, *pieces)
+
+
+def close_kernel(count, places_ref, back_ref, gate_ref, up_ref, *refs):
+    pieces = refs[:count]
+    out_ref, w_ref = refs[count:]
+    gather_units(places_ref, pieces, w_ref)
+    d_hidden = dot(back_ref[...], w_ref[...], 1, 0)
+    gate = gate_ref[...]
+    sigmoid = jax.nn.sigmoid(gate)
+    scaled = d_hidden * sigmoid
+    out_ref[0] = (scaled * up_ref[...] * (1.0 + gate * (1.0 - sigmoid))).astype(LOW)
+    out_ref[1] = (scaled * gate).astype(LOW)
+
+
+def close_units(places, back, gate, up, pieces):
+    count, features = back.shape
+    hidden = gate.shape[1]
+    column = pl.BlockSpec((count, UNIT), lambda j, p: (0, j))
+    return pl.pallas_call(
+        functools.partial(close_kernel, len(pieces)),
+        grid_spec=pltpu.PrefetchScalarGridSpec(
+            num_scalar_prefetch=1,
+            grid=(hidden // UNIT,),
+            in_specs=[pl.BlockSpec((count, features), lambda j, p: (0, 0)), column, column]
+            + [pl.BlockSpec((w.shape[0], UNIT), lambda j, p: (0, j)) for w in pieces],
+            out_specs=pl.BlockSpec((2, count, UNIT), lambda j, p: (0, 0, j)),
+            scratch_shapes=[pltpu.VMEM((features, UNIT), LOW)],
+        ),
+        out_shape=jax.ShapeDtypeStruct((2, count, hidden), LOW),
+        compiler_params=pltpu.CompilerParams(vmem_limit_bytes=VMEM_LIMIT),
+        cost_estimate=pl.CostEstimate(flops=7 * GIGA, bytes_accessed=0, transcendentals=0),
+        name="close_units",
+    )(places, back, gate, up, *pieces)
+
+
+def times_rows_kernel(pieces, places_ref, left_ref, *refs):
+    out_ref, w_ref = refs[len(pieces) :]
+    step = pl.program_id(0)
+    first = 0
+    for ref, units in zip(refs, pieces):
+
+        @pl.when((step >= first) & (step < first + units))
+        def _():
+            w_ref[...] = ref[...]
+
+        first += units
+    parts, unused, width = left_ref.shape
+    total_ = dot(left_ref[0], w_ref[:, :width], 1, 1)
+    for part in range(1, parts):
+        total_ += dot(left_ref[part], w_ref[:, part * width : (part + 1) * width], 1, 1)
+    out_ref[...] = total_.astype(LOW)
+
+
+def times_rows(places, left, pieces):
+    parts, count, width = left.shape
+    units = [piece.shape[0] // UNIT for piece in pieces]
+    firsts = [sum(units[:index]) for index in range(len(units))]
+
+    def spec(first, held):
+        return pl.BlockSpec(
+            (UNIT, parts * width), lambda s, p: (jnp.clip(s - first, 0, held - 1), 0)
+        )
+
+    return pl.pallas_call(
+        functools.partial(times_rows_kernel, units),
+        grid_spec=pltpu.PrefetchScalarGridSpec(
+            num_scalar_prefetch=1,
+            grid=(sum(units),),
+            in_specs=[pl.BlockSpec(left.shape, lambda s, p: (0, 0, 0))]
+            + [spec(first, held) for first, held in zip(firsts, units)],
+            out_specs=pl.BlockSpec((count, UNIT), lambda s, p: (0, p[s])),
+            scratch_shapes=[pltpu.VMEM((UNIT, parts * width), LOW)],
+        ),
+        out_shape=jax.ShapeDtypeStruct((count, sum(units) * UNIT), LOW),
+        compiler_params=pltpu.CompilerParams(vmem_limit_bytes=VMEM_LIMIT),
+        cost_estimate=pl.CostEstimate(
+            flops=2 * parts * count * width * sum(units) * UNIT, bytes_accessed=0, transcendentals=0
+        ),
+        name="times_rows",
+    )(places, left, *pieces)
+
+
+def weight_grad_kernel(outs, pairs, order_ref, *refs):
+    step = pl.program_id(0)
+    values = []
+    for left_ref, right_ref in zip(refs[:pairs], refs[pairs : 2 * pairs]):
+        left = left_ref[...]
+        for part in range(right_ref.shape[0]):
+            values.append(dot(left, right_ref[part], 0, 0).astype(LOW))
+    value = values[0] if len(values) == 1 else jnp.concatenate(values, axis=1)
+    first = 0
+    for ref, units in zip(refs[2 * pairs :], outs):
+
+        @pl.when((step >= first) & (step < first + units))
+        def _():
+            ref[...] = value
+
+        first += units
+
+
+def weight_grad(order, outs, *pairs):
+    lefts = [left for left, unused in pairs]
+    rights = [right for unused, right in pairs]
+    count, features = lefts[0].shape
+    wide = sum(right.shape[0] * right.shape[2] for right in rights)
+    firsts = [sum(outs[:index]) for index in range(len(outs))]
+
+    def spec(first, held):
+        return pl.BlockSpec((UNIT, wide), lambda s, p: (jnp.clip(s - first, 0, held - 1), 0))
+
+    return pl.pallas_call(
+        functools.partial(weight_grad_kernel, outs, len(pairs)),
+        grid_spec=pltpu.PrefetchScalarGridSpec(
+            num_scalar_prefetch=1,
+            grid=(features // UNIT,),
+            in_specs=[pl.BlockSpec((count, UNIT), lambda s, p: (0, p[s]))] * len(pairs)
+            + [pl.BlockSpec(right.shape, lambda s, p: (0, 0, 0)) for right in rights],
+            out_specs=[spec(first, held) for first, held in zip(firsts, outs)],
+        ),
+        out_shape=[jax.ShapeDtypeStruct((held * UNIT, wide), LOW) for held in outs],
+        compiler_params=pltpu.CompilerParams(vmem_limit_bytes=VMEM_LIMIT),
+        cost_estimate=pl.CostEstimate(
+            flops=2 * count * wide * features, bytes_accessed=0, transcendentals=0
+        ),
+        name="weight_grad",
+    )(order, *lefts, *rights)
 
 
 def masked_scores(key, query, key_block, query_block, starts):
@@ -229,6 +431,7 @@
         ),
         out_shape=jax.ShapeDtypeStruct((count, width), LOW),
         compiler_params=pltpu.CompilerParams(vmem_limit_bytes=VMEM_LIMIT),
+        cost_estimate=pl.CostEstimate(flops=10 * GIGA, bytes_accessed=0, transcendentals=0),
         name="attend",
     )(lows, starts, qkv, qkv, qkv)
 
@@ -352,8 +555,91 @@
         ),
         out_shape=jax.ShapeDtypeStruct((count, 3 * width), LOW),
         compiler_params=pltpu.CompilerParams(vmem_limit_bytes=VMEM_LIMIT),
+        cost_estimate=pl.CostEstimate(flops=20 * GIGA, bytes_accessed=0, transcendentals=0),
         name="attend_back",
     )(lows, starts, qkv, qkv, qkv, back, cos, sin)
+
+
+def blend_kernel(core_ref, x_ref, own_ref, other_ref, w_ref, unit_ref, mixed_ref):
+    core = core_ref[0]
+    pieces = []
+    for chip in range(own_ref.shape[0]):
+        own, other = own_ref[chip], other_ref[chip]
+        pieces.append(jnp.where(core == 0, own, other))
+        pieces.append(jnp.where(core == 0, other, own))
+    attended = jnp.concatenate(pieces, axis=1)
+    mixed = x_ref[...].astype(F32) + dot(attended, w_ref[...], 1, 1)
+    mixed_ref[...] = mixed
+    inverse = lax.rsqrt(jnp.mean(mixed * mixed, axis=-1, keepdims=True) + EPSILON)
+    unit_ref[...] = (mixed * inverse).astype(LOW)
+
+
+def blend(core, x_all, own, other, w_out):
+    count, features = x_all.shape
+    chips, unused, width = own.shape
+    return pl.pallas_call(
+        blend_kernel,
+        grid_spec=pltpu.PrefetchScalarGridSpec(
+            num_scalar_prefetch=1,
+            grid=(count // BLOCK,),
+            in_specs=[
+                pl.BlockSpec((BLOCK, features), lambda i, core: (i, 0)),
+                pl.BlockSpec((chips, BLOCK, width), lambda i, core: (0, i, 0)),
+                pl.BlockSpec((chips, BLOCK, width), lambda i, core: (0, i, 0)),
+                pl.BlockSpec((features, features), lambda i, core: (0, 0)),
+            ],
+            out_specs=[
+                pl.BlockSpec((BLOCK, features), lambda i, core: (i, 0)),
+                pl.BlockSpec((BLOCK, features), lambda i, core: (i, 0)),
+            ],
+        ),
+        out_shape=[
+            jax.ShapeDtypeStruct((count, features), LOW),
+            jax.ShapeDtypeStruct((count, features), F32),
+        ],
+        compiler_params=pltpu.CompilerParams(vmem_limit_bytes=VMEM_LIMIT),
+        cost_estimate=pl.CostEstimate(flops=15 * GIGA, bytes_accessed=0, transcendentals=0),
+        name="blend",
+    )(core, x_all, own, other, w_out)
+
+
+def finish_kernel(parts, scaled_parts, rows_ref, gain_ref, *refs):
+    weights = refs[:scaled_parts]
+    grads = refs[scaled_parts : scaled_parts + parts]
+    gain_grad_ref = refs[scaled_parts + parts]
+    width = rows_ref.shape[2] // parts
+
+    @pl.when(pl.program_id(0) == 0)
+    def _():
+        gain_grad_ref[...] = jnp.zeros_like(gain_grad_ref)
+
+    gain = gain_ref[...]
+    for part in range(parts):
+        raw = rows_ref[0, :, part * width : (part + 1) * width].astype(F32)
+        if part < scaled_parts:
+            product = raw * weights[part][...].astype(F32)
+            gain_grad_ref[...] += jnp.sum(product, axis=1, keepdims=True)
+            raw = raw * gain
+        grads[part][...] = raw
+
+
+def finish(rows, gain, weights, parts):
+    size, share, wide = rows.shape
+    width = wide // parts
+    column = pl.BlockSpec((share, 1), lambda i: (0, 0))
+    block = pl.BlockSpec((share, width), lambda i: (0, i))
+    out = pl.pallas_call(
+        functools.partial(finish_kernel, parts, len(weights)),
+        grid=(size,),
+        in_specs=[pl.BlockSpec((1, share, wide), lambda i: (i, 0, 0)), column]
+        + [block] * len(weights),
+        out_specs=[block] * parts + [column],
+        out_shape=[jax.ShapeDtypeStruct((share, size * width), F32)] * parts
+        + [jax.ShapeDtypeStruct((share, 1), F32)],
+        compiler_params=pltpu.CompilerParams(vmem_limit_bytes=VMEM_LIMIT),
+        name="finish",
+    )(rows, gain, *weights)
+    return out[:parts], out[parts][:, 0]
 
 
 def local(
@@ -377,16 +663,61 @@
     here = lax.axis_index("ctx") * rows
     share = w_query.shape[0]
 
+    core = (lax.axis_index("ctx") % 2).astype(jnp.int32).reshape(1)
+    square = lax.axis_size("fsdp") == 4
+
+    def pull_near(block, *others):
+        return near(after(block, *others)) if square else ()
+
+    def pull_far(pieces):
+        return far(pieces) if square else ()
+
+    def pulled(block, near_pieces, far_pieces):
+        if square:
+            return (block,) + tuple(near_pieces) + tuple(far_pieces)
+        return (lax.all_gather(block, "fsdp", axis=0, tiled=True),)
+
+    def push_near(part):
+        return reduce_near(part) if square else ()
+
+    def push_far(part, landed):
+        return reduce_far(part, landed) if square else ()
+
+    def pushed(part, landed, last):
+        if square:
+            return reduce_own(part, landed, last).astype(LOW)
+        return lax.psum_scatter(part[0], "fsdp", scatter_dimension=0, tiled=True)
+
+    def to_rows(value):
+        value = value.reshape(n_c, share, -1)
+        return lax.all_to_all(value, "ctx", split_axis=0, concat_axis=0, tiled=True)
+
+    me = lax.axis_index("fsdp")
+    if square:
+        places = [(me ^ bits) * 2 + low for bits in range(4) for low in range(2)]
+        order = [
+            (me ^ bits) * 2 + low
+            for bits, low in ((3, 0), (1, 0), (3, 1), (2, 1), (2, 0), (1, 1), (0, 0), (0, 1))
+        ]
+        outs = (2, 2, 4)
+    else:
+        places = order = range(features // UNIT)
+        outs = (features // UNIT,)
+    places, order = (jnp.stack([jnp.int32(place) for place in p]) for p in (places, order))
+
     gain_a = gain_attn.astype(F32)[:, None]
     gain_m = gain_mlp.astype(F32)[:, None]
 
     def scaled(weight, gain):
         return (weight.astype(F32) * gain).astype(LOW)
 
+
+    def paired(left, right):
+        return jnp.concatenate(
+            [left.reshape(share, n_c, -1), right.reshape(share, n_c, -1)], axis=2
+        ).reshape(share, -1)
+
     x_all = lax.all_gather(tokens, "ctx", axis=0, tiled=True)
-    out_all = lax.all_gather(w_out, ("fsdp", "ctx"), axis=0, tiled=True)
-    back_all = lax.all_gather(cotangent, "ctx", axis=0, tiled=True)
-
     stacked = jnp.concatenate(
         [
             scaled(w, gain_a).reshape(share, n_c, width)
@@ -394,10 +725,12 @@
         ],
         axis=2,
     ).reshape(share, 3 * features)
-    w_qkv = gather_fsdp(to_columns(stacked))
-    col_gate = gather_fsdp(to_columns(scaled(w_gate, gain_m)))
-    col_up = gather_fsdp(to_columns(scaled(w_up, gain_m)))
-    col_down = gather_fsdp(to_columns(w_down))
+    out_all = lax.all_gather(after(w_out, stacked), ("fsdp", "ctx"), axis=0, tiled=True)
+    qkv_rows = to_columns(stacked)
+    qkv_near = pull_near(qkv_rows)
+    two_rows = to_columns(after(paired(scaled(w_gate, gain_m), scaled(w_up, gain_m)), qkv_rows))
+    qkv_far = pull_far(qkv_near)
+    w_qkv = pulled(qkv_rows, qkv_near, qkv_far)
 
     position = jnp.arange(group, dtype=jnp.int32)
     doc_ends = jnp.cumsum(doc_lengths[0])
@@ -405,52 +738,78 @@
     starts = jnp.max(
         jnp.where(position[:, None] >= doc_starts[None, :], doc_starts[None, :], 0), axis=1
     ).astype(jnp.int32)
-    places = (position - starts).astype(F32)
+    turns = (position - starts).astype(F32)
     half = HD // 2
     lane = jnp.arange(128, dtype=jnp.int32)
     inv_freq = ROPE_BASE ** (-2.0 * (lane % half).astype(F32) / HD)
-    angles = places[:, None] * inv_freq[None, :]
+    angles = turns[:, None] * inv_freq[None, :]
     sign = jnp.where(lane % HD < half, -1.0, 1.0).astype(F32)
     cos = jnp.tile(jnp.cos(angles), (1, width // 128))
     sin = jnp.tile(jnp.sin(angles) * sign[None, :], (1, width // 128))
     lows = starts[::BLOCK] // BLOCK
     starts_row = starts[None, :]
 
-    unit, qkv = project(x_all, w_qkv, cos, sin)
+    unit, qkv = project(places, x_all, w_qkv, cos, sin)
     attended = attend(lows, starts_row, qkv)
-    attended_all = (
-        jnp.swapaxes(gather_ctx(attended), 0, 1).reshape(group, features)
-    )
-    mixed = x_all.astype(F32) + dot(attended_all, out_all, 1, 1)
-    inverse_mlp = lax.rsqrt(jnp.mean(mixed * mixed, axis=-1, keepdims=True) + EPSILON)
-    unit_mlp = (mixed * inverse_mlp).astype(LOW)
-
-    gate = dot(unit_mlp, col_gate, 1, 0)
-    up = dot(unit_mlp, col_up, 1, 0)
-    sigmoid = jax.nn.sigmoid(gate)
-    silu = gate * sigmoid
-    hidden = (silu * up).astype(LOW)
-    d_hidden = dot(back_all, col_down, 1, 0)
-    d_gate = (d_hidden * up * sigmoid * (1.0 + gate * (1.0 - sigmoid))).astype(LOW)
-    d_up = (d_hidden * silu).astype(LOW)
-    branch = dot(hidden, col_down, 1, 1).astype(LOW)
-    d_unit_part = (dot(d_gate, col_gate, 1, 1) + dot(d_up, col_up, 1, 1)).astype(LOW)
-    d_unit = scatter_ctx(d_unit_part)
-    branch_own = lax.psum_scatter(branch, "ctx", scatter_dimension=0, tiled=True).astype(F32)
+    down_rows = to_columns(after(w_down, two_rows, attended))
+    two_near = pull_near(two_rows)
+    attended_mine = spread_cores(after(attended, down_rows))
+    two_far = pull_far(two_near)
+    down_near = pull_near(down_rows, *two_near)
+    attended_mine = after(attended_mine, *two_far)
+    back_all = lax.all_gather(after(cotangent, attended_mine), "ctx", axis=0, tiled=True)
+    attended_other = other_core(attended_mine)
+    unit_mlp, mixed = blend(core, x_all, attended_mine, attended_other, out_all)
+    col_two = pulled(two_rows, two_near, two_far)
+    down_near = tuple(after(piece, unit_mlp) for piece in down_near)
+    down_far = pull_far(down_near)
+    col_down = pulled(down_rows, down_near, down_far)
+
+    gate, up, hidden = open_units(places, unit_mlp, col_two)
+    d_both = close_units(places, back_all, gate, up, col_down)
+    d_unit_sums = pair_sums(times_rows(places, d_both, col_two))
+    d_unit_landed = swap_chips(d_unit_sums)
+    part_down = weight_grad(order, outs, (after(back_all, d_unit_sums), hidden[None]))
+    down_landed = push_near(part_down)
+    part_gate = weight_grad(order, outs, (after(unit_mlp, part_down[0]), d_both[:1]))
+    gate_landed = push_near(part_gate)
+    part_up = weight_grad(order, outs, (after(unit_mlp, part_gate[0]), d_both[1:]))
+    up_landed = push_near(part_up)
     mixed_own = lax.dynamic_slice_in_dim(mixed, here, rows, 0)
-    layer_out = (mixed_own + branch_own).astype(LOW)
-
-    inverse_own = lax.dynamic_slice_in_dim(inverse_mlp, here, rows, 0)
+    d_unit = total(after(d_unit_landed, *down_landed, *gate_landed, part_up[0]))
+
+    inverse_own = lax.rsqrt(jnp.mean(mixed_own * mixed_own, axis=-1, keepdims=True) + EPSILON)
     unit_own = mixed_own * inverse_own
     d_mixed = cotangent.astype(F32) + inverse_own * (
         d_unit - unit_own * jnp.mean(d_unit * unit_own, axis=-1, keepdims=True)
     )
     d_mixed_low = d_mixed.astype(LOW)
     d_att = dot(d_mixed_low, out_all, 1, 0).astype(LOW)
+    d_mixed_all = lax.all_gather(d_mixed_low, "ctx", axis=0, tiled=True)
     d_att_own = lax.all_to_all(d_att, "ctx", split_axis=1, concat_axis=0, tiled=True)
+    down_last = push_far(part_down, down_landed)
+    gate_last = push_far(part_gate, gate_landed)
+    d_att_own = after(d_att_own, *down_last, *gate_last)
+    branch = times_rows(places, after(hidden, d_att_own)[None], col_down)
+    branch_own = lax.psum_scatter(branch, "ctx", scatter_dimension=0, tiled=True).astype(F32)
+    up_last = push_far(part_up, up_landed)
+    rows_down = to_rows(after(pushed(part_down, down_landed, down_last), d_att_own))
+
     d_qkv = attend_back(lows, starts_row, qkv, d_att_own, cos, sin)
-
-    d_first = scatter_ctx(dot(d_qkv, w_qkv, 1, 1).astype(LOW))
+    first_part = after(times_rows(places, d_qkv[None], w_qkv), rows_down, *up_landed)
+    first_landed = swap_chips(pair_sums(first_part))
+    part_qkv = weight_grad(order, outs, (unit, d_qkv[None]), (d_mixed_all, attended[None]))
+    qkv_landed = push_near(part_qkv)
+    first_landed = after(first_landed, *qkv_landed, *up_last)
+    two_mine = jnp.concatenate(
+        [pushed(part_gate, gate_landed, gate_last), pushed(part_up, up_landed, up_last)], axis=1
+    )
+    rows_two = to_rows(after(two_mine, first_landed))
+    qkv_last = push_far(part_qkv, qkv_landed)
+    rows_qkv = to_rows(after(pushed(part_qkv, qkv_landed, qkv_last), rows_two))
+
+    layer_out = (mixed_own + after(branch_own, rows_two)).astype(LOW)
+    d_first = total(first_landed)
     x_own = tokens.astype(F32)
     inverse = lax.rsqrt(jnp.mean(x_own * x_own, axis=-1, keepdims=True) + EPSILON)
     first_own = x_own * inverse
@@ -458,45 +817,22 @@
         d_first - first_own * jnp.mean(d_first * first_own, axis=-1, keepdims=True)
     )
 
-    def weight_grad(left, right):
-        part = dot(left, right, 0, 0).astype(LOW)
-        mine = scatter_fsdp(part).astype(LOW)
-        return lax.all_to_all(mine, "ctx", split_axis=0, concat_axis=1, tiled=True).astype(F32)
-
-    raw_gate = weight_grad(unit_mlp, d_gate)
-    raw_up = weight_grad(unit_mlp, d_up)
-    grad_down = weight_grad(back_all, hidden)
-    attended_own = lax.dynamic_slice_in_dim(attended_all, here, rows, 0)
-    grad_out = lax.psum_scatter(
-        dot(d_mixed_low, attended_own, 0, 0).astype(LOW),
-        ("fsdp", "ctx"),
-        scatter_dimension=0,
-        tiled=True,
-    ).astype(F32)
-    raw_qkv = weight_grad(unit, d_qkv).reshape(share, n_c, 3, width)
-    raw_query, raw_key, raw_value = (
-        raw_qkv[:, :, part].reshape(share, features) for part in range(3)
-    )
-    grad_gain_attn = jnp.sum(
-        raw_query * w_query.astype(F32)
-        + raw_key * w_key.astype(F32)
-        + raw_value * w_value.astype(F32),
-        axis=1,
-    )
-    grad_gain_mlp = jnp.sum(
-        raw_gate * w_gate.astype(F32) + raw_up * w_up.astype(F32), axis=1
+    (grad_down,), unused = finish(rows_down, gain_m, (), 1)
+    (grad_gate, grad_up), grad_gain_mlp = finish(rows_two, gain_m, (w_gate, w_up), 2)
+    (grad_query, grad_key, grad_value, grad_out), grad_gain_attn = finish(
+        rows_qkv, gain_a, (w_query, w_key, w_value), 4
     )
     return (
         layer_out,
         grad_tokens,
         grad_gain_attn,
-        raw_query * gain_a,
-        raw_key * gain_a,
-        raw_value * gain_a,
+        grad_query,
+        grad_key,
+        grad_value,
         grad_out,
         grad_gain_mlp,
-        raw_gate * gain_m,
-        raw_up * gain_m,
+        grad_gate,
+        grad_up,
         grad_down,
     )
 

time: 861 us -> 700 us (0.81)
  Pallas kernels: 40 us -> 189 us
  waiting for transfers between devices: 438 us -> 315 us
  matrix products: 104 us -> 4.99 us
  local copies, waits for them, and re-layouts: 101 us -> 34.5 us
  other arithmetic: 67.4 us -> 54.8 us
  starting transfers between devices: 87.1 us -> 76.9 us
    pallas_call x1 -> x14, Pallas kernels: 9.46 us -> 158 us  [the longest x4 46.8 us: weight_grad(): pl.pallas_call(functools.partial(weight_grad_kernel, outs, len(pairs)), g...]
    dot_general x14 -> x1, matrix products: 104 us -> 4.99 us  [dot(): lax.dot_general(left, right, (((left_dim,), (right_dim,)), ((), ())), pre...]
    ppermute x35 -> x31, waiting for transfers between devices: 224 us -> 148 us  [the longest x4 34.8 us: reduce_far(): lax.ppermute(send_y, 'fsdp', flip('fsdp', 4, 2))]
    all_to_all x4 -> x3, waiting for transfers between devices: 121 us -> 79.5 us  [to_columns(): lax.all_to_all(rows_block, 'ctx', split_axis=1, concat_axis=0, tiled=True)]
    dynamic_update_slice x20 -> x0, local copies, waits for them, and re-layouts: 29.8 us -> none  [gather_fsdp(): out = lax.dynamic_update_slice_in_dim(out, piece, place, 0)]
    all_to_all x7 -> x6, waiting for transfers between devices: 90.9 us -> 71.9 us  [the longest x2 39.5 us: swap_chips(): lax.all_to_all(sums, 'ctx', 0, 0, axis_index_groups=same_core_groups(lax....]
    all_to_all x1, waiting for transfers between devices: 0.01 us -> 12.9 us  [local(): lax.all_to_all(d_att, 'ctx', split_axis=1, concat_axis=0, tiled=True)]
    slice x9 -> x7, local copies, waits for them, and re-layouts: 18.3 us -> 9.35 us  [the longest x1 4.65 us: local(): d_both[1:]]
  transfers between devices with their start and end apart: 52 -> 46, of which waited for: 25 -> 27; matrix products, arithmetic and copies ran while one was open for 24% -> 11% of each run, Pallas kernels for 5% -> 22%
where the time goes in v2:
time: 700 us; the launch traced here: 690 us
  waiting for transfers between devices  315 us (45%)
  Pallas kernels  189 us (27%)
  starting transfers between devices  76.9 us (11%)
  other arithmetic  54.8 us (8%)
  local copies, waits for them, and re-layouts  34.5 us (5%)
  between operations  14.8 us (2%)
    all_to_all x3, waiting for transfers between devices, to_columns(): lax.all_to_all(rows_block, 'ctx', split_axis=1, concat_axis=0, tiled=True)  79.5 us
    pallas_call x4, Pallas kernels, weight_grad(): pl.pallas_call(functools.partial(weight_grad_kernel, outs, len(pairs)), g...  46.8 us
    all_to_all x2, waiting for transfers between devices, swap_chips(): lax.all_to_all(sums, 'ctx', 0, 0, axis_index_groups=same_core_groups(lax....  39.5 us
    pallas_call x3, Pallas kernels, times_rows(): pl.pallas_call(functools.partial(times_rows_kernel, units), grid_spec=plt...  38.2 us
    ppermute x4, waiting for transfers between devices, reduce_far(): lax.ppermute(send_y, 'fsdp', flip('fsdp', 4, 2))  34.8 us
    ppermute x3, waiting for transfers between devices, near(): lax.ppermute(block, 'fsdp', flip('fsdp', 4, 1))  31.5 us
    ppermute x3, waiting for transfers between devices, far(): lax.ppermute(from_x[:half], 'fsdp', flip('fsdp', 4, 2))  20.9 us
    ppermute x4, waiting for transfers between devices, reduce_near(): lax.ppermute(part[0], 'fsdp', flip('fsdp', 4, 1))  19.7 us
  transfers between devices with their start and end apart: 46, of which 27 were waited for; matrix products, arithmetic and copies ran while one was open for 11% of the time, Pallas kernels for 22%

profile of v2, /device:TPU:0, one launch (start us, length us, event | category | flops | bytes accessed | tf_op | source)
XLA Modules:
  0.0 689.8 jit_solution(16420545395092197170)
XLA Ops:
  22.2 36.7 %all-to-all-done = bf16[64,8,768]{2,0,1:T(8,128)(2,1)S(1)} async-done(((bf16[64,8,768]{2,0,1:T(8,128)(2,1)}), bf16[64,8,768]{2,0,1:T(8,128)(2,1)S(1)}, u32[]{:S(2)}, u32[]{:S(2)}) %all-to-all-start) | async-done | bytes 786464 | tf_op jit(solution)/shard_map/all_to_all | solution.py:125
  68.4 16.6 %collective-permute-done.refs_1_ = bf16[512,768]{1,0:T(8,128)(2,1)} collective-permute-done((bf16[512,768]{1,0:T(8,128)(2,1)S(1)}, bf16[512,768]{1,0:T(8,128)(2,1)}, u32[]{:S(2)}, u32[]{:S(2)}) %collective-permute-start) | collective-permute-done | bytes 786464 | tf_op jit(solution)/shard_map/ppermute | solution.py:42
  133.1 38.4 %all-to-all-done.2 = bf16[64,8,1024]{2,0,1:T(8,128)(2,1)S(1)} async-done(((bf16[64,8,1024]{2,0,1:T(8,128)(2,1)}), bf16[64,8,1024]{2,0,1:T(8,128)(2,1)S(1)}, u32[]{:S(2)}, u32[]{:S(2)}) %all-to-all-start.2) | async-done | bytes 1048608 | tf_op jit(solution)/shard_map/all_to_all | solution.py:125
  179.1 13.8 %collective-permute-done.4.refs_1_.refs_6_ = bf16[512,2048]{1,0:T(8,128)(2,1)} collective-permute-done((bf16[512,2048]{1,0:T(8,128)(2,1)S(1)}, bf16[512,2048]{1,0:T(8,128)(2,1)}, u32[]{:S(2)}, u32[]{:S(2)}) %collective-permute-start.4) | collective-permute-done | bytes 2097184 | tf_op jit(solution)/shard_map/ppermute | solution.py:42
  198.8 20.0 %collective-permute-done.5.refs_3_.refs_8_ = bf16[256,2048]{1,0:T(8,128)(2,1)S(1)} collective-permute-done((bf16[256,2048]{1,0:T(8,128)(2,1)S(1)}, bf16[256,2048]{1,0:T(8,128)(2,1)S(1)}, u32[]{:S(2)}, u32[]{:S(2)}) %collective-permute-start.5) | collective-permute-done | bytes 1048608 | tf_op jit(solution)/shard_map/ppermute | solution.py:51
  221.6 13.3 %all-to-all-done.3.own_ref = bf16[4,1024,256]{2,1,0:T(8,128)(2,1)} async-done(((bf16[4,1024,256]{2,1,0:T(8,128)(2,1)}), bf16[4,1024,256]{2,1,0:T(8,128)(2,1)}, u32[]{:S(2)}, u32[]{:S(2)}) %all-to-all-start.3) | async-done | bytes 2097184 | tf_op jit(solution)/shard_map/all_to_all | solution.py:85
  239.5 16.6 %blend.1 = (bf16[1024,2048]{1,0:T(8,128)(2,1)}, f32[1024,2048]{1,0:T(8,128)}) custom-call(s32[1]{0:T(128)} %bitcast.core_ref, bf16[1024,2048]{1,0:T(8,128)(2,1)} %all-gather.5.cloned.1.call-done.x_ref, bf16[4,1024,256]{2,1,0:T(8,128)(2,1)} %all-to-all-done.3.own_ref, bf16[4,1024,256]{2,1,0:T(8,128)(2,1)} %collective-permute-done.8.other_ref, ...), custom_call_target="tpu_custom_call" | custom-call | flops 15000000512 | tf_op jit(solution)/shard_map/blend/pallas_call | solution.py:580
  262.8 15.6 %open_units.1 = (f32[1024,1024]{1,0:T(8,128)}, f32[1024,1024]{1,0:T(8,128)}, bf16[1024,1024]{1,0:T(8,128)(2,1)}) custom-call(s32[8]{0:T(128)} %stack.46.places_ref, bf16[1024,2048]{1,0:T(8,128)(2,1)} %get-tuple-element.79.left_ref.refs_0_, bf16[512,2048]{1,0:T(8,128)(2,1)} %bitcast.101, bf16[512,2048]{1,0:T(8,128)(2,1)} %collective-permute-done.4.refs_1_.refs_6_, ...), custom_call_target="tpu_custom_call" | custom-call | flops 12000000000 | tf_op jit(solution)/shard_map/open_units/pallas_call | solution.py:221
  280.6 12.5 %close_units.1.left_ref = bf16[2,1024,1024]{2,1,0:T(8,128)(2,1)} custom-call(s32[8]{0:T(128)} %stack.46.places_ref, bf16[1024,2048]{1,0:T(8,128)(2,1)} %all-gather.9.cloned.1.call-done.back_ref.refs_0_, f32[1024,1024]{1,0:T(8,128)} %get-tuple-element.68.gate_ref, f32[1024,1024]{1,0:T(8,128)} %get-tuple-element.69.up_ref, bf16[512,1024]{1,0:T(8,128)(2,1)} %bitcast.108, ...), custom_call_target="tpu_custom_call" | custom-call | flops 7000000000 | tf_op jit(solution)/shard_map/close_units/pallas_call | solution.py:259
  293.1 16.8 %times_rows.3 = bf16[1024,2048]{1,0:T(8,128)(2,1)} custom-call(s32[8]{0:T(128)} %stack.46.places_ref, bf16[2,1024,1024]{2,1,0:T(8,128)(2,1)} %close_units.1.left_ref, bf16[512,2048]{1,0:T(8,128)(2,1)} %bitcast.103, bf16[512,2048]{1,0:T(8,128)(2,1)} %collective-permute-done.4.refs_1_.refs_6_, bf16[512,2048]{1,0:T(8,128)(2,1)} %collective-permute-done.6.refs_2_.refs_7_, ...), custom_call_target="tpu_custom_call" | custom-call | flops 8589934592 | tf_op jit(solution)/shard_map/times_rows/pallas_call | solution.py:304
  330.3 11.5 %weight_grad.4 = (bf16[512,1024]{1,0:T(8,128)(2,1)}, bf16[512,1024]{1,0:T(8,128)(2,1)}, bf16[1024,1024]{1,0:T(8,128)(2,1)}) custom-call(s32[8]{0:T(128)} %stack.47.order_ref, bf16[1024,2048]{1,0:T(8,128)(2,1)} %all-gather.9.cloned.1.call-done.back_ref.refs_0_, bf16[1,1024,1024]{2,1,0:T(8,128)(2,1)} %bitcast.125), custom_call_target="tpu_custom_call" | custom-call | flops 4294967296 | tf_op jit(solution)/shard_map/weight_grad/pallas_call | solution.py:351
  343.3 11.4 %weight_grad.5 = (bf16[512,1024]{1,0:T(8,128)(2,1)}, bf16[512,1024]{1,0:T(8,128)(2,1)}, bf16[1024,1024]{1,0:T(8,128)(2,1)}) custom-call(s32[8]{0:T(128)} %stack.47.order_ref, bf16[1024,2048]{1,0:T(8,128)(2,1)} %get-tuple-element.79.left_ref.refs_0_, bf16[1,1024,1024]{2,1,0:T(8,128)(2,1)} %get-tuple-element.110.refs_1_), custom_call_target="tpu_custom_call" | custom-call | flops 4294967296 | tf_op jit(solution)/shard_map/weight_grad/pallas_call | solution.py:351
  358.7 11.4 %weight_grad.6 = (bf16[512,1024]{1,0:T(8,128)(2,1)}, bf16[512,1024]{1,0:T(8,128)(2,1)}, bf16[1024,1024]{1,0:T(8,128)(2,1)}) custom-call(s32[8]{0:T(128)} %stack.47.order_ref, bf16[1024,2048]{1,0:T(8,128)(2,1)} %get-tuple-element.79.left_ref.refs_0_, bf16[1,1024,1024]{2,1,0:T(8,128)(2,1)} %get-tuple-element.109.refs_1_), custom_call_target="tpu_custom_call" | custom-call | flops 4294967296 | tf_op jit(solution)/shard_map/weight_grad/pallas_call | solution.py:351
  370.1 19.7 %collective-permute-done.16 = bf16[512,1024]{1,0:T(8,128)(2,1)S(1)} collective-permute-done((bf16[512,1024]{1,0:T(8,128)(2,1)}, bf16[512,1024]{1,0:T(8,128)(2,1)S(1)}, u32[]{:S(2)}, u32[]{:S(2)}) %collective-permute-start.16) | collective-permute-done | bytes 1048608 | tf_op jit(solution)/shard_map/ppermute | solution.py:58
  389.8 13.0 %collective-permute-done.15 = bf16[512,1024]{1,0:T(8,128)(2,1)} collective-permute-done((bf16[512,1024]{1,0:T(8,128)(2,1)}, bf16[512,1024]{1,0:T(8,128)(2,1)}, u32[]{:S(2)}, u32[]{:S(2)}) %collective-permute-start.15) | collective-permute-done | bytes 1048608 | tf_op jit(solution)/shard_map/ppermute | solution.py:59
  440.5 12.9 %all-to-all-done.5 = bf16[128,8,256]{2,0,1:T(8,128)(2,1)} async-done(((bf16[128,8,256]{2,0,1:T(8,128)(2,1)}), bf16[128,8,256]{2,0,1:T(8,128)(2,1)}, u32[]{:S(2)}, u32[]{:S(2)}) %all-to-all-start.5) | async-done | bytes 524320 | tf_op jit(solution)/shard_map/all_to_all | solution.py:789
  457.4 19.6 %attend_back.1 = bf16[1024,768]{1,0:T(8,128)(2,1)} custom-call(s32[4]{0:T(128)} %and_select_fusion.2.lo_ref, s32[1,1024]{1,0:T(1,128)} %bitcast.124, bf16[1024,768]{1,0:T(8,128)(2,1)} %get-tuple-element.59.q_ref.k_ref.v_ref, bf16[1024,768]{1,0:T(8,128)(2,1)} %get-tuple-element.59.q_ref.k_ref.v_ref, bf16[1024,768]{1,0:T(8,128)(2,1)} %get-tuple-element.59.q_ref.k_ref.v_ref, ...), custom_call_target="tpu_custom_call" | custom-call | flops 20000000000 | tf_op jit(solution)/shard_map/attend_back/pallas_call | solution.py:534
  491.4 11.4 %times_rows.4 = bf16[1024,2048]{1,0:T(8,128)(2,1)} custom-call(s32[8]{0:T(128)} %stack.46.places_ref, bf16[1,1024,1024]{2,1,0:T(8,128)(2,1)} %bitcast.126, bf16[512,1024]{1,0:T(8,128)(2,1)} %bitcast.109, bf16[512,1024]{1,0:T(8,128)(2,1)} %copy-done.23, bf16[512,1024]{1,0:T(8,128)(2,1)} %copy-done.22, bf16[256,1024]{1,0:T(8,128)(2,1)} %copy-done.29, ...), custom_call_target="tpu_custom_call" | custom-call | flops 4294967296 | tf_op jit(solution)/shard_map/times_rows/pallas_call | solution.py:304
  513.5 13.9 %collective-permute-done.23 = bf16[256,1024]{1,0:T(8,128)(2,1)S(1)} collective-permute-done((bf16[256,1024]{1,0:T(8,128)(2,1)S(1)}, bf16[256,1024]{1,0:T(8,128)(2,1)S(1)}, u32[]{:S(2)}, u32[]{:S(2)}) %collective-permute-start.23) | collective-permute-done | bytes 524320 | tf_op jit(solution)/shard_map/ppermute | solution.py:69
  530.8 12.5 %weight_grad.7 = (bf16[512,1024]{1,0:T(8,128)(2,1)}, bf16[512,1024]{1,0:T(8,128)(2,1)}, bf16[1024,1024]{1,0:T(8,128)(2,1)}) custom-call(s32[8]{0:T(128)} %stack.47.order_ref, bf16[1024,2048]{1,0:T(8,128)(2,1)} %get-tuple-element.90.refs_0_, bf16[1024,2048]{1,0:T(8,128)(2,1)} %all-gather.11.cloned.1.call-done.refs_1_, bf16[1,1024,768]{2,1,0:T(8,128)(2,1)} %bitcast.128, ...), custom_call_target="tpu_custom_call" | custom-call | flops 4294967296 | tf_op jit(solution)/shard_map/weight_grad/pallas_call | solution.py:351
  550.4 39.5 %all-to-all-done.7 = bf16[4,128,2048]{2,1,0:T(8,128)(2,1)S(1)} async-done(((bf16[4,128,2048]{2,1,0:T(8,128)(2,1)}), bf16[4,128,2048]{2,1,0:T(8,128)(2,1)S(1)}, u32[]{:S(2)}, u32[]{:S(2)}) %all-to-all-start.7) | async-done | bytes 2097184 | tf_op jit(solution)/shard_map/all_to_all | solution.py:110
  597.8 13.4 %collective-permute-done.29 = bf16[256,1024]{1,0:T(8,128)(2,1)S(1)} collective-permute-done((bf16[256,1024]{1,0:T(8,128)(2,1)S(1)}, bf16[256,1024]{1,0:T(8,128)(2,1)S(1)}, u32[]{:S(2)}, u32[]{:S(2)}) %collective-permute-start.29) | collective-permute-done | bytes 524320 | tf_op jit(solution)/shard_map/ppermute | solution.py:69
  614.1 12.7 %collective-permute-done.30 = bf16[256,1024]{1,0:T(8,128)(2,1)S(1)} collective-permute-done((bf16[256,1024]{1,0:T(8,128)(2,1)S(1)}, bf16[256,1024]{1,0:T(8,128)(2,1)S(1)}, u32[]{:S(2)}, u32[]{:S(2)}) %collective-permute-start.30) | collective-permute-done | bytes 524320 | tf_op jit(solution)/shard_map/ppermute | solution.py:70
  629.3 15.3 %all-to-all-done.8.rows_ref = bf16[8,64,2048]{2,1,0:T(8,128)(2,1)} async-done(((bf16[8,64,2048]{2,1,0:T(8,128)(2,1)}), bf16[8,64,2048]{2,1,0:T(8,128)(2,1)}, u32[]{:S(2)}, u32[]{:S(2)}) %all-to-all-start.8) | async-done | bytes 2097184 | tf_op jit(solution)/shard_map/all_to_all | solution.py:693
  (226 shorter events, 256.6 us)
Async XLA Ops:
  7.2 92.0 %all-gather.5.cloned.1.call-start = ((), (), s32[]{:S(2)}) async-start(), calls=%async_computation.11 | async-start | bytes 4718592 | tf_op jit(solution)/shard_map/all_gather | solution.py:720
  7.9 231.6 %all-gather.7.cloned.1.call-start = ((), (), s32[]{:S(2)}) async-start(), calls=%async_computation.12 | async-start | bytes 8650752 | tf_op jit(solution)/shard_map/all_gather | solution.py:728
  12.2 46.6 %all-to-all-start = ((bf16[64,8,768]{2,0,1:T(8,128)(2,1)}), bf16[64,8,768]{2,0,1:T(8,128)(2,1)S(1)}, u32[]{:S(2)}, u32[]{:S(2)}) async-start(bf16[64,8,768]{2,0,1:T(8,128)(2,1)} %pad_maximum_fusion.3), calls=%async_computation | async-start | bytes 1572864 | tf_op jit(solution)/shard_map/all_to_all | solution.py:125
  60.4 64.7 %all-to-all-start.1 = ((bf16[64,8,2048]{2,0,1:T(8,128)(2,1)}), bf16[64,8,2048]{2,0,1:T(8,128)(2,1)S(1)}, u32[]{:S(2)}, u32[]{:S(2)}) async-start(bf16[64,8,2048]{2,0,1:T(8,128)(2,1)} %bitcast.79), calls=%async_computation.1 | async-start | bytes 4194304 | tf_op jit(solution)/shard_map/all_to_all | solution.py:125
  126.3 45.2 %all-to-all-start.2 = ((bf16[64,8,1024]{2,0,1:T(8,128)(2,1)}), bf16[64,8,1024]{2,0,1:T(8,128)(2,1)S(1)}, u32[]{:S(2)}, u32[]{:S(2)}) async-start(bf16[64,8,1024]{2,0,1:T(8,128)(2,1)} %bitcast.82), calls=%async_computation.2 | async-start | bytes 2097152 | tf_op jit(solution)/shard_map/all_to_all | solution.py:125
  129.9 63.0 %collective-permute-start.4 = (bf16[512,2048]{1,0:T(8,128)(2,1)S(1)}, bf16[512,2048]{1,0:T(8,128)(2,1)}, u32[]{:S(2)}, u32[]{:S(2)}) collective-permute-start(bf16[512,2048]{1,0:T(8,128)(2,1)S(1)} %bitcast.99), channel_id=1, source_target_pairs={{0,8},{8,0},{16,24},{24,16},{1,9},{9,1},{17,25},{25,17},{2,10},{10... | collective-permute-start | bytes 6291464 | tf_op jit(solution)/shard_map/ppermute | solution.py:42
  131.5 64.4 %collective-permute-start.6 = (bf16[512,2048]{1,0:T(8,128)(2,1)S(1)}, bf16[512,2048]{1,0:T(8,128)(2,1)}, u32[]{:S(2)}, u32[]{:S(2)}) collective-permute-start(bf16[512,2048]{1,0:T(8,128)(2,1)S(1)} %bitcast.100), channel_id=1, source_target_pairs={{0,16},{8,24},{16,0},{24,8},{1,17},{9,25},{17,1},{25,9},{2,18},{10... | collective-permute-start | bytes 6291464 | tf_op jit(solution)/shard_map/ppermute | solution.py:43
  174.3 60.6 %all-to-all-start.3 = ((bf16[4,1024,256]{2,1,0:T(8,128)(2,1)}), bf16[4,1024,256]{2,1,0:T(8,128)(2,1)}, u32[]{:S(2)}, u32[]{:S(2)}) async-start(bf16[4,1024,256]{2,1,0:T(8,128)(2,1)} %broadcast_in_dim.60), calls=%async_computation.3 | async-start | bytes 4194304 | tf_op jit(solution)/shard_map/all_to_all | solution.py:85
  178.8 101.8 %all-gather.9.cloned.1.call-start = ((), (), s32[]{:S(2)}) async-start(), calls=%async_computation.13 | async-start | bytes 4718592 | tf_op jit(solution)/shard_map/all_gather | solution.py:760
  321.1 81.7 %all-to-all-start.4 = ((bf16[4,128,2048]{2,1,0:T(8,128)(2,1)}), bf16[4,128,2048]{2,1,0:T(8,128)(2,1)S(1)}, u32[]{:S(2)}, u32[]{:S(2)}) async-start(bf16[4,128,2048]{2,1,0:T(8,128)(2,1)} %fusion.1), calls=%async_computation.4 | async-start | bytes 4194304 | tf_op jit(solution)/shard_map/all_to_all | solution.py:110
  324.7 206.1 %all-gather.11.cloned.1.call-start = ((), (), s32[]{:S(2)}) async-start(), calls=%async_computation.15 | async-start | bytes 4718592 | tf_op jit(solution)/shard_map/all_gather | solution.py:788
  341.8 48.0 %collective-permute-start.14 = (bf16[512,1024]{1,0:T(8,128)(2,1)}, bf16[512,1024]{1,0:T(8,128)(2,1)}, u32[]{:S(2)}, u32[]{:S(2)}) collective-permute-start(bf16[512,1024]{1,0:T(8,128)(2,1)} %get-tuple-element.74), channel_id=1, source_target_pairs={{0,8},{8,0},{16,24},{24,16},{1,9},{9,1},{17,25},{25,17},{2,10},{10... | collective-permute-start | bytes 3145736 | tf_op jit(solution)/shard_map/ppermute | solution.py:58
  354.7 35.1 %collective-permute-start.16 = (bf16[512,1024]{1,0:T(8,128)(2,1)}, bf16[512,1024]{1,0:T(8,128)(2,1)S(1)}, u32[]{:S(2)}, u32[]{:S(2)}) collective-permute-start(bf16[512,1024]{1,0:T(8,128)(2,1)} %get-tuple-element.77), channel_id=1, source_target_pairs={{0,8},{8,0},{16,24},{24,16},{1,9},{9,1},{17,25},{25,17},{2,10},{10... | collective-permute-start | bytes 3145736 | tf_op jit(solution)/shard_map/ppermute | solution.py:58
  355.2 34.5 %collective-permute-start.17 = (bf16[512,1024]{1,0:T(8,128)(2,1)}, bf16[512,1024]{1,0:T(8,128)(2,1)}, u32[]{:S(2)}, u32[]{:S(2)}) collective-permute-start(bf16[512,1024]{1,0:T(8,128)(2,1)} %get-tuple-element.78), channel_id=1, source_target_pairs={{0,16},{8,24},{16,0},{24,8},{1,17},{9,25},{17,1},{25,9},{2,18},{10... | collective-permute-start | bytes 3145736 | tf_op jit(solution)/shard_map/ppermute | solution.py:59
  356.7 46.1 %collective-permute-start.15 = (bf16[512,1024]{1,0:T(8,128)(2,1)}, bf16[512,1024]{1,0:T(8,128)(2,1)}, u32[]{:S(2)}, u32[]{:S(2)}) collective-permute-start(bf16[512,1024]{1,0:T(8,128)(2,1)} %get-tuple-element.75), channel_id=1, source_target_pairs={{0,16},{8,24},{16,0},{24,8},{1,17},{9,25},{17,1},{25,9},{2,18},{10... | collective-permute-start | bytes 3145736 | tf_op jit(solution)/shard_map/ppermute | solution.py:59
  418.8 34.7 %all-to-all-start.5 = ((bf16[128,8,256]{2,0,1:T(8,128)(2,1)}), bf16[128,8,256]{2,0,1:T(8,128)(2,1)}, u32[]{:S(2)}, u32[]{:S(2)}) async-start(bf16[128,8,256]{2,0,1:T(8,128)(2,1)} %bitcast.104), calls=%async_computation.5 | async-start | bytes 1048576 | tf_op jit(solution)/shard_map/all_to_all | solution.py:789
  426.2 60.8 %collective-permute-start.22 = (bf16[512,1024]{1,0:T(8,128)(2,1)}, bf16[512,1024]{1,0:T(8,128)(2,1)S(1)}, u32[]{:S(2)}, u32[]{:S(2)}) collective-permute-start(bf16[512,1024]{1,0:T(8,128)(2,1)} %get-tuple-element.80), channel_id=1, source_target_pairs={{0,8},{8,0},{16,24},{24,16},{1,9},{9,1},{17,25},{25,17},{2,10},{10... | collective-permute-start | bytes 3145736 | tf_op jit(solution)/shard_map/ppermute | solution.py:58
  427.8 59.2 %collective-permute-start.24 = (bf16[512,1024]{1,0:T(8,128)(2,1)}, bf16[512,1024]{1,0:T(8,128)(2,1)}, u32[]{:S(2)}, u32[]{:S(2)}) collective-permute-start(bf16[512,1024]{1,0:T(8,128)(2,1)} %get-tuple-element.87), channel_id=1, source_target_pairs={{0,16},{8,24},{16,0},{24,8},{1,17},{9,25},{17,1},{25,9},{2,18},{10... | collective-permute-start | bytes 3145736 | tf_op jit(solution)/shard_map/ppermute | solution.py:59
  453.5 33.9 %all-to-all-start.6 = ((bf16[8,64,1024]{2,1,0:T(8,128)(2,1)}), bf16[8,64,1024]{2,1,0:T(8,128)(2,1)S(1)}, u32[]{:S(2)}, u32[]{:S(2)}) async-start(bf16[8,64,1024]{2,1,0:T(8,128)(2,1)} %bitcast.28), calls=%async_computation.7 | async-start | bytes 2097152 | tf_op jit(solution)/shard_map/all_to_all | solution.py:693
  457.1 201.2 %reduce-scatter.2.cloned.1.call-start = ((), (), s32[]{:S(2)}) async-start(), calls=%async_computation.14 | async-start | bytes 4718592 | tf_op jit(solution)/shard_map/reduce_scatter | solution.py:794
  507.3 82.6 %all-to-all-start.7 = ((bf16[4,128,2048]{2,1,0:T(8,128)(2,1)}), bf16[4,128,2048]{2,1,0:T(8,128)(2,1)S(1)}, u32[]{:S(2)}, u32[]{:S(2)}) async-start(bf16[4,128,2048]{2,1,0:T(8,128)(2,1)} %fusion), calls=%async_computation.8 | async-start | bytes 4194304 | tf_op jit(solution)/shard_map/all_to_all | solution.py:110
  543.2 46.6 %collective-permute-start.27 = (bf16[512,1024]{1,0:T(8,128)(2,1)}, bf16[512,1024]{1,0:T(8,128)(2,1)}, u32[]{:S(2)}, u32[]{:S(2)}) collective-permute-start(bf16[512,1024]{1,0:T(8,128)(2,1)} %get-tuple-element.91), channel_id=1, source_target_pairs={{0,8},{8,0},{16,24},{24,16},{1,9},{9,1},{17,25},{25,17},{2,10},{10... | collective-permute-start | bytes 3145736 | tf_op jit(solution)/shard_map/ppermute | solution.py:58
  544.9 45.0 %collective-permute-start.28 = (bf16[512,1024]{1,0:T(8,128)(2,1)}, bf16[512,1024]{1,0:T(8,128)(2,1)}, u32[]{:S(2)}, u32[]{:S(2)}) collective-permute-start(bf16[512,1024]{1,0:T(8,128)(2,1)} %get-tuple-element.92), channel_id=1, source_target_pairs={{0,16},{8,24},{16,0},{24,8},{1,17},{9,25},{17,1},{25,9},{2,18},{10... | collective-permute-start | bytes 3145736 | tf_op jit(solution)/shard_map/ppermute | solution.py:59
  591.2 53.4 %all-to-all-start.8 = ((bf16[8,64,2048]{2,1,0:T(8,128)(2,1)}), bf16[8,64,2048]{2,1,0:T(8,128)(2,1)}, u32[]{:S(2)}, u32[]{:S(2)}) async-start(bf16[8,64,2048]{2,1,0:T(8,128)(2,1)} %bitcast.85), calls=%async_computation.9 | async-start | bytes 4194304 | tf_op jit(solution)/shard_map/all_to_all | solution.py:693
  (55 other events, 745.7 us)
Sparse Core Ops, SparseCore 0:
  9.6 76.8 all-gather.4
  89.5 118.4 all-gather.6
  235.1 45.4 all-gather.8
  407.2 74.2 all-gather.10
  502.9 88.6 reduce-scatter.1

commit v3 on v2

--- a/solution.py
+++ b/solution.py
@@ -772,11 +772,9 @@
     part_down = weight_grad(order, outs, (after(back_all, d_unit_sums), hidden[None]))
     down_landed = push_near(part_down)
     part_gate = weight_grad(order, outs, (after(unit_mlp, part_down[0]), d_both[:1]))
-    gate_landed = push_near(part_gate)
     part_up = weight_grad(order, outs, (after(unit_mlp, part_gate[0]), d_both[1:]))
-    up_landed = push_near(part_up)
     mixed_own = lax.dynamic_slice_in_dim(mixed, here, rows, 0)
-    d_unit = total(after(d_unit_landed, *down_landed, *gate_landed, part_up[0]))
+    d_unit = total(after(d_unit_landed, *down_landed, part_up[0]))
 
     inverse_own = lax.rsqrt(jnp.mean(mixed_own * mixed_own, axis=-1, keepdims=True) + EPSILON)
     unit_own = mixed_own * inverse_own
@@ -785,31 +783,40 @@
     )
     d_mixed_low = d_mixed.astype(LOW)
     d_att = dot(d_mixed_low, out_all, 1, 0).astype(LOW)
-    d_mixed_all = lax.all_gather(d_mixed_low, "ctx", axis=0, tiled=True)
+    gate_landed = push_near(part_gate)
+    branch = times_rows(places, after(hidden, d_att)[None], col_down)
+    down_landed = tuple(after(piece, d_att) for piece in down_landed)
     d_att_own = lax.all_to_all(d_att, "ctx", split_axis=1, concat_axis=0, tiled=True)
     down_last = push_far(part_down, down_landed)
     gate_last = push_far(part_gate, gate_landed)
-    d_att_own = after(d_att_own, *down_last, *gate_last)
-    branch = times_rows(places, after(hidden, d_att_own)[None], col_down)
-    branch_own = lax.psum_scatter(branch, "ctx", scatter_dimension=0, tiled=True).astype(F32)
+    d_att_own = after(d_att_own, branch, *down_last, *gate_landed)
+    d_mixed_all = lax.all_gather(after(d_mixed_low, d_att_own), "ctx", axis=0, tiled=True)
+    part_up = [after(part_up[0], d_att_own)] + list(part_up[1:])
+    if square:
+        part_up[1] = after(part_up[1], d_att_own)
+    up_landed = push_near(part_up)
     up_last = push_far(part_up, up_landed)
     rows_down = to_rows(after(pushed(part_down, down_landed, down_last), d_att_own))
 
     d_qkv = attend_back(lows, starts_row, qkv, d_att_own, cos, sin)
-    first_part = after(times_rows(places, d_qkv[None], w_qkv), rows_down, *up_landed)
-    first_landed = swap_chips(pair_sums(first_part))
-    part_qkv = weight_grad(order, outs, (unit, d_qkv[None]), (d_mixed_all, attended[None]))
+    first_part = times_rows(places, d_qkv[None], w_qkv)
+    d_first = lax.psum_scatter(first_part, "ctx", scatter_dimension=0, tiled=True).astype(F32)
+    part_qkv = weight_grad(
+        order, outs, (unit, after(d_qkv, first_part, *up_landed, *gate_last)[None]), (d_mixed_all, attended[None])
+    )
+    part_qkv = [after(part, rows_down, *up_last) for part in part_qkv]
     qkv_landed = push_near(part_qkv)
-    first_landed = after(first_landed, *qkv_landed, *up_last)
     two_mine = jnp.concatenate(
         [pushed(part_gate, gate_landed, gate_last), pushed(part_up, up_landed, up_last)], axis=1
     )
-    rows_two = to_rows(after(two_mine, first_landed))
+    rows_two = after(to_rows(after(two_mine, rows_down)), *qkv_landed)
+    branch_own = lax.psum_scatter(
+        after(branch, part_qkv[0]), "ctx", scatter_dimension=0, tiled=True
+    ).astype(F32)
     qkv_last = push_far(part_qkv, qkv_landed)
     rows_qkv = to_rows(after(pushed(part_qkv, qkv_landed, qkv_last), rows_two))
 
     layer_out = (mixed_own + after(branch_own, rows_two)).astype(LOW)
-    d_first = total(first_landed)
     x_own = tokens.astype(F32)
     inverse = lax.rsqrt(jnp.mean(x_own * x_own, axis=-1, keepdims=True) + EPSILON)
     first_own = x_own * inverse

time: 700 us -> 642 us (0.917)
  waiting for transfers between devices: 315 us -> 265 us
    all_to_all x2 -> x1, waiting for transfers between devices: 39.5 us -> 4.38 us  [swap_chips(): lax.all_to_all(sums, 'ctx', 0, 0, axis_index_groups=same_core_groups(lax....]
    all_to_all x3, waiting for transfers between devices: 19.1 us -> 41.1 us  [to_rows(): return lax.all_to_all(value, 'ctx', split_axis=0, concat_axis=0, tiled=True)]
    ppermute x4, waiting for transfers between devices: 34.8 us -> 17.4 us  [reduce_far(): lax.ppermute(send_y, 'fsdp', flip('fsdp', 4, 2))]
    all_to_all x1, waiting for transfers between devices: 12.9 us -> 0.01 us  [local(): lax.all_to_all(d_att, 'ctx', split_axis=1, concat_axis=0, tiled=True)]
    ppermute x4, waiting for transfers between devices: 13.2 us -> 1.21 us  [reduce_far(): lax.ppermute(send_x, 'fsdp', flip('fsdp', 4, 1))]
  transfers between devices with their start and end apart: 46 -> 45, of which waited for: 27 -> 25; matrix products, arithmetic and copies ran while one was open for 11% -> 11% of each run, Pallas kernels for 22% -> 25%
where the time goes in v3:
time: 642 us; the launch traced here: 630 us
  waiting for transfers between devices  265 us (41%)
  Pallas kernels  189 us (29%)
  starting transfers between devices  77.7 us (12%)
  other arithmetic  48.1 us (7%)
  local copies, waits for them, and re-layouts  31.2 us (5%)
  between operations  15.1 us (2%)
    all_to_all x3, waiting for transfers between devices, to_columns(): lax.all_to_all(rows_block, 'ctx', split_axis=1, concat_axis=0, tiled=True)  79.6 us
    pallas_call x4, Pallas kernels, weight_grad(): pl.pallas_call(functools.partial(weight_grad_kernel, outs, len(pairs)), g...  47 us
    all_to_all x3, waiting for transfers between devices, to_rows(): return lax.all_to_all(value, 'ctx', split_axis=0, concat_axis=0, tiled=True)  41.1 us
    pallas_call x3, Pallas kernels, times_rows(): pl.pallas_call(functools.partial(times_rows_kernel, units), grid_spec=plt...  38.2 us
    ppermute x3, waiting for transfers between devices, near(): lax.ppermute(block, 'fsdp', flip('fsdp', 4, 1))  31.3 us
    ppermute x4, waiting for transfers between devices, reduce_near(): lax.ppermute(part[0], 'fsdp', flip('fsdp', 4, 1))  23.6 us
    ppermute x3, waiting for transfers between devices, far(): lax.ppermute(from_x[:half], 'fsdp', flip('fsdp', 4, 2))  20.9 us
    pallas_call x1, Pallas kernels, attend_back(): pl.pallas_call(functools.partial(attend_back_kernel, heads), grid_spec=pl...  19.6 us
  transfers between devices with their start and end apart: 45, of which 25 were waited for; matrix products, arithmetic and copies ran while one was open for 11% of the time, Pallas kernels for 25%

profile of v3, /device:TPU:0, one launch (start us, length us, event | category | flops | bytes accessed | tf_op | source)
XLA Modules:
  0.0 630.3 jit_solution(13099170434467674493)
XLA Ops:
  22.2 36.7 %all-to-all-done = bf16[64,8,768]{2,0,1:T(8,128)(2,1)S(1)} async-done(((bf16[64,8,768]{2,0,1:T(8,128)(2,1)}), bf16[64,8,768]{2,0,1:T(8,128)(2,1)S(1)}, u32[]{:S(2)}, u32[]{:S(2)}) %all-to-all-start) | async-done | bytes 786464 | tf_op jit(solution)/shard_map/all_to_all | solution.py:125
  68.4 16.6 %collective-permute-done.refs_1_ = bf16[512,768]{1,0:T(8,128)(2,1)} collective-permute-done((bf16[512,768]{1,0:T(8,128)(2,1)S(1)}, bf16[512,768]{1,0:T(8,128)(2,1)}, u32[]{:S(2)}, u32[]{:S(2)}) %collective-permute-start) | collective-permute-done | bytes 786464 | tf_op jit(solution)/shard_map/ppermute | solution.py:42
  100.0 10.1 %project.1 = (bf16[1024,2048]{1,0:T(8,128)(2,1)}, bf16[1024,768]{1,0:T(8,128)(2,1)}) custom-call(s32[8]{0:T(128)} %stack.46.places_ref, bf16[1024,2048]{1,0:T(8,128)(2,1)} %all-gather.5.cloned.1.call-done.x_ref, f32[1024,256]{1,0:T(8,128)} %bitcast.102, f32[1024,256]{1,0:T(8,128)} %bitcast.100, bf16[512,768]{1,0:T(8,128)(2,1)} %bitcast.114, ...), custom_call_target="tpu_custom_call" | custom-call | flops 8999999488 | tf_op jit(solution)/shard_map/project/pallas_call | solution.py:176
  110.1 10.6 %attend.1 = bf16[1024,256]{1,0:T(8,128)(2,1)} custom-call(s32[4]{0:T(128)} %and_select_fusion.2.lo_ref, s32[1,1024]{1,0:T(1,128)} %bitcast.117, bf16[1024,768]{1,0:T(8,128)(2,1)} %get-tuple-element.68.q_ref.k_ref.v_ref, bf16[1024,768]{1,0:T(8,128)(2,1)} %get-tuple-element.68.q_ref.k_ref.v_ref, bf16[1024,768]{1,0:T(8,128)(2,1)} %get-tuple-element.68.q_ref.k_ref.v_ref), custom_call_target="tpu_custom_call" | custom-call | flops 10000000000 | tf_op jit(solution)/shard_map/attend/pallas_call | solution.py:418
  133.1 38.4 %all-to-all-done.2 = bf16[64,8,1024]{2,0,1:T(8,128)(2,1)S(1)} async-done(((bf16[64,8,1024]{2,0,1:T(8,128)(2,1)}), bf16[64,8,1024]{2,0,1:T(8,128)(2,1)S(1)}, u32[]{:S(2)}, u32[]{:S(2)}) %all-to-all-start.2) | async-done | bytes 1048608 | tf_op jit(solution)/shard_map/all_to_all | solution.py:125
  179.1 13.7 %collective-permute-done.4.refs_1_.refs_6_ = bf16[512,2048]{1,0:T(8,128)(2,1)} collective-permute-done((bf16[512,2048]{1,0:T(8,128)(2,1)S(1)}, bf16[512,2048]{1,0:T(8,128)(2,1)}, u32[]{:S(2)}, u32[]{:S(2)}) %collective-permute-start.4) | collective-permute-done | bytes 2097184 | tf_op jit(solution)/shard_map/ppermute | solution.py:42
  198.8 20.1 %collective-permute-done.5.refs_3_.refs_8_ = bf16[256,2048]{1,0:T(8,128)(2,1)S(1)} collective-permute-done((bf16[256,2048]{1,0:T(8,128)(2,1)S(1)}, bf16[256,2048]{1,0:T(8,128)(2,1)S(1)}, u32[]{:S(2)}, u32[]{:S(2)}) %collective-permute-start.5) | collective-permute-done | bytes 1048608 | tf_op jit(solution)/shard_map/ppermute | solution.py:51
  221.6 13.4 %all-to-all-done.3.own_ref = bf16[4,1024,256]{2,1,0:T(8,128)(2,1)} async-done(((bf16[4,1024,256]{2,1,0:T(8,128)(2,1)}), bf16[4,1024,256]{2,1,0:T(8,128)(2,1)}, u32[]{:S(2)}, u32[]{:S(2)}) %all-to-all-start.3) | async-done | bytes 2097184 | tf_op jit(solution)/shard_map/all_to_all | solution.py:85
  239.6 16.6 %blend.1 = (bf16[1024,2048]{1,0:T(8,128)(2,1)}, f32[1024,2048]{1,0:T(8,128)}) custom-call(s32[1]{0:T(128)} %bitcast.core_ref, bf16[1024,2048]{1,0:T(8,128)(2,1)} %all-gather.5.cloned.1.call-done.x_ref, bf16[4,1024,256]{2,1,0:T(8,128)(2,1)} %all-to-all-done.3.own_ref, bf16[4,1024,256]{2,1,0:T(8,128)(2,1)} %collective-permute-done.8.other_ref, ...), custom_call_target="tpu_custom_call" | custom-call | flops 15000000512 | tf_op jit(solution)/shard_map/blend/pallas_call | solution.py:580
  262.9 15.6 %open_units.1 = (f32[1024,1024]{1,0:T(8,128)}, f32[1024,1024]{1,0:T(8,128)}, bf16[1024,1024]{1,0:T(8,128)(2,1)}) custom-call(s32[8]{0:T(128)} %stack.46.places_ref, bf16[1024,2048]{1,0:T(8,128)(2,1)} %get-tuple-element.87.left_ref.refs_0_, bf16[512,2048]{1,0:T(8,128)(2,1)} %bitcast.95, bf16[512,2048]{1,0:T(8,128)(2,1)} %collective-permute-done.4.refs_1_.refs_6_, ...), custom_call_target="tpu_custom_call" | custom-call | flops 12000000000 | tf_op jit(solution)/shard_map/open_units/pallas_call | solution.py:221
  280.6 12.5 %close_units.1.left_ref = bf16[2,1024,1024]{2,1,0:T(8,128)(2,1)} custom-call(s32[8]{0:T(128)} %stack.46.places_ref, bf16[1024,2048]{1,0:T(8,128)(2,1)} %all-gather.9.cloned.1.call-done.back_ref.refs_0_, f32[1024,1024]{1,0:T(8,128)} %get-tuple-element.77.gate_ref, f32[1024,1024]{1,0:T(8,128)} %get-tuple-element.78.up_ref, bf16[512,1024]{1,0:T(8,128)(2,1)} %bitcast.106, ...), custom_call_target="tpu_custom_call" | custom-call | flops 7000000000 | tf_op jit(solution)/shard_map/close_units/pallas_call | solution.py:259
  293.1 16.8 %times_rows.3 = bf16[1024,2048]{1,0:T(8,128)(2,1)} custom-call(s32[8]{0:T(128)} %stack.46.places_ref, bf16[2,1024,1024]{2,1,0:T(8,128)(2,1)} %close_units.1.left_ref, bf16[512,2048]{1,0:T(8,128)(2,1)} %bitcast.97, bf16[512,2048]{1,0:T(8,128)(2,1)} %collective-permute-done.4.refs_1_.refs_6_, bf16[512,2048]{1,0:T(8,128)(2,1)} %collective-permute-done.6.refs_2_.refs_7_, ...), custom_call_target="tpu_custom_call" | custom-call | flops 8589934592 | tf_op jit(solution)/shard_map/times_rows/pallas_call | solution.py:304
  326.9 11.9 %weight_grad.4 = (bf16[512,1024]{1,0:T(8,128)(2,1)}, bf16[512,1024]{1,0:T(8,128)(2,1)}, bf16[1024,1024]{1,0:T(8,128)(2,1)}) custom-call(s32[8]{0:T(128)} %stack.47.order_ref, bf16[1024,2048]{1,0:T(8,128)(2,1)} %all-gather.9.cloned.1.call-done.back_ref.refs_0_, bf16[1,1024,1024]{2,1,0:T(8,128)(2,1)} %bitcast.119), custom_call_target="tpu_custom_call" | custom-call | flops 4294967296 | tf_op jit(solution)/shard_map/weight_grad/pallas_call | solution.py:351
  344.3 11.4 %weight_grad.5 = (bf16[512,1024]{1,0:T(8,128)(2,1)}, bf16[512,1024]{1,0:T(8,128)(2,1)}, bf16[1024,1024]{1,0:T(8,128)(2,1)}) custom-call(s32[8]{0:T(128)} %stack.47.order_ref, bf16[1024,2048]{1,0:T(8,128)(2,1)} %get-tuple-element.87.left_ref.refs_0_, bf16[1,1024,1024]{2,1,0:T(8,128)(2,1)} %get-tuple-element.128.refs_1_), custom_call_target="tpu_custom_call" | custom-call | flops 4294967296 | tf_op jit(solution)/shard_map/weight_grad/pallas_call | solution.py:351
  356.9 11.5 %weight_grad.6 = (bf16[512,1024]{1,0:T(8,128)(2,1)}, bf16[512,1024]{1,0:T(8,128)(2,1)}, bf16[1024,1024]{1,0:T(8,128)(2,1)}) custom-call(s32[8]{0:T(128)} %stack.47.order_ref, bf16[1024,2048]{1,0:T(8,128)(2,1)} %get-tuple-element.87.left_ref.refs_0_, bf16[1,1024,1024]{2,1,0:T(8,128)(2,1)} %get-tuple-element.127.refs_1_), custom_call_target="tpu_custom_call" | custom-call | flops 4294967296 | tf_op jit(solution)/shard_map/weight_grad/pallas_call | solution.py:351
  392.6 11.4 %times_rows.4 = bf16[1024,2048]{1,0:T(8,128)(2,1)} custom-call(s32[8]{0:T(128)} %stack.46.places_ref, bf16[1,1024,1024]{2,1,0:T(8,128)(2,1)} %bitcast.120, bf16[512,1024]{1,0:T(8,128)(2,1)} %bitcast.107, bf16[512,1024]{1,0:T(8,128)(2,1)} %copy-done.22, bf16[512,1024]{1,0:T(8,128)(2,1)} %copy-done.21, bf16[256,1024]{1,0:T(8,128)(2,1)} %copy-done.28, ...), custom_call_target="tpu_custom_call" | custom-call | flops 4294967296 | tf_op jit(solution)/shard_map/times_rows/pallas_call | solution.py:304
  405.4 19.6 %attend_back.1 = bf16[1024,768]{1,0:T(8,128)(2,1)} custom-call(s32[4]{0:T(128)} %and_select_fusion.2.lo_ref, s32[1,1024]{1,0:T(1,128)} %bitcast.118, bf16[1024,768]{1,0:T(8,128)(2,1)} %get-tuple-element.68.q_ref.k_ref.v_ref, bf16[1024,768]{1,0:T(8,128)(2,1)} %get-tuple-element.68.q_ref.k_ref.v_ref, bf16[1024,768]{1,0:T(8,128)(2,1)} %get-tuple-element.68.q_ref.k_ref.v_ref, ...), custom_call_target="tpu_custom_call" | custom-call | flops 20000000000 | tf_op jit(solution)/shard_map/attend_back/pallas_call | solution.py:534
  425.0 10.1 %times_rows.5 = bf16[1024,2048]{1,0:T(8,128)(2,1)} custom-call(s32[8]{0:T(128)} %stack.46.places_ref, bf16[1,1024,768]{2,1,0:T(8,128)(2,1)} %bitcast.121, bf16[512,768]{1,0:T(8,128)(2,1)} %bitcast.115, bf16[512,768]{1,0:T(8,128)(2,1)} %collective-permute-done.refs_1_, bf16[512,768]{1,0:T(8,128)(2,1)} %collective-permute-done.1.refs_2_, ...), custom_call_target="tpu_custom_call" | custom-call | flops 3221225472 | tf_op jit(solution)/shard_map/times_rows/pallas_call | solution.py:304
  449.8 14.0 %collective-permute-done.21 = bf16[512,1024]{1,0:T(8,128)(2,1)S(1)} collective-permute-done((bf16[512,1024]{1,0:T(8,128)(2,1)}, bf16[512,1024]{1,0:T(8,128)(2,1)S(1)}, u32[]{:S(2)}, u32[]{:S(2)}) %collective-permute-start.21) | collective-permute-done | bytes 1048608 | tf_op jit(solution)/shard_map/ppermute | solution.py:59
  475.8 12.1 %weight_grad.7 = (bf16[512,1024]{1,0:T(8,128)(2,1)}, bf16[512,1024]{1,0:T(8,128)(2,1)}, bf16[1024,1024]{1,0:T(8,128)(2,1)}) custom-call(s32[8]{0:T(128)} %stack.47.order_ref, bf16[1024,2048]{1,0:T(8,128)(2,1)} %get-tuple-element.91.refs_0_, bf16[1024,2048]{1,0:T(8,128)(2,1)} %all-gather.11.cloned.1.call-done.refs_1_, bf16[1,1024,768]{2,1,0:T(8,128)(2,1)} %bitcast.122, ...), custom_call_target="tpu_custom_call" | custom-call | flops 4294967296 | tf_op jit(solution)/shard_map/weight_grad/pallas_call | solution.py:351
  502.7 23.0 %collective-permute-done.26 = bf16[512,1024]{1,0:T(8,128)(2,1)S(1)} collective-permute-done((bf16[512,1024]{1,0:T(8,128)(2,1)}, bf16[512,1024]{1,0:T(8,128)(2,1)S(1)}, u32[]{:S(2)}, u32[]{:S(2)}) %collective-permute-start.26) | collective-permute-done | bytes 1048608 | tf_op jit(solution)/shard_map/ppermute | solution.py:58
  528.3 12.2 %collective-permute-done.28 = bf16[256,1024]{1,0:T(8,128)(2,1)S(1)} collective-permute-done((bf16[256,1024]{1,0:T(8,128)(2,1)S(1)}, bf16[256,1024]{1,0:T(8,128)(2,1)S(1)}, u32[]{:S(2)}, u32[]{:S(2)}) %collective-permute-start.28) | collective-permute-done | bytes 524320 | tf_op jit(solution)/shard_map/ppermute | solution.py:69
  544.6 13.4 %all-to-all-done.7.rows_ref = bf16[8,64,2048]{2,1,0:T(8,128)(2,1)S(1)} async-done(((bf16[8,64,2048]{2,1,0:T(8,128)(2,1)}), bf16[8,64,2048]{2,1,0:T(8,128)(2,1)S(1)}, u32[]{:S(2)}, u32[]{:S(2)}) %all-to-all-start.7) | async-done | bytes 2097184 | tf_op jit(solution)/shard_map/all_to_all | solution.py:693
  582.8 27.7 %all-to-all-done.8.rows_ref = bf16[8,64,1024]{2,1,0:T(8,128)(2,1)S(1)} async-done(((bf16[8,64,1024]{2,1,0:T(8,128)(2,1)}), bf16[8,64,1024]{2,1,0:T(8,128)(2,1)S(1)}, u32[]{:S(2)}, u32[]{:S(2)}) %all-to-all-start.8) | async-done | bytes 1048608 | tf_op jit(solution)/shard_map/all_to_all | solution.py:693
  (219 shorter events, 215.9 us)
Async XLA Ops:
  7.2 92.1 %all-gather.5.cloned.1.call-start = ((), (), s32[]{:S(2)}) async-start(), calls=%async_computation.11 | async-start | bytes 4718592 | tf_op jit(solution)/shard_map/all_gather | solution.py:720
  7.9 231.7 %all-gather.7.cloned.1.call-start = ((), (), s32[]{:S(2)}) async-start(), calls=%async_computation.12 | async-start | bytes 8650752 | tf_op jit(solution)/shard_map/all_gather | solution.py:728
  12.3 46.6 %all-to-all-start = ((bf16[64,8,768]{2,0,1:T(8,128)(2,1)}), bf16[64,8,768]{2,0,1:T(8,128)(2,1)S(1)}, u32[]{:S(2)}, u32[]{:S(2)}) async-start(bf16[64,8,768]{2,0,1:T(8,128)(2,1)} %pad_maximum_fusion.3), calls=%async_computation | async-start | bytes 1572864 | tf_op jit(solution)/shard_map/all_to_all | solution.py:125
  60.5 64.7 %all-to-all-start.1 = ((bf16[64,8,2048]{2,0,1:T(8,128)(2,1)}), bf16[64,8,2048]{2,0,1:T(8,128)(2,1)S(1)}, u32[]{:S(2)}, u32[]{:S(2)}) async-start(bf16[64,8,2048]{2,0,1:T(8,128)(2,1)} %bitcast.74), calls=%async_computation.1 | async-start | bytes 4194304 | tf_op jit(solution)/shard_map/all_to_all | solution.py:125
  126.3 45.2 %all-to-all-start.2 = ((bf16[64,8,1024]{2,0,1:T(8,128)(2,1)}), bf16[64,8,1024]{2,0,1:T(8,128)(2,1)S(1)}, u32[]{:S(2)}, u32[]{:S(2)}) async-start(bf16[64,8,1024]{2,0,1:T(8,128)(2,1)} %bitcast.77), calls=%async_computation.2 | async-start | bytes 2097152 | tf_op jit(solution)/shard_map/all_to_all | solution.py:125
  129.9 63.0 %collective-permute-start.4 = (bf16[512,2048]{1,0:T(8,128)(2,1)S(1)}, bf16[512,2048]{1,0:T(8,128)(2,1)}, u32[]{:S(2)}, u32[]{:S(2)}) collective-permute-start(bf16[512,2048]{1,0:T(8,128)(2,1)S(1)} %bitcast.93), channel_id=1, source_target_pairs={{0,8},{8,0},{16,24},{24,16},{1,9},{9,1},{17,25},{25,17},{2,10},{10... | collective-permute-start | bytes 6291464 | tf_op jit(solution)/shard_map/ppermute | solution.py:42
  131.5 64.4 %collective-permute-start.6 = (bf16[512,2048]{1,0:T(8,128)(2,1)S(1)}, bf16[512,2048]{1,0:T(8,128)(2,1)}, u32[]{:S(2)}, u32[]{:S(2)}) collective-permute-start(bf16[512,2048]{1,0:T(8,128)(2,1)S(1)} %bitcast.94), channel_id=1, source_target_pairs={{0,16},{8,24},{16,0},{24,8},{1,17},{9,25},{17,1},{25,9},{2,18},{10... | collective-permute-start | bytes 6291464 | tf_op jit(solution)/shard_map/ppermute | solution.py:43
  174.4 60.6 %all-to-all-start.3 = ((bf16[4,1024,256]{2,1,0:T(8,128)(2,1)}), bf16[4,1024,256]{2,1,0:T(8,128)(2,1)}, u32[]{:S(2)}, u32[]{:S(2)}) async-start(bf16[4,1024,256]{2,1,0:T(8,128)(2,1)} %broadcast_in_dim.62), calls=%async_computation.3 | async-start | bytes 4194304 | tf_op jit(solution)/shard_map/all_to_all | solution.py:85
  178.9 101.7 %all-gather.9.cloned.1.call-start = ((), (), s32[]{:S(2)}) async-start(), calls=%async_computation.13 | async-start | bytes 4718592 | tf_op jit(solution)/shard_map/all_gather | solution.py:760
  321.1 52.7 %all-to-all-start.4 = ((bf16[4,128,2048]{2,1,0:T(8,128)(2,1)}), bf16[4,128,2048]{2,1,0:T(8,128)(2,1)S(1)}, u32[]{:S(2)}, u32[]{:S(2)}) async-start(bf16[4,128,2048]{2,1,0:T(8,128)(2,1)} %fusion), calls=%async_computation.4 | async-start | bytes 4194304 | tf_op jit(solution)/shard_map/all_to_all | solution.py:110
  338.8 29.5 %collective-permute-start.14 = (bf16[512,1024]{1,0:T(8,128)(2,1)}, bf16[512,1024]{1,0:T(8,128)(2,1)S(1)}, u32[]{:S(2)}, u32[]{:S(2)}) collective-permute-start(bf16[512,1024]{1,0:T(8,128)(2,1)} %get-tuple-element.83), channel_id=1, source_target_pairs={{0,8},{8,0},{16,24},{24,16},{1,9},{9,1},{17,25},{25,17},{2,10},{10... | collective-permute-start | bytes 3145736 | tf_op jit(solution)/shard_map/ppermute | solution.py:58
  340.3 29.0 %collective-permute-start.15 = (bf16[512,1024]{1,0:T(8,128)(2,1)}, bf16[512,1024]{1,0:T(8,128)(2,1)}, u32[]{:S(2)}, u32[]{:S(2)}) collective-permute-start(bf16[512,1024]{1,0:T(8,128)(2,1)} %get-tuple-element.84), channel_id=1, source_target_pairs={{0,16},{8,24},{16,0},{24,8},{1,17},{9,25},{17,1},{25,9},{2,18},{10... | collective-permute-start | bytes 3145736 | tf_op jit(solution)/shard_map/ppermute | solution.py:59
  355.8 48.2 %collective-permute-start.18 = (bf16[512,1024]{1,0:T(8,128)(2,1)}, bf16[512,1024]{1,0:T(8,128)(2,1)}, u32[]{:S(2)}, u32[]{:S(2)}) collective-permute-start(bf16[512,1024]{1,0:T(8,128)(2,1)} %get-tuple-element.86), channel_id=1, source_target_pairs={{0,8},{8,0},{16,24},{24,16},{1,9},{9,1},{17,25},{25,17},{2,10},{10... | collective-permute-start | bytes 3145736 | tf_op jit(solution)/shard_map/ppermute | solution.py:58
  356.3 47.7 %collective-permute-start.19 = (bf16[512,1024]{1,0:T(8,128)(2,1)}, bf16[512,1024]{1,0:T(8,128)(2,1)}, u32[]{:S(2)}, u32[]{:S(2)}) collective-permute-start(bf16[512,1024]{1,0:T(8,128)(2,1)} %get-tuple-element.95), channel_id=1, source_target_pairs={{0,16},{8,24},{16,0},{24,8},{1,17},{9,25},{17,1},{25,9},{2,18},{10... | collective-permute-start | bytes 3145736 | tf_op jit(solution)/shard_map/ppermute | solution.py:59
  387.0 88.8 %all-gather.11.cloned.1.call-start = ((), (), s32[]{:S(2)}) async-start(), calls=%async_computation.14 | async-start | bytes 4718592 | tf_op jit(solution)/shard_map/all_gather | solution.py:793
  405.4 176.0 %reduce-scatter.5.cloned.1.call-start = ((), (), s32[]{:S(2)}) async-start(), calls=%async_computation.16 | async-start | bytes 4718592 | tf_op jit(solution)/shard_map/reduce_scatter | solution.py:803
  438.0 26.4 %collective-permute-start.20 = (bf16[512,1024]{1,0:T(8,128)(2,1)}, bf16[512,1024]{1,0:T(8,128)(2,1)}, u32[]{:S(2)}, u32[]{:S(2)}) collective-permute-start(bf16[512,1024]{1,0:T(8,128)(2,1)} %get-tuple-element.98), channel_id=1, source_target_pairs={{0,8},{8,0},{16,24},{24,16},{1,9},{9,1},{17,25},{25,17},{2,10},{10... | collective-permute-start | bytes 3145736 | tf_op jit(solution)/shard_map/ppermute | solution.py:58
  440.5 47.4 %all-to-all-start.6 = ((bf16[8,64,1024]{2,1,0:T(8,128)(2,1)}), bf16[8,64,1024]{2,1,0:T(8,128)(2,1)S(1)}, u32[]{:S(2)}, u32[]{:S(2)}) async-start(bf16[8,64,1024]{2,1,0:T(8,128)(2,1)} %bitcast.30), calls=%async_computation.6 | async-start | bytes 2097152 | tf_op jit(solution)/shard_map/all_to_all | solution.py:693
  445.3 173.6 %reduce-scatter.3.cloned.1.call-start = ((), (), s32[]{:S(2)}) async-start(), calls=%async_computation.15 | async-start | bytes 4718592 | tf_op jit(solution)/shard_map/reduce_scatter | solution.py:813
  447.7 27.3 %collective-permute-start.22 = (bf16[256,1024]{1,0:T(8,128)(2,1)S(1)}, bf16[256,1024]{1,0:T(8,128)(2,1)S(1)}, u32[]{:S(2)}, u32[]{:S(2)}) collective-permute-start(bf16[256,1024]{1,0:T(8,128)(2,1)S(1)} %get-tuple-element.140), channel_id=1, source_target_pairs={{0,16},{8,24},{16,0},{24,8},{1,17},{9,25},{17,1},{25,9},{2,18},{10... | collective-permute-start | bytes 1572872 | tf_op jit(solution)/shard_map/ppermute | solution.py:69
  449.2 26.5 %collective-permute-start.23 = (bf16[256,1024]{1,0:T(8,128)(2,1)S(1)}, bf16[256,1024]{1,0:T(8,128)(2,1)}, u32[]{:S(2)}, u32[]{:S(2)}) collective-permute-start(bf16[256,1024]{1,0:T(8,128)(2,1)S(1)} %get-tuple-element.139), channel_id=1, source_target_pairs={{0,8},{8,0},{16,24},{24,16},{1,9},{9,1},{17,25},{25,17},{2,10},{10... | collective-permute-start | bytes 1572872 | tf_op jit(solution)/shard_map/ppermute | solution.py:70
  495.1 63.0 %all-to-all-start.7 = ((bf16[8,64,2048]{2,1,0:T(8,128)(2,1)}), bf16[8,64,2048]{2,1,0:T(8,128)(2,1)S(1)}, u32[]{:S(2)}, u32[]{:S(2)}) async-start(bf16[8,64,2048]{2,1,0:T(8,128)(2,1)} %bitcast.80), calls=%async_computation.8 | async-start | bytes 4194304 | tf_op jit(solution)/shard_map/all_to_all | solution.py:693
  501.3 27.0 %collective-permute-start.27 = (bf16[512,1024]{1,0:T(8,128)(2,1)}, bf16[512,1024]{1,0:T(8,128)(2,1)S(1)}, u32[]{:S(2)}, u32[]{:S(2)}) collective-permute-start(bf16[512,1024]{1,0:T(8,128)(2,1)} %get-tuple-element.110), channel_id=1, source_target_pairs={{0,16},{8,24},{16,0},{24,8},{1,17},{9,25},{17,1},{25,9},{2,18},{10... | collective-permute-start | bytes 3145736 | tf_op jit(solution)/shard_map/ppermute | solution.py:59
  561.6 49.0 %all-to-all-start.8 = ((bf16[8,64,1024]{2,1,0:T(8,128)(2,1)}), bf16[8,64,1024]{2,1,0:T(8,128)(2,1)S(1)}, u32[]{:S(2)}, u32[]{:S(2)}) async-start(bf16[8,64,1024]{2,1,0:T(8,128)(2,1)} %bitcast.87), calls=%async_computation.10 | async-start | bytes 2097152 | tf_op jit(solution)/shard_map/all_to_all | solution.py:693
  (53 other events, 694.8 us)
Sparse Core Ops, SparseCore 0:
  9.6 76.8 all-gather.4
  89.5 118.4 all-gather.6
  235.1 45.4 all-gather.8
  405.5 49.2 all-gather.10
  456.9 60.1 reduce-scatter.4
  519.3 95.6 reduce-scatter.2

commit v4 on v3

--- a/solution.py
+++ b/solution.py
@@ -79,15 +79,13 @@
     return jnp.concatenate([top + last[0].astype(F32), low + last[1].astype(F32)])
 
 
-def spread_cores(block):
-    size = lax.axis_size("ctx")
-    pairs = size // 2
+def spread_cores(copies):
     return lax.all_to_all(
-        jnp.broadcast_to(block[None], (pairs,) + block.shape),
+        copies,
         "ctx",
         0,
         0,
-        axis_index_groups=same_core_groups(size),
+        axis_index_groups=same_core_groups(lax.axis_size("ctx")),
         tiled=True,
     )
 
@@ -97,13 +95,8 @@
 
 
 def pair_sums(part):
-    size = lax.axis_size("ctx")
-    core = lax.axis_index("ctx") % 2
-    shaped = part.reshape(size // 2, 2, part.shape[0] // size, part.shape[1])
-    mine = lax.dynamic_index_in_dim(shaped, core, 1, keepdims=False)
-    theirs = lax.dynamic_index_in_dim(shaped, 1 - core, 1, keepdims=False)
-    got = other_core(theirs)
-    return (mine.astype(F32) + got.astype(F32)).astype(part.dtype)
+    got = other_core(part[1])
+    return (part[0].astype(F32) + got.astype(F32)).astype(part.dtype)
 
 
 def swap_chips(sums):
@@ -121,8 +114,15 @@
     return jnp.sum(landed.astype(F32), axis=0)
 
 
-def to_columns(rows_block):
-    return lax.all_to_all(rows_block, "ctx", split_axis=1, concat_axis=0, tiled=True)
+def by_owner(rows_block):
+    size = lax.axis_size("ctx")
+    shaped = rows_block.reshape(rows_block.shape[0], size, -1)
+    return lax.optimization_barrier(jnp.swapaxes(shaped, 0, 1))
+
+
+def to_columns(pieces):
+    landed = lax.all_to_all(pieces, "ctx", 0, 0, tiled=True)
+    return landed.reshape(-1, landed.shape[2])
 
 
 def swap_halves(values):
@@ -273,51 +273,70 @@
     )(places, back, gate, up, *pieces)
 
 
-def times_rows_kernel(pieces, places_ref, left_ref, *refs):
-    out_ref, w_ref = refs[len(pieces) :]
+def times_rows_kernel(pieces, chips, places_ref, core_ref, left_ref, *refs):
+    out_ref = refs[len(pieces)]
     step = pl.program_id(0)
-    first = 0
+    parts, count, width = left_ref.shape
+
+    def put(ref):
+        value = dot(left_ref[0], ref[:, :width], 1, 1)
+        for part in range(1, parts):
+            value += dot(left_ref[part], ref[:, part * width : (part + 1) * width], 1, 1)
+        low = value.astype(LOW)
+        if not chips:
+            out_ref[...] = low
+            return
+        rows = count // (2 * chips)
+        for chip in range(chips):
+            first = low[2 * chip * rows : (2 * chip + 1) * rows]
+            second = low[(2 * chip + 1) * rows : (2 * chip + 2) * rows]
+            out_ref[0, chip] = jnp.where(core_ref[0] == 0, first, second)
+            out_ref[1, chip] = jnp.where(core_ref[0] == 0, second, first)
+
+    first_step = 0
     for ref, units in zip(refs, pieces):
 
-        @pl.when((step >= first) & (step < first + units))
+        @pl.when((step >= first_step) & (step < first_step + units))
         def _():
-            w_ref[...] = ref[...]
-
-        first += units
-    parts, unused, width = left_ref.shape
-    total_ = dot(left_ref[0], w_ref[:, :width], 1, 1)
-    for part in range(1, parts):
-        total_ += dot(left_ref[part], w_ref[:, part * width : (part + 1) * width], 1, 1)
-    out_ref[...] = total_.astype(LOW)
-
-
-def times_rows(places, left, pieces):
+            put(ref)
+
+        first_step += units
+
+
+def times_rows(places, core, left, pieces, chips=0):
     parts, count, width = left.shape
     units = [piece.shape[0] // UNIT for piece in pieces]
     firsts = [sum(units[:index]) for index in range(len(units))]
 
     def spec(first, held):
         return pl.BlockSpec(
-            (UNIT, parts * width), lambda s, p: (jnp.clip(s - first, 0, held - 1), 0)
+            (UNIT, parts * width), lambda s, p, c: (jnp.clip(s - first, 0, held - 1), 0)
         )
 
+    features = sum(units) * UNIT
+    if chips:
+        rows = count // (2 * chips)
+        out_spec = pl.BlockSpec((2, chips, rows, UNIT), lambda s, p, c: (0, 0, 0, p[s]))
+        shape = (2, chips, rows, features)
+    else:
+        out_spec = pl.BlockSpec((count, UNIT), lambda s, p, c: (0, p[s]))
+        shape = (count, features)
     return pl.pallas_call(
-        functools.partial(times_rows_kernel, units),
+        functools.partial(times_rows_kernel, units, chips),
         grid_spec=pltpu.PrefetchScalarGridSpec(
-            num_scalar_prefetch=1,
+            num_scalar_prefetch=2,
             grid=(sum(units),),
-            in_specs=[pl.BlockSpec(left.shape, lambda s, p: (0, 0, 0))]
+            in_specs=[pl.BlockSpec(left.shape, lambda s, p, c: (0, 0, 0))]
             + [spec(first, held) for first, held in zip(firsts, units)],
-            out_specs=pl.BlockSpec((count, UNIT), lambda s, p: (0, p[s])),
-            scratch_shapes=[pltpu.VMEM((UNIT, parts * width), LOW)],
-        ),
-        out_shape=jax.ShapeDtypeStruct((count, sum(units) * UNIT), LOW),
+            out_specs=out_spec,
+        ),
+        out_shape=jax.ShapeDtypeStruct(shape, LOW),
         compiler_params=pltpu.CompilerParams(vmem_limit_bytes=VMEM_LIMIT),
         cost_estimate=pl.CostEstimate(
-            flops=2 * parts * count * width * sum(units) * UNIT, bytes_accessed=0, transcendentals=0
+            flops=2 * parts * count * width * features, bytes_accessed=0, transcendentals=0
         ),
         name="times_rows",
-    )(places, left, *pieces)
+    )(places, core, left, *pieces)
 
 
 def weight_grad_kernel(outs, pairs, order_ref, *refs):
@@ -408,10 +427,12 @@
         ((jnp.zeros((1, BLOCK), F32),) * heads, (jnp.zeros((HD, BLOCK), F32),) * heads),
     )
     turned = jnp.concatenate([totals[h] / sums[h] for h in range(heads)], axis=0)
-    out_ref[...] = turned.T.astype(LOW)
-
-
-def attend(lows, starts, qkv):
+    low = turned.T.astype(LOW)
+    for chip in range(out_ref.shape[0]):
+        out_ref[chip] = low
+
+
+def attend(lows, starts, qkv, chips):
     count = qkv.shape[0]
     width = qkv.shape[1] // 3
     heads = width // HD
@@ -426,10 +447,10 @@
                 pl.BlockSpec((count, width), lambda i, lo: (0, 1)),
                 pl.BlockSpec((count, width), lambda i, lo: (0, 2)),
             ],
-            out_specs=pl.BlockSpec((BLOCK, width), lambda i, lo: (i, 0)),
+            out_specs=pl.BlockSpec((chips, BLOCK, width), lambda i, lo: (0, i, 0)),
             scratch_shapes=[pltpu.VMEM((heads, count, BLOCK), F32)],
         ),
-        out_shape=jax.ShapeDtypeStruct((count, width), LOW),
+        out_shape=jax.ShapeDtypeStruct((chips, count, width), LOW),
         compiler_params=pltpu.CompilerParams(vmem_limit_bytes=VMEM_LIMIT),
         cost_estimate=pl.CostEstimate(flops=10 * GIGA, bytes_accessed=0, transcendentals=0),
         name="attend",
@@ -615,23 +636,26 @@
 
     gain = gain_ref[...]
     for part in range(parts):
-        raw = rows_ref[0, :, part * width : (part + 1) * width].astype(F32)
-        if part < scaled_parts:
-            product = raw * weights[part][...].astype(F32)
-            gain_grad_ref[...] += jnp.sum(product, axis=1, keepdims=True)
-            raw = raw * gain
-        grads[part][...] = raw
+        for index in range(rows_ref.shape[0]):
+            lane = slice(index * width, (index + 1) * width)
+            raw = rows_ref[index, :, part * width : (part + 1) * width].astype(F32)
+            if part < scaled_parts:
+                product = raw * weights[part][:, lane].astype(F32)
+                gain_grad_ref[...] += jnp.sum(product, axis=1, keepdims=True)
+                raw = raw * gain
+            grads[part][:, lane] = raw
 
 
 def finish(rows, gain, weights, parts):
     size, share, wide = rows.shape
     width = wide // parts
     column = pl.BlockSpec((share, 1), lambda i: (0, 0))
-    block = pl.BlockSpec((share, width), lambda i: (0, i))
+    held = min(size, max(1, 2048 // width))
+    block = pl.BlockSpec((share, held * width), lambda i: (0, i))
     out = pl.pallas_call(
         functools.partial(finish_kernel, parts, len(weights)),
-        grid=(size,),
-        in_specs=[pl.BlockSpec((1, share, wide), lambda i: (i, 0, 0)), column]
+        grid=(size // held,),
+        in_specs=[pl.BlockSpec((held, share, wide), lambda i: (i, 0, 0)), column]
         + [block] * len(weights),
         out_specs=[block] * parts + [column],
         out_shape=[jax.ShapeDtypeStruct((share, size * width), F32)] * parts
@@ -726,9 +750,11 @@
         axis=2,
     ).reshape(share, 3 * features)
     out_all = lax.all_gather(after(w_out, stacked), ("fsdp", "ctx"), axis=0, tiled=True)
-    qkv_rows = to_columns(stacked)
+    qkv_rows = to_columns(by_owner(stacked))
     qkv_near = pull_near(qkv_rows)
-    two_rows = to_columns(after(paired(scaled(w_gate, gain_m), scaled(w_up, gain_m)), qkv_rows))
+    two_rows = to_columns(
+        after(by_owner(paired(scaled(w_gate, gain_m), scaled(w_up, gain_m))), qkv_rows)
+    )
     qkv_far = pull_far(qkv_near)
     w_qkv = pulled(qkv_rows, qkv_near, qkv_far)
 
@@ -750,8 +776,8 @@
     starts_row = starts[None, :]
 
     unit, qkv = project(places, x_all, w_qkv, cos, sin)
-    attended = attend(lows, starts_row, qkv)
-    down_rows = to_columns(after(w_down, two_rows, attended))
+    attended = attend(lows, starts_row, qkv, n_c // 2)
+    down_rows = to_columns(after(by_owner(w_down), two_rows, attended))
     two_near = pull_near(two_rows)
     attended_mine = spread_cores(after(attended, down_rows))
     two_far = pull_far(two_near)
@@ -767,7 +793,7 @@
 
     gate, up, hidden = open_units(places, unit_mlp, col_two)
     d_both = close_units(places, back_all, gate, up, col_down)
-    d_unit_sums = pair_sums(times_rows(places, d_both, col_two))
+    d_unit_sums = pair_sums(times_rows(places, core, d_both, col_two, n_c // 2))
     d_unit_landed = swap_chips(d_unit_sums)
     part_down = weight_grad(order, outs, (after(back_all, d_unit_sums), hidden[None]))
     down_landed = push_near(part_down)
@@ -784,7 +810,7 @@
     d_mixed_low = d_mixed.astype(LOW)
     d_att = dot(d_mixed_low, out_all, 1, 0).astype(LOW)
     gate_landed = push_near(part_gate)
-    branch = times_rows(places, after(hidden, d_att)[None], col_down)
+    branch = times_rows(places, core, after(hidden, d_att)[None], col_down)
     down_landed = tuple(after(piece, d_att) for piece in down_landed)
     d_att_own = lax.all_to_all(d_att, "ctx", split_axis=1, concat_axis=0, tiled=True)
     down_last = push_far(part_down, down_landed)
@@ -799,10 +825,10 @@
     rows_down = to_rows(after(pushed(part_down, down_landed, down_last), d_att_own))
 
     d_qkv = attend_back(lows, starts_row, qkv, d_att_own, cos, sin)
-    first_part = times_rows(places, d_qkv[None], w_qkv)
+    first_part = times_rows(places, core, d_qkv[None], w_qkv)
     d_first = lax.psum_scatter(first_part, "ctx", scatter_dimension=0, tiled=True).astype(F32)
     part_qkv = weight_grad(
-        order, outs, (unit, after(d_qkv, first_part, *up_landed, *gate_last)[None]), (d_mixed_all, attended[None])
+        order, outs, (unit, after(d_qkv, first_part, *up_landed, *gate_last)[None]), (d_mixed_all, attended[:1])
     )
     part_qkv = [after(part, rows_down, *up_last) for part in part_qkv]
     qkv_landed = push_near(part_qkv)

time: 642 us -> 633 us (0.986)
  local copies, waits for them, and re-layouts: 31.2 us -> 24.1 us
  Pallas kernels: 189 us -> 182 us
    ppermute x3, waiting for transfers between devices: 4.53 us -> 37.7 us  [near(): lax.ppermute(block, 'fsdp', flip('fsdp', 4, 2))]
    ppermute x3, waiting for transfers between devices: 31.3 us -> 1.2 us  [near(): lax.ppermute(block, 'fsdp', flip('fsdp', 4, 1))]
    ppermute x3, waiting for transfers between devices: 20.9 us -> 3.83 us  [far(): lax.ppermute(from_x[:half], 'fsdp', flip('fsdp', 4, 2))]
    ppermute x3, waiting for transfers between devices: 4.06 us -> 20 us  [far(): lax.ppermute(from_y[half:], 'fsdp', flip('fsdp', 4, 1))]
    ppermute x4, waiting for transfers between devices: 23.6 us -> 37.2 us  [reduce_near(): lax.ppermute(part[0], 'fsdp', flip('fsdp', 4, 1))]
    ppermute x4, waiting for transfers between devices: 14 us -> 0.55 us  [reduce_near(): lax.ppermute(part[1], 'fsdp', flip('fsdp', 4, 2))]
    pallas_call x3, Pallas kernels: 18.5 us -> 11.7 us  [finish(): pl.pallas_call(functools.partial(finish_kernel, parts, len(weights)), gri...]
  transfers between devices with their start and end apart: 45 -> 45, of which waited for: 25 -> 24; matrix products, arithmetic and copies ran while one was open for 11% -> 10% of each run, Pallas kernels for 25% -> 25%
where the time goes in v4:
time: 633 us; the launch traced here: 621 us
  waiting for transfers between devices  268 us (42%)
  Pallas kernels  182 us (29%)
  starting transfers between devices  79 us (12%)
  other arithmetic  47.9 us (8%)
  local copies, waits for them, and re-layouts  24.1 us (4%)
  between operations  15.1 us (2%)
    all_to_all x3, waiting for transfers between devices, to_columns(): landed = lax.all_to_all(pieces, 'ctx', 0, 0, tiled=True)  81.6 us
    pallas_call x4, Pallas kernels, weight_grad(): pl.pallas_call(functools.partial(weight_grad_kernel, outs, len(pairs)), g...  46.9 us
    all_to_all x3, waiting for transfers between devices, to_rows(): return lax.all_to_all(value, 'ctx', split_axis=0, concat_axis=0, tiled=True)  45 us
    ppermute x3, waiting for transfers between devices, near(): lax.ppermute(block, 'fsdp', flip('fsdp', 4, 2))  37.7 us
    pallas_call x3, Pallas kernels, times_rows(): pl.pallas_call(functools.partial(times_rows_kernel, units, chips), grid_s...  37.6 us
    ppermute x4, waiting for transfers between devices, reduce_near(): lax.ppermute(part[0], 'fsdp', flip('fsdp', 4, 1))  37.2 us
    ppermute x3, waiting for transfers between devices, far(): lax.ppermute(from_y[half:], 'fsdp', flip('fsdp', 4, 1))  20 us
    pallas_call x1, Pallas kernels, attend_back(): pl.pallas_call(functools.partial(attend_back_kernel, heads), grid_spec=pl...  19.9 us
  transfers between devices with their start and end apart: 45, of which 24 were waited for; matrix products, arithmetic and copies ran while one was open for 10% of the time, Pallas kernels for 25%

profile of v4, /device:TPU:0, one launch (start us, length us, event | category | flops | bytes accessed | tf_op | source)
XLA Modules:
  0.0 620.9 jit_solution(6980258053781020354)
XLA Ops:
  21.4 37.5 %all-to-all-done = bf16[8,64,768]{2,1,0:T(8,128)(2,1)S(1)} async-done(((bf16[8,64,768]{2,1,0:T(8,128)(2,1)}), bf16[8,64,768]{2,1,0:T(8,128)(2,1)S(1)}, u32[]{:S(2)}, u32[]{:S(2)}) %all-to-all-start) | async-done | bytes 786464 | tf_op jit(solution)/shard_map/all_to_all | solution.py:124
  66.9 16.6 %collective-permute-done.1.refs_2_ = bf16[512,768]{1,0:T(8,128)(2,1)} collective-permute-done((bf16[512,768]{1,0:T(8,128)(2,1)S(1)}, bf16[512,768]{1,0:T(8,128)(2,1)}, u32[]{:S(2)}, u32[]{:S(2)}) %collective-permute-start.1) | collective-permute-done | bytes 786464 | tf_op jit(solution)/shard_map/ppermute | solution.py:43
  98.4 10.2 %project.1 = (bf16[1024,2048]{1,0:T(8,128)(2,1)}, bf16[1024,768]{1,0:T(8,128)(2,1)}) custom-call(s32[8]{0:T(128)} %stack.46.places_ref, bf16[1024,2048]{1,0:T(8,128)(2,1)} %all-gather.5.cloned.1.call-done.x_ref, f32[1024,256]{1,0:T(8,128)} %bitcast.93, f32[1024,256]{1,0:T(8,128)} %bitcast.91, bf16[512,768]{1,0:T(8,128)(2,1)} %bitcast.105, ...), custom_call_target="tpu_custom_call" | custom-call | flops 8999999488 | tf_op jit(solution)/shard_map/project/pallas_call | solution.py:176
  108.6 10.6 %attend.1 = bf16[4,1024,256]{2,1,0:T(8,128)(2,1)} custom-call(s32[4]{0:T(128)} %and_select_fusion.2.lo_ref, s32[1,1024]{1,0:T(1,128)} %bitcast.107, bf16[1024,768]{1,0:T(8,128)(2,1)} %get-tuple-element.68.q_ref.k_ref.v_ref, bf16[1024,768]{1,0:T(8,128)(2,1)} %get-tuple-element.68.q_ref.k_ref.v_ref, bf16[1024,768]{1,0:T(8,128)(2,1)} %get-tuple-element.68.q_ref.k_ref.v_ref), custom_call_target="tpu_custom_call" | custom-call | flops 10000000000 | tf_op jit(solution)/shard_map/attend/pallas_call | solution.py:439
  131.8 38.4 %all-to-all-done.2 = bf16[8,64,1024]{2,1,0:T(8,128)(2,1)S(1)} async-done(((bf16[8,64,1024]{2,1,0:T(8,128)(2,1)}), bf16[8,64,1024]{2,1,0:T(8,128)(2,1)S(1)}, u32[]{:S(2)}, u32[]{:S(2)}) %all-to-all-start.2) | async-done | bytes 1048608 | tf_op jit(solution)/shard_map/all_to_all | solution.py:124
  174.8 16.8 %collective-permute-done.6.refs_2_.refs_7_ = bf16[512,2048]{1,0:T(8,128)(2,1)} collective-permute-done((bf16[512,2048]{1,0:T(8,128)(2,1)S(1)}, bf16[512,2048]{1,0:T(8,128)(2,1)}, u32[]{:S(2)}, u32[]{:S(2)}) %collective-permute-start.6) | collective-permute-done | bytes 2097184 | tf_op jit(solution)/shard_map/ppermute | solution.py:43
  197.4 20.0 %collective-permute-done.7.refs_4_.refs_9_ = bf16[256,2048]{1,0:T(8,128)(2,1)S(1)} collective-permute-done((bf16[256,2048]{1,0:T(8,128)(2,1)S(1)}, bf16[256,2048]{1,0:T(8,128)(2,1)S(1)}, u32[]{:S(2)}, u32[]{:S(2)}) %collective-permute-start.7) | collective-permute-done | bytes 1048608 | tf_op jit(solution)/shard_map/ppermute | solution.py:52
  220.2 10.9 %all-to-all-done.3.own_ref = bf16[4,1024,256]{2,1,0:T(8,128)(2,1)} async-done(((bf16[4,1024,256]{2,1,0:T(8,128)(2,1)}), bf16[4,1024,256]{2,1,0:T(8,128)(2,1)}, u32[]{:S(2)}, u32[]{:S(2)}) %all-to-all-start.3) | async-done | bytes 2097184 | tf_op jit(solution)/shard_map/all_to_all | solution.py:83
  235.7 16.8 %blend.1 = (bf16[1024,2048]{1,0:T(8,128)(2,1)}, f32[1024,2048]{1,0:T(8,128)}) custom-call(s32[1]{0:T(128)} %bitcast.core_ref, bf16[1024,2048]{1,0:T(8,128)(2,1)} %all-gather.5.cloned.1.call-done.x_ref, bf16[4,1024,256]{2,1,0:T(8,128)(2,1)} %all-to-all-done.3.own_ref, bf16[4,1024,256]{2,1,0:T(8,128)(2,1)} %collective-permute-done.8.other_ref, ...), custom_call_target="tpu_custom_call" | custom-call | flops 15000000512 | tf_op jit(solution)/shard_map/blend/pallas_call | solution.py:601
  260.1 15.6 %open_units.1 = (f32[1024,1024]{1,0:T(8,128)}, f32[1024,1024]{1,0:T(8,128)}, bf16[1024,1024]{1,0:T(8,128)(2,1)}) custom-call(s32[8]{0:T(128)} %stack.46.places_ref, bf16[1024,2048]{1,0:T(8,128)(2,1)} %get-tuple-element.87.left_ref.refs_0_, bf16[512,2048]{1,0:T(8,128)(2,1)} %bitcast.86, bf16[512,2048]{1,0:T(8,128)(2,1)} %collective-permute-done.4.refs_1_.refs_6_, ...), custom_call_target="tpu_custom_call" | custom-call | flops 12000000000 | tf_op jit(solution)/shard_map/open_units/pallas_call | solution.py:221
  277.4 12.5 %close_units.1.left_ref = bf16[2,1024,1024]{2,1,0:T(8,128)(2,1)} custom-call(s32[8]{0:T(128)} %stack.46.places_ref, bf16[1024,2048]{1,0:T(8,128)(2,1)} %all-gather.9.cloned.1.call-done.back_ref.refs_0_, f32[1024,1024]{1,0:T(8,128)} %get-tuple-element.77.gate_ref, f32[1024,1024]{1,0:T(8,128)} %get-tuple-element.78.up_ref, bf16[512,1024]{1,0:T(8,128)(2,1)} %bitcast.97, ...), custom_call_target="tpu_custom_call" | custom-call | flops 7000000000 | tf_op jit(solution)/shard_map/close_units/pallas_call | solution.py:259
  289.8 16.3 %times_rows.3 = bf16[2,4,128,2048]{3,2,1,0:T(8,128)(2,1)} custom-call(s32[8]{0:T(128)} %stack.46.places_ref, s32[1]{0:T(128)} %bitcast.core_ref, bf16[2,1024,1024]{2,1,0:T(8,128)(2,1)} %close_units.1.left_ref, bf16[512,2048]{1,0:T(8,128)(2,1)} %bitcast.88, bf16[512,2048]{1,0:T(8,128)(2,1)} %collective-permute-done.4.refs_1_.refs_6_, ...), custom_call_target="tpu_custom_call" | custom-call | flops 8589934592 | tf_op jit(solution)/shard_map/times_rows/pallas_call | solution.py:324
  320.2 11.9 %weight_grad.4 = (bf16[512,1024]{1,0:T(8,128)(2,1)}, bf16[512,1024]{1,0:T(8,128)(2,1)}, bf16[1024,1024]{1,0:T(8,128)(2,1)}) custom-call(s32[8]{0:T(128)} %stack.47.order_ref, bf16[1024,2048]{1,0:T(8,128)(2,1)} %all-gather.9.cloned.1.call-done.back_ref.refs_0_, bf16[1,1024,1024]{2,1,0:T(8,128)(2,1)} %bitcast.109), custom_call_target="tpu_custom_call" | custom-call | flops 4294967296 | tf_op jit(solution)/shard_map/weight_grad/pallas_call | solution.py:370
  337.6 11.4 %weight_grad.5 = (bf16[512,1024]{1,0:T(8,128)(2,1)}, bf16[512,1024]{1,0:T(8,128)(2,1)}, bf16[1024,1024]{1,0:T(8,128)(2,1)}) custom-call(s32[8]{0:T(128)} %stack.47.order_ref, bf16[1024,2048]{1,0:T(8,128)(2,1)} %get-tuple-element.87.left_ref.refs_0_, bf16[1,1024,1024]{2,1,0:T(8,128)(2,1)} %get-tuple-element.128.refs_1_), custom_call_target="tpu_custom_call" | custom-call | flops 4294967296 | tf_op jit(solution)/shard_map/weight_grad/pallas_call | solution.py:370
  350.2 11.4 %weight_grad.6 = (bf16[512,1024]{1,0:T(8,128)(2,1)}, bf16[512,1024]{1,0:T(8,128)(2,1)}, bf16[1024,1024]{1,0:T(8,128)(2,1)}) custom-call(s32[8]{0:T(128)} %stack.47.order_ref, bf16[1024,2048]{1,0:T(8,128)(2,1)} %get-tuple-element.87.left_ref.refs_0_, bf16[1,1024,1024]{2,1,0:T(8,128)(2,1)} %get-tuple-element.127.refs_1_), custom_call_target="tpu_custom_call" | custom-call | flops 4294967296 | tf_op jit(solution)/shard_map/weight_grad/pallas_call | solution.py:370
  385.9 11.2 %times_rows.4 = bf16[1024,2048]{1,0:T(8,128)(2,1)} custom-call(s32[8]{0:T(128)} %stack.46.places_ref, s32[1]{0:T(128)} %bitcast.core_ref, bf16[1,1024,1024]{2,1,0:T(8,128)(2,1)} %bitcast.110, bf16[512,1024]{1,0:T(8,128)(2,1)} %bitcast.98, bf16[512,1024]{1,0:T(8,128)(2,1)} %copy-done.23, bf16[512,1024]{1,0:T(8,128)(2,1)} %copy-done.22, ...), custom_call_target="tpu_custom_call" | custom-call | flops 4294967296 | tf_op jit(solution)/shard_map/times_rows/pallas_call | solution.py:324
  398.7 19.9 %attend_back.1 = bf16[1024,768]{1,0:T(8,128)(2,1)} custom-call(s32[4]{0:T(128)} %and_select_fusion.2.lo_ref, s32[1,1024]{1,0:T(1,128)} %bitcast.108, bf16[1024,768]{1,0:T(8,128)(2,1)} %get-tuple-element.68.q_ref.k_ref.v_ref, bf16[1024,768]{1,0:T(8,128)(2,1)} %get-tuple-element.68.q_ref.k_ref.v_ref, bf16[1024,768]{1,0:T(8,128)(2,1)} %get-tuple-element.68.q_ref.k_ref.v_ref, ...), custom_call_target="tpu_custom_call" | custom-call | flops 20000000000 | tf_op jit(solution)/shard_map/attend_back/pallas_call | solution.py:555
  418.6 10.0 %times_rows.5 = bf16[1024,2048]{1,0:T(8,128)(2,1)} custom-call(s32[8]{0:T(128)} %stack.46.places_ref, s32[1]{0:T(128)} %bitcast.core_ref, bf16[1,1024,768]{2,1,0:T(8,128)(2,1)} %bitcast.111, bf16[512,768]{1,0:T(8,128)(2,1)} %bitcast.106, bf16[512,768]{1,0:T(8,128)(2,1)} %collective-permute-done.refs_1_, bf16[512,768]{1,0:T(8,128)(2,1)} %collective-permute-done.1.refs_2_, ...), custom_call_target="tpu_custom_call" | custom-call | flops 3221225472 | tf_op jit(solution)/shard_map/times_rows/pallas_call | solution.py:324
  443.1 14.2 %collective-permute-done.20 = bf16[512,1024]{1,0:T(8,128)(2,1)S(1)} collective-permute-done((bf16[512,1024]{1,0:T(8,128)(2,1)}, bf16[512,1024]{1,0:T(8,128)(2,1)S(1)}, u32[]{:S(2)}, u32[]{:S(2)}) %collective-permute-start.20) | collective-permute-done | bytes 1048608 | tf_op jit(solution)/shard_map/ppermute | solution.py:58
  469.3 12.1 %weight_grad.7 = (bf16[512,1024]{1,0:T(8,128)(2,1)}, bf16[512,1024]{1,0:T(8,128)(2,1)}, bf16[1024,1024]{1,0:T(8,128)(2,1)}) custom-call(s32[8]{0:T(128)} %stack.47.order_ref, bf16[1024,2048]{1,0:T(8,128)(2,1)} %get-tuple-element.91.refs_0_, bf16[1024,2048]{1,0:T(8,128)(2,1)} %all-gather.11.cloned.1.call-done.refs_1_, bf16[1,1024,768]{2,1,0:T(8,128)(2,1)} %bitcast.112, ...), custom_call_target="tpu_custom_call" | custom-call | flops 4294967296 | tf_op jit(solution)/shard_map/weight_grad/pallas_call | solution.py:370
  496.2 23.0 %collective-permute-done.26 = bf16[512,1024]{1,0:T(8,128)(2,1)S(1)} collective-permute-done((bf16[512,1024]{1,0:T(8,128)(2,1)}, bf16[512,1024]{1,0:T(8,128)(2,1)S(1)}, u32[]{:S(2)}, u32[]{:S(2)}) %collective-permute-start.26) | collective-permute-done | bytes 1048608 | tf_op jit(solution)/shard_map/ppermute | solution.py:58
  522.0 12.1 %collective-permute-done.28 = bf16[256,1024]{1,0:T(8,128)(2,1)S(1)} collective-permute-done((bf16[256,1024]{1,0:T(8,128)(2,1)S(1)}, bf16[256,1024]{1,0:T(8,128)(2,1)S(1)}, u32[]{:S(2)}, u32[]{:S(2)}) %collective-permute-start.28) | collective-permute-done | bytes 524320 | tf_op jit(solution)/shard_map/ppermute | solution.py:69
  538.1 13.3 %all-to-all-done.7.rows_ref = bf16[8,64,2048]{2,1,0:T(8,128)(2,1)S(1)} async-done(((bf16[8,64,2048]{2,1,0:T(8,128)(2,1)}), bf16[8,64,2048]{2,1,0:T(8,128)(2,1)S(1)}, u32[]{:S(2)}, u32[]{:S(2)}) %all-to-all-start.7) | async-done | bytes 2097184 | tf_op jit(solution)/shard_map/all_to_all | solution.py:717
  572.4 31.7 %all-to-all-done.8.rows_ref = bf16[8,64,1024]{2,1,0:T(8,128)(2,1)S(1)} async-done(((bf16[8,64,1024]{2,1,0:T(8,128)(2,1)}), bf16[8,64,1024]{2,1,0:T(8,128)(2,1)S(1)}, u32[]{:S(2)}, u32[]{:S(2)}) %all-to-all-start.8) | async-done | bytes 1048608 | tf_op jit(solution)/shard_map/all_to_all | solution.py:717
  (218 shorter events, 201.1 us)
Async XLA Ops:
  7.2 90.5 %all-gather.5.cloned.1.call-start = ((), (), s32[]{:S(2)}) async-start(), calls=%async_computation.11 | async-start | bytes 4718592 | tf_op jit(solution)/shard_map/all_gather | solution.py:744
  7.9 227.8 %all-gather.7.cloned.1.call-start = ((), (), s32[]{:S(2)}) async-start(), calls=%async_computation.12 | async-start | bytes 8650752 | tf_op jit(solution)/shard_map/all_gather | solution.py:752
  12.3 46.6 %all-to-all-start = ((bf16[8,64,768]{2,1,0:T(8,128)(2,1)}), bf16[8,64,768]{2,1,0:T(8,128)(2,1)S(1)}, u32[]{:S(2)}, u32[]{:S(2)}) async-start(bf16[8,64,768]{2,1,0:T(8,128)(2,1)} %maximum_bitcast_fusion.1), calls=%async_computation | async-start | bytes 1572864 | tf_op jit(solution)/shard_map/all_to_all | solution.py:124
  58.9 66.1 %all-to-all-start.1 = ((bf16[8,64,2048]{2,1,0:T(8,128)(2,1)}), bf16[8,64,2048]{2,1,0:T(8,128)(2,1)S(1)}, u32[]{:S(2)}, u32[]{:S(2)}) async-start(bf16[8,64,2048]{2,1,0:T(8,128)(2,1)} %maximum_bitcast_fusion), calls=%async_computation.1 | async-start | bytes 4194304 | tf_op jit(solution)/shard_map/all_to_all | solution.py:124
  125.0 45.2 %all-to-all-start.2 = ((bf16[8,64,1024]{2,1,0:T(8,128)(2,1)}), bf16[8,64,1024]{2,1,0:T(8,128)(2,1)S(1)}, u32[]{:S(2)}, u32[]{:S(2)}) async-start(bf16[8,64,1024]{2,1,0:T(8,128)(2,1)} %bitcast.74), calls=%async_computation.2 | async-start | bytes 2097152 | tf_op jit(solution)/shard_map/all_to_all | solution.py:124
  128.5 63.0 %collective-permute-start.6 = (bf16[512,2048]{1,0:T(8,128)(2,1)S(1)}, bf16[512,2048]{1,0:T(8,128)(2,1)}, u32[]{:S(2)}, u32[]{:S(2)}) collective-permute-start(bf16[512,2048]{1,0:T(8,128)(2,1)S(1)} %bitcast.84), channel_id=1, source_target_pairs={{0,16},{8,24},{16,0},{24,8},{1,17},{9,25},{17,1},{25,9},{2,18},{10... | collective-permute-start | bytes 6291464 | tf_op jit(solution)/shard_map/ppermute | solution.py:43
  130.2 64.2 %collective-permute-start.4 = (bf16[512,2048]{1,0:T(8,128)(2,1)S(1)}, bf16[512,2048]{1,0:T(8,128)(2,1)}, u32[]{:S(2)}, u32[]{:S(2)}) collective-permute-start(bf16[512,2048]{1,0:T(8,128)(2,1)S(1)} %bitcast.85), channel_id=1, source_target_pairs={{0,8},{8,0},{16,24},{24,16},{1,9},{9,1},{17,25},{25,17},{2,10},{10... | collective-permute-start | bytes 6291464 | tf_op jit(solution)/shard_map/ppermute | solution.py:42
  170.2 60.9 %all-to-all-start.3 = ((bf16[4,1024,256]{2,1,0:T(8,128)(2,1)}), bf16[4,1024,256]{2,1,0:T(8,128)(2,1)}, u32[]{:S(2)}, u32[]{:S(2)}) async-start(bf16[4,1024,256]{2,1,0:T(8,128)(2,1)} %attend.1), calls=%async_computation.3 | async-start | bytes 4194304 | tf_op jit(solution)/shard_map/all_to_all | solution.py:83
  174.7 102.7 %all-gather.9.cloned.1.call-start = ((), (), s32[]{:S(2)}) async-start(), calls=%async_computation.13 | async-start | bytes 4718592 | tf_op jit(solution)/shard_map/all_gather | solution.py:786
  314.4 52.7 %all-to-all-start.4 = ((bf16[4,128,2048]{2,1,0:T(8,128)(2,1)}), bf16[4,128,2048]{2,1,0:T(8,128)(2,1)S(1)}, u32[]{:S(2)}, u32[]{:S(2)}) async-start(bf16[4,128,2048]{2,1,0:T(8,128)(2,1)} %fusion), calls=%async_computation.4 | async-start | bytes 4194304 | tf_op jit(solution)/shard_map/all_to_all | solution.py:103
  332.2 29.4 %collective-permute-start.15 = (bf16[512,1024]{1,0:T(8,128)(2,1)}, bf16[512,1024]{1,0:T(8,128)(2,1)S(1)}, u32[]{:S(2)}, u32[]{:S(2)}) collective-permute-start(bf16[512,1024]{1,0:T(8,128)(2,1)} %get-tuple-element.84), channel_id=1, source_target_pairs={{0,16},{8,24},{16,0},{24,8},{1,17},{9,25},{17,1},{25,9},{2,18},{10... | collective-permute-start | bytes 3145736 | tf_op jit(solution)/shard_map/ppermute | solution.py:59
  333.7 28.8 %collective-permute-start.14 = (bf16[512,1024]{1,0:T(8,128)(2,1)}, bf16[512,1024]{1,0:T(8,128)(2,1)}, u32[]{:S(2)}, u32[]{:S(2)}) collective-permute-start(bf16[512,1024]{1,0:T(8,128)(2,1)} %get-tuple-element.83), channel_id=1, source_target_pairs={{0,8},{8,0},{16,24},{24,16},{1,9},{9,1},{17,25},{25,17},{2,10},{10... | collective-permute-start | bytes 3145736 | tf_op jit(solution)/shard_map/ppermute | solution.py:58
  349.1 48.1 %collective-permute-start.18 = (bf16[512,1024]{1,0:T(8,128)(2,1)}, bf16[512,1024]{1,0:T(8,128)(2,1)}, u32[]{:S(2)}, u32[]{:S(2)}) collective-permute-start(bf16[512,1024]{1,0:T(8,128)(2,1)} %get-tuple-element.86), channel_id=1, source_target_pairs={{0,8},{8,0},{16,24},{24,16},{1,9},{9,1},{17,25},{25,17},{2,10},{10... | collective-permute-start | bytes 3145736 | tf_op jit(solution)/shard_map/ppermute | solution.py:58
  349.7 47.5 %collective-permute-start.19 = (bf16[512,1024]{1,0:T(8,128)(2,1)}, bf16[512,1024]{1,0:T(8,128)(2,1)}, u32[]{:S(2)}, u32[]{:S(2)}) collective-permute-start(bf16[512,1024]{1,0:T(8,128)(2,1)} %get-tuple-element.95), channel_id=1, source_target_pairs={{0,16},{8,24},{16,0},{24,8},{1,17},{9,25},{17,1},{25,9},{2,18},{10... | collective-permute-start | bytes 3145736 | tf_op jit(solution)/shard_map/ppermute | solution.py:59
  380.3 89.0 %all-gather.11.cloned.1.call-start = ((), (), s32[]{:S(2)}) async-start(), calls=%async_computation.14 | async-start | bytes 4718592 | tf_op jit(solution)/shard_map/all_gather | solution.py:819
  398.7 172.4 %reduce-scatter.5.cloned.1.call-start = ((), (), s32[]{:S(2)}) async-start(), calls=%async_computation.16 | async-start | bytes 4718592 | tf_op jit(solution)/shard_map/reduce_scatter | solution.py:829
  431.4 26.4 %collective-permute-start.21 = (bf16[512,1024]{1,0:T(8,128)(2,1)}, bf16[512,1024]{1,0:T(8,128)(2,1)}, u32[]{:S(2)}, u32[]{:S(2)}) collective-permute-start(bf16[512,1024]{1,0:T(8,128)(2,1)} %get-tuple-element.100), channel_id=1, source_target_pairs={{0,16},{8,24},{16,0},{24,8},{1,17},{9,25},{17,1},{25,9},{2,18},{10... | collective-permute-start | bytes 3145736 | tf_op jit(solution)/shard_map/ppermute | solution.py:59
  434.0 47.4 %all-to-all-start.6 = ((bf16[8,64,1024]{2,1,0:T(8,128)(2,1)}), bf16[8,64,1024]{2,1,0:T(8,128)(2,1)S(1)}, u32[]{:S(2)}, u32[]{:S(2)}) async-start(bf16[8,64,1024]{2,1,0:T(8,128)(2,1)} %bitcast.25), calls=%async_computation.6 | async-start | bytes 2097152 | tf_op jit(solution)/shard_map/all_to_all | solution.py:717
  438.8 170.7 %reduce-scatter.3.cloned.1.call-start = ((), (), s32[]{:S(2)}) async-start(), calls=%async_computation.15 | async-start | bytes 4718592 | tf_op jit(solution)/shard_map/reduce_scatter | solution.py:839
  440.9 27.6 %collective-permute-start.23 = (bf16[256,1024]{1,0:T(8,128)(2,1)S(1)}, bf16[256,1024]{1,0:T(8,128)(2,1)S(1)}, u32[]{:S(2)}, u32[]{:S(2)}) collective-permute-start(bf16[256,1024]{1,0:T(8,128)(2,1)S(1)} %get-tuple-element.139), channel_id=1, source_target_pairs={{0,8},{8,0},{16,24},{24,16},{1,9},{9,1},{17,25},{25,17},{2,10},{10... | collective-permute-start | bytes 1572872 | tf_op jit(solution)/shard_map/ppermute | solution.py:70
  442.5 26.8 %collective-permute-start.22 = (bf16[256,1024]{1,0:T(8,128)(2,1)S(1)}, bf16[256,1024]{1,0:T(8,128)(2,1)}, u32[]{:S(2)}, u32[]{:S(2)}) collective-permute-start(bf16[256,1024]{1,0:T(8,128)(2,1)S(1)} %get-tuple-element.140), channel_id=1, source_target_pairs={{0,16},{8,24},{16,0},{24,8},{1,17},{9,25},{17,1},{25,9},{2,18},{10... | collective-permute-start | bytes 1572872 | tf_op jit(solution)/shard_map/ppermute | solution.py:69
  488.6 62.7 %all-to-all-start.7 = ((bf16[8,64,2048]{2,1,0:T(8,128)(2,1)}), bf16[8,64,2048]{2,1,0:T(8,128)(2,1)S(1)}, u32[]{:S(2)}, u32[]{:S(2)}) async-start(bf16[8,64,2048]{2,1,0:T(8,128)(2,1)} %bitcast.77), calls=%async_computation.8 | async-start | bytes 4194304 | tf_op jit(solution)/shard_map/all_to_all | solution.py:717
  494.8 27.2 %collective-permute-start.27 = (bf16[512,1024]{1,0:T(8,128)(2,1)}, bf16[512,1024]{1,0:T(8,128)(2,1)S(1)}, u32[]{:S(2)}, u32[]{:S(2)}) collective-permute-start(bf16[512,1024]{1,0:T(8,128)(2,1)} %get-tuple-element.110), channel_id=1, source_target_pairs={{0,16},{8,24},{16,0},{24,8},{1,17},{9,25},{17,1},{25,9},{2,18},{10... | collective-permute-start | bytes 3145736 | tf_op jit(solution)/shard_map/ppermute | solution.py:59
  554.9 49.3 %all-to-all-start.8 = ((bf16[8,64,1024]{2,1,0:T(8,128)(2,1)}), bf16[8,64,1024]{2,1,0:T(8,128)(2,1)S(1)}, u32[]{:S(2)}, u32[]{:S(2)}) async-start(bf16[8,64,1024]{2,1,0:T(8,128)(2,1)} %bitcast.78), calls=%async_computation.10 | async-start | bytes 2097152 | tf_op jit(solution)/shard_map/all_to_all | solution.py:717
  (54 other events, 725.8 us)
Sparse Core Ops, SparseCore 0:
  9.6 77.7 all-gather.4
  90.4 113.8 all-gather.6
  231.3 46.0 all-gather.8
  398.8 49.2 all-gather.10
  450.2 59.5 reduce-scatter.4
  512.0 96.1 reduce-scatter.2

commit v5 on v4

--- a/solution.py
+++ b/solution.py
@@ -13,6 +13,7 @@
 ROPE_BASE = 130000.0
 BLOCK = 256
 UNIT = 256
+CHUNK = 512
 VMEM_LIMIT = 56 * 1024 * 1024
 GIGA = 1000 * 1000 * 1000
 LOW = jnp.bfloat16
@@ -205,12 +206,14 @@
     gate_ref, up_ref, hidden_ref, w_gate_ref, w_up_ref = refs[2 * count :]
     gather_units(places_ref, gate_pieces, w_gate_ref)
     gather_units(places_ref, up_pieces, w_up_ref)
-    left = left_ref[...]
-    gate = dot(left, w_gate_ref[...], 1, 0)
-    gate_ref[...] = gate
-    up = dot(left, w_up_ref[...], 1, 0)
-    up_ref[...] = up
-    hidden_ref[...] = (gate * jax.nn.sigmoid(gate) * up).astype(LOW)
+    for first in range(0, left_ref.shape[0], CHUNK):
+        rows = slice(first, first + CHUNK)
+        left = left_ref[rows, :]
+        gate = dot(left, w_gate_ref[...], 1, 0)
+        gate_ref[rows, :] = gate
+        up = dot(left, w_up_ref[...], 1, 0)
+        up_ref[rows, :] = up
+        hidden_ref[rows, :] = (gate * jax.nn.sigmoid(gate) * up).astype(LOW)
 
 
 def open_units(places, left, pieces):
@@ -244,12 +247,14 @@
     pieces = refs[:count]
     out_ref, w_ref = refs[count:]
     gather_units(places_ref, pieces, w_ref)
-    d_hidden = dot(back_ref[...], w_ref[...], 1, 0)
-    gate = gate_ref[...]
-    sigmoid = jax.nn.sigmoid(gate)
-    scaled = d_hidden * sigmoid
-    out_ref[0] = (scaled * up_ref[...] * (1.0 + gate * (1.0 - sigmoid))).astype(LOW)
-    out_ref[1] = (scaled * gate).astype(LOW)
+    for first in range(0, back_ref.shape[0], CHUNK):
+        rows = slice(first, first + CHUNK)
+        d_hidden = dot(back_ref[rows, :], w_ref[...], 1, 0)
+        gate = gate_ref[rows, :]
+        sigmoid = jax.nn.sigmoid(gate)
+        scaled = d_hidden * sigmoid
+        out_ref[0, rows, :] = (scaled * up_ref[rows, :] * (1.0 + gate * (1.0 - sigmoid))).astype(LOW)
+        out_ref[1, rows, :] = (scaled * gate).astype(LOW)
 
 
 def close_units(places, back, gate, up, pieces):
@@ -342,15 +347,15 @@
 def weight_grad_kernel(outs, pairs, order_ref, *refs):
     step = pl.program_id(0)
     values = []
-    for left_ref, right_ref in zip(refs[:pairs], refs[pairs : 2 * pairs]):
-        left = left_ref[...]
+    for index, right_ref in enumerate(refs[2 * pairs : 3 * pairs]):
+        left = jnp.concatenate([refs[2 * index][...], refs[2 * index + 1][...]], axis=1)
         for part in range(right_ref.shape[0]):
             values.append(dot(left, right_ref[part], 0, 0).astype(LOW))
     value = values[0] if len(values) == 1 else jnp.concatenate(values, axis=1)
     first = 0
-    for ref, units in zip(refs[2 * pairs :], outs):
-
-        @pl.when((step >= first) & (step < first + units))
+    for ref, units in zip(refs[3 * pairs :], outs):
+
+        @pl.when((step >= first // 2) & (step < (first + units) // 2))
         def _():
             ref[...] = value
 
@@ -365,14 +370,20 @@
     firsts = [sum(outs[:index]) for index in range(len(outs))]
 
     def spec(first, held):
-        return pl.BlockSpec((UNIT, wide), lambda s, p: (jnp.clip(s - first, 0, held - 1), 0))
+        return pl.BlockSpec(
+            (2 * UNIT, wide), lambda s, p: (jnp.clip(s - first // 2, 0, held // 2 - 1), 0)
+        )
 
     return pl.pallas_call(
         functools.partial(weight_grad_kernel, outs, len(pairs)),
         grid_spec=pltpu.PrefetchScalarGridSpec(
             num_scalar_prefetch=1,
-            grid=(features // UNIT,),
-            in_specs=[pl.BlockSpec((count, UNIT), lambda s, p: (0, p[s]))] * len(pairs)
+            grid=(features // (2 * UNIT),),
+            in_specs=[
+                pl.BlockSpec((count, UNIT), lambda s, p: (0, p[2 * s])),
+                pl.BlockSpec((count, UNIT), lambda s, p: (0, p[2 * s + 1])),
+            ]
+            * len(pairs)
             + [pl.BlockSpec(right.shape, lambda s, p: (0, 0, 0)) for right in rights],
             out_specs=[spec(first, held) for first, held in zip(firsts, outs)],
         ),
@@ -382,7 +393,7 @@
             flops=2 * count * wide * features, bytes_accessed=0, transcendentals=0
         ),
         name="weight_grad",
-    )(order, *lefts, *rights)
+    )(order, *[left for left in lefts for unused in range(2)], *rights)
 
 
 def masked_scores(key, query, key_block, query_block, starts):
@@ -581,7 +592,7 @@
     )(lows, starts, qkv, qkv, qkv, back, cos, sin)
 
 
-def blend_kernel(core_ref, x_ref, own_ref, other_ref, w_ref, unit_ref, mixed_ref):
+def blend_kernel(core_ref, x_ref, own_ref, other_ref, w_ref, unit_ref, mixed_ref, attended_ref):
     core = core_ref[0]
     pieces = []
     for chip in range(own_ref.shape[0]):
@@ -589,6 +600,7 @@
         pieces.append(jnp.where(core == 0, own, other))
         pieces.append(jnp.where(core == 0, other, own))
     attended = jnp.concatenate(pieces, axis=1)
+    attended_ref[...] = attended
     mixed = x_ref[...].astype(F32) + dot(attended, w_ref[...], 1, 1)
     mixed_ref[...] = mixed
     inverse = lax.rsqrt(jnp.mean(mixed * mixed, axis=-1, keepdims=True) + EPSILON)
@@ -612,11 +624,13 @@
             out_specs=[
                 pl.BlockSpec((BLOCK, features), lambda i, core: (i, 0)),
                 pl.BlockSpec((BLOCK, features), lambda i, core: (i, 0)),
+                pl.BlockSpec((BLOCK, features), lambda i, core: (i, 0)),
             ],
         ),
         out_shape=[
             jax.ShapeDtypeStruct((count, features), LOW),
             jax.ShapeDtypeStruct((count, features), F32),
+            jax.ShapeDtypeStruct((count, features), LOW),
         ],
         compiler_params=pltpu.CompilerParams(vmem_limit_bytes=VMEM_LIMIT),
         cost_estimate=pl.CostEstimate(flops=15 * GIGA, bytes_accessed=0, transcendentals=0),
@@ -681,7 +695,7 @@
     w_down,
 ):
     rows, features = tokens.shape
-    n_c = lax.axis_size("ctx")
+    n_c, n_f = lax.axis_size("ctx"), lax.axis_size("fsdp")
     group = rows * n_c
     width = features // n_c
     here = lax.axis_index("ctx") * rows
@@ -785,7 +799,7 @@
     attended_mine = after(attended_mine, *two_far)
     back_all = lax.all_gather(after(cotangent, attended_mine), "ctx", axis=0, tiled=True)
     attended_other = other_core(attended_mine)
-    unit_mlp, mixed = blend(core, x_all, attended_mine, attended_other, out_all)
+    unit_mlp, mixed, attended_all = blend(core, x_all, attended_mine, attended_other, out_all)
     col_two = pulled(two_rows, two_near, two_far)
     down_near = tuple(after(piece, unit_mlp) for piece in down_near)
     down_far = pull_far(down_near)
@@ -809,14 +823,21 @@
     )
     d_mixed_low = d_mixed.astype(LOW)
     d_att = dot(d_mixed_low, out_all, 1, 0).astype(LOW)
-    gate_landed = push_near(part_gate)
     branch = times_rows(places, core, after(hidden, d_att)[None], col_down)
     down_landed = tuple(after(piece, d_att) for piece in down_landed)
-    d_att_own = lax.all_to_all(d_att, "ctx", split_axis=1, concat_axis=0, tiled=True)
+    owners = jnp.swapaxes(d_mixed_low.reshape(rows, n_f, n_c, share), 1, 2)
+    both_ways = jnp.concatenate(
+        [d_att.reshape(rows, n_c, width), owners.reshape(rows, n_c, n_f * share)], axis=2
+    ).reshape(rows, -1)
+    d_att_own = lax.all_to_all(both_ways, "ctx", split_axis=1, concat_axis=0, tiled=True)
     down_last = push_far(part_down, down_landed)
+    part_gate = [after(part, *down_last) for part in part_gate]
+    gate_landed = push_near(part_gate)
     gate_last = push_far(part_gate, gate_landed)
-    d_att_own = after(d_att_own, branch, *down_last, *gate_landed)
-    d_mixed_all = lax.all_gather(after(d_mixed_low, d_att_own), "ctx", axis=0, tiled=True)
+    d_att_own = after(d_att_own, branch, *down_last)
+    branch_own = lax.psum_scatter(
+        after(branch, d_att_own), "ctx", scatter_dimension=0, tiled=True
+    )
     part_up = [after(part_up[0], d_att_own)] + list(part_up[1:])
     if square:
         part_up[1] = after(part_up[1], d_att_own)
@@ -826,23 +847,30 @@
 
     d_qkv = attend_back(lows, starts_row, qkv, d_att_own, cos, sin)
     first_part = times_rows(places, core, d_qkv[None], w_qkv)
+    first_part = after(first_part, rows_down, *gate_landed, *up_landed)
     d_first = lax.psum_scatter(first_part, "ctx", scatter_dimension=0, tiled=True).astype(F32)
     part_qkv = weight_grad(
-        order, outs, (unit, after(d_qkv, first_part, *up_landed, *gate_last)[None]), (d_mixed_all, attended[:1])
-    )
-    part_qkv = [after(part, rows_down, *up_last) for part in part_qkv]
+        order, outs, (unit, after(d_qkv, first_part)[None])
+    )
+    part_out = dot(after(d_att_own, part_qkv[0])[:, width:], attended_all, 0, 0).astype(LOW)
+    if square:
+        part_out = part_out.reshape(n_f, share, features)
+        terms = [lax.dynamic_index_in_dim(part_out, me ^ bits, 0, False) for bits in range(4)]
+        for bits in range(1, 4):
+            terms[bits] = lax.ppermute(terms[bits], "fsdp", flip("fsdp", 4, bits))
+        grad_out = sum(term.astype(F32) for term in terms)
+    else:
+        grad_out = lax.psum_scatter(part_out, "fsdp", scatter_dimension=0, tiled=True).astype(F32)
+    part_qkv = [after(part, *up_last, *gate_last) for part in part_qkv]
     qkv_landed = push_near(part_qkv)
     two_mine = jnp.concatenate(
         [pushed(part_gate, gate_landed, gate_last), pushed(part_up, up_landed, up_last)], axis=1
     )
-    rows_two = after(to_rows(after(two_mine, rows_down)), *qkv_landed)
-    branch_own = lax.psum_scatter(
-        after(branch, part_qkv[0]), "ctx", scatter_dimension=0, tiled=True
-    ).astype(F32)
+    rows_two = after(to_rows(after(two_mine, rows_down)), grad_out, *qkv_landed)
     qkv_last = push_far(part_qkv, qkv_landed)
     rows_qkv = to_rows(after(pushed(part_qkv, qkv_landed, qkv_last), rows_two))
 
-    layer_out = (mixed_own + after(branch_own, rows_two)).astype(LOW)
+    layer_out = (mixed_own + after(branch_own, rows_two).astype(F32)).astype(LOW)
     x_own = tokens.astype(F32)
     inverse = lax.rsqrt(jnp.mean(x_own * x_own, axis=-1, keepdims=True) + EPSILON)
     first_own = x_own * inverse
@@ -852,8 +880,8 @@
 
     (grad_down,), unused = finish(rows_down, gain_m, (), 1)
     (grad_gate, grad_up), grad_gain_mlp = finish(rows_two, gain_m, (w_gate, w_up), 2)
-    (grad_query, grad_key, grad_value, grad_out), grad_gain_attn = finish(
-        rows_qkv, gain_a, (w_query, w_key, w_value), 4
+    (grad_query, grad_key, grad_value), grad_gain_attn = finish(
+        rows_qkv, gain_a, (w_query, w_key, w_value), 3
     )
     return (
         layer_out,

time: 633 us -> 625 us (0.987)
  Pallas kernels: 182 us -> 174 us
    ppermute x3, waiting for transfers between devices: 37.7 us -> 3.7 us  [near(): lax.ppermute(block, 'fsdp', flip('fsdp', 4, 2))]
    ppermute x3, waiting for transfers between devices: 1.2 us -> 32.6 us  [near(): lax.ppermute(block, 'fsdp', flip('fsdp', 4, 1))]
    all_to_all x3, waiting for transfers between devices: 45 us -> 19.1 us  [to_rows(): return lax.all_to_all(value, 'ctx', split_axis=0, concat_axis=0, tiled=True)]
    ppermute x4, waiting for transfers between devices: 37.2 us -> 18.9 us  [reduce_near(): lax.ppermute(part[0], 'fsdp', flip('fsdp', 4, 1))]
    ppermute x3, waiting for transfers between devices: 20 us -> 3.43 us  [far(): lax.ppermute(from_y[half:], 'fsdp', flip('fsdp', 4, 1))]
    ppermute x3, waiting for transfers between devices: 3.83 us -> 20.2 us  [far(): lax.ppermute(from_x[:half], 'fsdp', flip('fsdp', 4, 2))]
    ppermute x4, waiting for transfers between devices: 3.64 us -> 14.3 us  [reduce_far(): lax.ppermute(send_x, 'fsdp', flip('fsdp', 4, 1))]
    ppermute x4, waiting for transfers between devices: 13.3 us -> 23.5 us  [reduce_far(): lax.ppermute(send_y, 'fsdp', flip('fsdp', 4, 2))]
  transfers between devices with their start and end apart: 45 -> 47, of which waited for: 24 -> 30; matrix products, arithmetic and copies ran while one was open for 10% -> 9% of each run, Pallas kernels for 25% -> 24%
where the time goes in v5:
time: 625 us; the launch traced here: 617 us
  waiting for transfers between devices  268 us (43%)
  Pallas kernels  174 us (28%)
  starting transfers between devices  81.7 us (13%)
  other arithmetic  45.8 us (7%)
  local copies, waits for them, and re-layouts  24.1 us (4%)
  between operations  14.5 us (2%)
  matrix products  8.26 us (1%)
    all_to_all x3, waiting for transfers between devices, to_columns(): landed = lax.all_to_all(pieces, 'ctx', 0, 0, tiled=True)  82.1 us
    pallas_call x4, Pallas kernels, weight_grad(): pl.pallas_call(functools.partial(weight_grad_kernel, outs, len(pairs)), g...  38.9 us
    pallas_call x3, Pallas kernels, times_rows(): pl.pallas_call(functools.partial(times_rows_kernel, units, chips), grid_s...  37.5 us
    ppermute x3, waiting for transfers between devices, near(): lax.ppermute(block, 'fsdp', flip('fsdp', 4, 1))  32.6 us
    ppermute x4, waiting for transfers between devices, reduce_far(): lax.ppermute(send_y, 'fsdp', flip('fsdp', 4, 2))  23.5 us
    ppermute x3, waiting for transfers between devices, far(): lax.ppermute(from_x[:half], 'fsdp', flip('fsdp', 4, 2))  20.2 us
    pallas_call x1, Pallas kernels, attend_back(): pl.pallas_call(functools.partial(attend_back_kernel, heads), grid_spec=pl...  19.9 us
    all_to_all x3, waiting for transfers between devices, to_rows(): return lax.all_to_all(value, 'ctx', split_axis=0, concat_axis=0, tiled=True)  19.1 us
  transfers between devices with their start and end apart: 47, of which 30 were waited for; matrix products, arithmetic and copies ran while one was open for 9% of the time, Pallas kernels for 24%

profile of v5, /device:TPU:0, one launch (start us, length us, event | category | flops | bytes accessed | tf_op | source)
XLA Modules:
  0.0 616.8 jit_solution(18008038162312950663)
XLA Ops:
  21.2 37.6 %all-to-all-done = bf16[8,64,768]{2,1,0:T(8,128)(2,1)S(1)} async-done(((bf16[8,64,768]{2,1,0:T(8,128)(2,1)}), bf16[8,64,768]{2,1,0:T(8,128)(2,1)S(1)}, u32[]{:S(2)}, u32[]{:S(2)}) %all-to-all-start) | async-done | bytes 786464 | tf_op jit(solution)/shard_map/all_to_all | solution.py:125
  66.8 16.6 %collective-permute-done.refs_1_ = bf16[512,768]{1,0:T(8,128)(2,1)} collective-permute-done((bf16[512,768]{1,0:T(8,128)(2,1)S(1)}, bf16[512,768]{1,0:T(8,128)(2,1)}, u32[]{:S(2)}, u32[]{:S(2)}) %collective-permute-start) | collective-permute-done | bytes 786464 | tf_op jit(solution)/shard_map/ppermute | solution.py:43
  98.3 10.2 %project.1 = (bf16[1024,2048]{1,0:T(8,128)(2,1)}, bf16[1024,768]{1,0:T(8,128)(2,1)}) custom-call(s32[8]{0:T(128)} %stack.46.places_ref, bf16[1024,2048]{1,0:T(8,128)(2,1)} %all-gather.4.cloned.1.call-done.x_ref, f32[1024,256]{1,0:T(8,128)} %bitcast.106, f32[1024,256]{1,0:T(8,128)} %bitcast.104, bf16[512,768]{1,0:T(8,128)(2,1)} %bitcast.122, ...), custom_call_target="tpu_custom_call" | custom-call | flops 8999999488 | tf_op jit(solution)/shard_map/project/pallas_call | solution.py:177
  108.6 10.6 %attend.1 = bf16[4,1024,256]{2,1,0:T(8,128)(2,1)} custom-call(s32[4]{0:T(128)} %and_select_fusion.2.lo_ref, s32[1,1024]{1,0:T(1,128)} %bitcast.124, bf16[1024,768]{1,0:T(8,128)(2,1)} %get-tuple-element.72.q_ref.k_ref.v_ref, bf16[1024,768]{1,0:T(8,128)(2,1)} %get-tuple-element.72.q_ref.k_ref.v_ref, bf16[1024,768]{1,0:T(8,128)(2,1)} %get-tuple-element.72.q_ref.k_ref.v_ref), custom_call_target="tpu_custom_call" | custom-call | flops 10000000000 | tf_op jit(solution)/shard_map/attend/pallas_call | solution.py:450
  131.5 39.2 %all-to-all-done.2 = bf16[8,64,1024]{2,1,0:T(8,128)(2,1)S(1)} async-done(((bf16[8,64,1024]{2,1,0:T(8,128)(2,1)}), bf16[8,64,1024]{2,1,0:T(8,128)(2,1)S(1)}, u32[]{:S(2)}, u32[]{:S(2)}) %all-to-all-start.2) | async-done | bytes 1048608 | tf_op jit(solution)/shard_map/all_to_all | solution.py:125
  175.3 16.0 %collective-permute-done.4.refs_1_.refs_6_ = bf16[512,2048]{1,0:T(8,128)(2,1)} collective-permute-done((bf16[512,2048]{1,0:T(8,128)(2,1)S(1)}, bf16[512,2048]{1,0:T(8,128)(2,1)}, u32[]{:S(2)}, u32[]{:S(2)}) %collective-permute-start.4) | collective-permute-done | bytes 2097184 | tf_op jit(solution)/shard_map/ppermute | solution.py:43
  197.2 20.2 %collective-permute-done.5.refs_3_.refs_8_ = bf16[256,2048]{1,0:T(8,128)(2,1)S(1)} collective-permute-done((bf16[256,2048]{1,0:T(8,128)(2,1)S(1)}, bf16[256,2048]{1,0:T(8,128)(2,1)S(1)}, u32[]{:S(2)}, u32[]{:S(2)}) %collective-permute-start.5) | collective-permute-done | bytes 1048608 | tf_op jit(solution)/shard_map/ppermute | solution.py:52
  219.9 10.8 %all-to-all-done.3.own_ref = bf16[4,1024,256]{2,1,0:T(8,128)(2,1)} async-done(((bf16[4,1024,256]{2,1,0:T(8,128)(2,1)}), bf16[4,1024,256]{2,1,0:T(8,128)(2,1)}, u32[]{:S(2)}, u32[]{:S(2)}) %all-to-all-start.3) | async-done | bytes 2097184 | tf_op jit(solution)/shard_map/all_to_all | solution.py:84
  235.3 17.4 %blend.1 = (bf16[1024,2048]{1,0:T(8,128)(2,1)}, f32[1024,2048]{1,0:T(8,128)}, bf16[1024,2048]{1,0:T(8,128)(2,1)}) custom-call(s32[1]{0:T(128)} %bitcast.core_ref, bf16[1024,2048]{1,0:T(8,128)(2,1)} %all-gather.4.cloned.1.call-done.x_ref, bf16[4,1024,256]{2,1,0:T(8,128)(2,1)} %all-to-all-done.3.own_ref, ...), custom_call_target="tpu_custom_call" | custom-call | flops 15000000512 | tf_op jit(solution)/shard_map/blend/pallas_call | solution.py:613
  260.1 15.6 %open_units.1 = (f32[1024,1024]{1,0:T(8,128)}, f32[1024,1024]{1,0:T(8,128)}, bf16[1024,1024]{1,0:T(8,128)(2,1)}) custom-call(s32[8]{0:T(128)} %stack.46.places_ref, bf16[1024,2048]{1,0:T(8,128)(2,1)} %get-tuple-element.91.left_ref.refs_0_.refs_1_, bf16[512,2048]{1,0:T(8,128)(2,1)} %bitcast.97, bf16[512,2048]{1,0:T(8,128)(2,1)} %collective-permute-done.4.refs_1_.refs_6_, ...), custom_call_target="tpu_custom_call" | custom-call | flops 12000000000 | tf_op jit(solution)/shard_map/open_units/pallas_call | solution.py:224
  277.7 12.7 %close_units.1.left_ref = bf16[2,1024,1024]{2,1,0:T(8,128)(2,1)} custom-call(s32[8]{0:T(128)} %stack.46.places_ref, bf16[1024,2048]{1,0:T(8,128)(2,1)} %all-gather.8.cloned.1.call-done.back_ref.refs_0_.refs_1_, f32[1024,1024]{1,0:T(8,128)} %get-tuple-element.81.gate_ref, f32[1024,1024]{1,0:T(8,128)} %get-tuple-element.82.up_ref, ...), custom_call_target="tpu_custom_call" | custom-call | flops 7000000000 | tf_op jit(solution)/shard_map/close_units/pallas_call | solution.py:264
  290.4 16.3 %times_rows.3 = bf16[2,4,128,2048]{3,2,1,0:T(8,128)(2,1)} custom-call(s32[8]{0:T(128)} %stack.46.places_ref, s32[1]{0:T(128)} %bitcast.core_ref, bf16[2,1024,1024]{2,1,0:T(8,128)(2,1)} %close_units.1.left_ref, bf16[512,2048]{1,0:T(8,128)(2,1)} %bitcast.99, bf16[512,2048]{1,0:T(8,128)(2,1)} %collective-permute-done.4.refs_1_.refs_6_, ...), custom_call_target="tpu_custom_call" | custom-call | flops 8589934592 | tf_op jit(solution)/shard_map/times_rows/pallas_call | solution.py:329
  321.0 10.5 %weight_grad.4 = (bf16[512,1024]{1,0:T(8,128)(2,1)}, bf16[512,1024]{1,0:T(8,128)(2,1)}, bf16[1024,1024]{1,0:T(8,128)(2,1)}) custom-call(s32[8]{0:T(128)} %stack.47.order_ref, bf16[1024,2048]{1,0:T(8,128)(2,1)} %all-gather.8.cloned.1.call-done.back_ref.refs_0_.refs_1_, bf16[1024,2048]{1,0:T(8,128)(2,1)} %all-gather.8.cloned.1.call-done.back_ref.refs_0_.refs_1_, ...), custom_call_target="tpu_custom_call" | custom-call | flops 4294967296 | tf_op jit(solution)/shard_map/weight_grad/pallas_call | solution.py:377
  336.8 10.0 %weight_grad.5 = (bf16[512,1024]{1,0:T(8,128)(2,1)}, bf16[512,1024]{1,0:T(8,128)(2,1)}, bf16[1024,1024]{1,0:T(8,128)(2,1)}) custom-call(s32[8]{0:T(128)} %stack.47.order_ref, bf16[1024,2048]{1,0:T(8,128)(2,1)} %get-tuple-element.91.left_ref.refs_0_.refs_1_, bf16[1024,2048]{1,0:T(8,128)(2,1)} %get-tuple-element.91.left_ref.refs_0_.refs_1_, ...), custom_call_target="tpu_custom_call" | custom-call | flops 4294967296 | tf_op jit(solution)/shard_map/weight_grad/pallas_call | solution.py:377
  346.8 10.0 %weight_grad.6 = (bf16[512,1024]{1,0:T(8,128)(2,1)}, bf16[512,1024]{1,0:T(8,128)(2,1)}, bf16[1024,1024]{1,0:T(8,128)(2,1)}) custom-call(s32[8]{0:T(128)} %stack.47.order_ref, bf16[1024,2048]{1,0:T(8,128)(2,1)} %get-tuple-element.91.left_ref.refs_0_.refs_1_, bf16[1024,2048]{1,0:T(8,128)(2,1)} %get-tuple-element.91.left_ref.refs_0_.refs_1_, ...), custom_call_target="tpu_custom_call" | custom-call | flops 4294967296 | tf_op jit(solution)/shard_map/weight_grad/pallas_call | solution.py:377
  358.3 9.5 %all-to-all-done.4 = bf16[4,128,2048]{2,1,0:T(8,128)(2,1)S(1)} async-done(((bf16[4,128,2048]{2,1,0:T(8,128)(2,1)}), bf16[4,128,2048]{2,1,0:T(8,128)(2,1)S(1)}, u32[]{:S(2)}, u32[]{:S(2)}) %all-to-all-start.4) | async-done | bytes 2097184 | tf_op jit(solution)/shard_map/all_to_all | solution.py:104
  386.8 11.2 %times_rows.4 = bf16[1024,2048]{1,0:T(8,128)(2,1)} custom-call(s32[8]{0:T(128)} %stack.46.places_ref, s32[1]{0:T(128)} %bitcast.core_ref, bf16[1,1024,1024]{2,1,0:T(8,128)(2,1)} %bitcast.127, bf16[512,1024]{1,0:T(8,128)(2,1)} %bitcast.111, bf16[512,1024]{1,0:T(8,128)(2,1)} %copy-done.22, bf16[512,1024]{1,0:T(8,128)(2,1)} %copy-done.21, ...), custom_call_target="tpu_custom_call" | custom-call | flops 4294967296 | tf_op jit(solution)/shard_map/times_rows/pallas_call | solution.py:329
  398.0 9.6 %all-to-all-done.5 = bf16[128,8,512]{0,2,1:T(8,128)(2,1)S(1)} async-done(((bf16[128,8,512]{0,2,1:T(8,128)(2,1)}), bf16[128,8,512]{0,2,1:T(8,128)(2,1)S(1)}, u32[]{:S(2)}, u32[]{:S(2)}) %all-to-all-start.5) | async-done | bytes 1048608 | tf_op jit(solution)/shard_map/all_to_all | solution.py:832
  421.9 19.9 %attend_back.1 = bf16[1024,768]{1,0:T(8,128)(2,1)} custom-call(s32[4]{0:T(128)} %and_select_fusion.2.lo_ref, s32[1,1024]{1,0:T(1,128)} %bitcast.125, bf16[1024,768]{1,0:T(8,128)(2,1)} %get-tuple-element.72.q_ref.k_ref.v_ref, bf16[1024,768]{1,0:T(8,128)(2,1)} %get-tuple-element.72.q_ref.k_ref.v_ref, bf16[1024,768]{1,0:T(8,128)(2,1)} %get-tuple-element.72.q_ref.k_ref.v_ref, ...), custom_call_target="tpu_custom_call" | custom-call | flops 20000000000 | tf_op jit(solution)/shard_map/attend_back/pallas_call | solution.py:566
  441.7 10.0 %times_rows.5 = bf16[1024,2048]{1,0:T(8,128)(2,1)} custom-call(s32[8]{0:T(128)} %stack.46.places_ref, s32[1]{0:T(128)} %bitcast.core_ref, bf16[1,1024,768]{2,1,0:T(8,128)(2,1)} %bitcast.128, bf16[512,768]{1,0:T(8,128)(2,1)} %bitcast.123, bf16[512,768]{1,0:T(8,128)(2,1)} %collective-permute-done.refs_1_, bf16[512,768]{1,0:T(8,128)(2,1)} %collective-permute-done.1.refs_2_, ...), custom_call_target="tpu_custom_call" | custom-call | flops 3221225472 | tf_op jit(solution)/shard_map/times_rows/pallas_call | solution.py:329
  471.7 11.5 %collective-permute-done.19 = bf16[256,1024]{1,0:T(8,128)(2,1)S(1)} collective-permute-done((bf16[256,1024]{1,0:T(8,128)(2,1)S(1)}, bf16[256,1024]{1,0:T(8,128)(2,1)S(1)}, u32[]{:S(2)}, u32[]{:S(2)}) %collective-permute-start.19) | collective-permute-done | bytes 524320 | tf_op jit(solution)/shard_map/ppermute | solution.py:70
  498.0 9.8 %collective-permute-done.25 = bf16[256,1024]{1,0:T(8,128)(2,1)S(1)} collective-permute-done((bf16[256,1024]{1,0:T(8,128)(2,1)S(1)}, bf16[256,1024]{1,0:T(8,128)(2,1)S(1)}, u32[]{:S(2)}, u32[]{:S(2)}) %collective-permute-start.25) | collective-permute-done | bytes 524320 | tf_op jit(solution)/shard_map/ppermute | solution.py:71
  514.3 8.5 %weight_grad.7 = (bf16[512,768]{1,0:T(8,128)(2,1)}, bf16[512,768]{1,0:T(8,128)(2,1)}, bf16[1024,768]{1,0:T(8,128)(2,1)}) custom-call(s32[8]{0:T(128)} %stack.47.order_ref, bf16[1024,2048]{1,0:T(8,128)(2,1)} %get-tuple-element.111.refs_0_.refs_1_, bf16[1024,2048]{1,0:T(8,128)(2,1)} %get-tuple-element.111.refs_0_.refs_1_, bf16[1,1024,768]{2,1,0:T(8,128)(2,1)} %bitcast.129), custom_call_target="tpu_custom_call" | custom-call | flops 3221225472 | tf_op jit(solution)/shard_map/weight_grad/pallas_call | solution.py:377
  525.3 17.6 %collective-permute-done.29 = bf16[512,768]{1,0:T(8,128)(2,1)} collective-permute-done((bf16[512,768]{1,0:T(8,128)(2,1)}, bf16[512,768]{1,0:T(8,128)(2,1)}, u32[]{:S(2)}, u32[]{:S(2)}) %collective-permute-start.29) | collective-permute-done | bytes 786464 | tf_op jit(solution)/shard_map/ppermute | solution.py:59
  (226 shorter events, 241.0 us)
Async XLA Ops:
  7.2 90.4 %all-gather.4.cloned.1.call-start = ((), (), s32[]{:S(2)}) async-start(), calls=%async_computation.11 | async-start | bytes 4718592 | tf_op jit(solution)/shard_map/all_gather | solution.py:758
  7.9 227.4 %all-gather.6.cloned.1.call-start = ((), (), s32[]{:S(2)}) async-start(), calls=%async_computation.12 | async-start | bytes 8650752 | tf_op jit(solution)/shard_map/all_gather | solution.py:766
  12.2 46.6 %all-to-all-start = ((bf16[8,64,768]{2,1,0:T(8,128)(2,1)}), bf16[8,64,768]{2,1,0:T(8,128)(2,1)S(1)}, u32[]{:S(2)}, u32[]{:S(2)}) async-start(bf16[8,64,768]{2,1,0:T(8,128)(2,1)} %maximum_bitcast_fusion.1), calls=%async_computation | async-start | bytes 1572864 | tf_op jit(solution)/shard_map/all_to_all | solution.py:125
  58.8 65.6 %all-to-all-start.1 = ((bf16[8,64,2048]{2,1,0:T(8,128)(2,1)}), bf16[8,64,2048]{2,1,0:T(8,128)(2,1)S(1)}, u32[]{:S(2)}, u32[]{:S(2)}) async-start(bf16[8,64,2048]{2,1,0:T(8,128)(2,1)} %maximum_bitcast_fusion), calls=%async_computation.1 | async-start | bytes 4194304 | tf_op jit(solution)/shard_map/all_to_all | solution.py:125
  124.5 46.3 %all-to-all-start.2 = ((bf16[8,64,1024]{2,1,0:T(8,128)(2,1)}), bf16[8,64,1024]{2,1,0:T(8,128)(2,1)S(1)}, u32[]{:S(2)}, u32[]{:S(2)}) async-start(bf16[8,64,1024]{2,1,0:T(8,128)(2,1)} %bitcast.86), calls=%async_computation.2 | async-start | bytes 2097152 | tf_op jit(solution)/shard_map/all_to_all | solution.py:125
  128.2 63.1 %collective-permute-start.4 = (bf16[512,2048]{1,0:T(8,128)(2,1)S(1)}, bf16[512,2048]{1,0:T(8,128)(2,1)}, u32[]{:S(2)}, u32[]{:S(2)}) collective-permute-start(bf16[512,2048]{1,0:T(8,128)(2,1)S(1)} %bitcast.95), channel_id=1, source_target_pairs={{0,8},{8,0},{16,24},{24,16},{1,9},{9,1},{17,25},{25,17},{2,10},{10... | collective-permute-start | bytes 6291464 | tf_op jit(solution)/shard_map/ppermute | solution.py:43
  129.6 64.5 %collective-permute-start.6 = (bf16[512,2048]{1,0:T(8,128)(2,1)S(1)}, bf16[512,2048]{1,0:T(8,128)(2,1)}, u32[]{:S(2)}, u32[]{:S(2)}) collective-permute-start(bf16[512,2048]{1,0:T(8,128)(2,1)S(1)} %bitcast.96), channel_id=1, source_target_pairs={{0,16},{8,24},{16,0},{24,8},{1,17},{9,25},{17,1},{25,9},{2,18},{10... | collective-permute-start | bytes 6291464 | tf_op jit(solution)/shard_map/ppermute | solution.py:44
  170.8 59.9 %all-to-all-start.3 = ((bf16[4,1024,256]{2,1,0:T(8,128)(2,1)}), bf16[4,1024,256]{2,1,0:T(8,128)(2,1)}, u32[]{:S(2)}, u32[]{:S(2)}) async-start(bf16[4,1024,256]{2,1,0:T(8,128)(2,1)} %attend.1), calls=%async_computation.3 | async-start | bytes 4194304 | tf_op jit(solution)/shard_map/all_to_all | solution.py:84
  175.2 102.5 %all-gather.8.cloned.1.call-start = ((), (), s32[]{:S(2)}) async-start(), calls=%async_computation.13 | async-start | bytes 4718592 | tf_op jit(solution)/shard_map/all_gather | solution.py:800
  230.8 25.6 %collective-permute-start.10 = (bf16[512,1024]{1,0:T(8,128)(2,1)S(1)}, bf16[512,1024]{1,0:T(8,128)(2,1)S(1)}, u32[]{:S(2)}, u32[]{:S(2)}) collective-permute-start(bf16[512,1024]{1,0:T(8,128)(2,1)S(1)} %bitcast.108), channel_id=1, source_target_pairs={{0,16},{8,24},{16,0},{24,8},{1,17},{9,25},{17,1},{25,9},{2,18},{10... | collective-permute-start | bytes 3145736 | tf_op jit(solution)/shard_map/ppermute | solution.py:44
  232.3 25.9 %collective-permute-start.9 = (bf16[512,1024]{1,0:T(8,128)(2,1)S(1)}, bf16[512,1024]{1,0:T(8,128)(2,1)S(1)}, u32[]{:S(2)}, u32[]{:S(2)}) collective-permute-start(bf16[512,1024]{1,0:T(8,128)(2,1)S(1)} %bitcast.109), channel_id=1, source_target_pairs={{0,8},{8,0},{16,24},{24,16},{1,9},{9,1},{17,25},{25,17},{2,10},{10... | collective-permute-start | bytes 3145736 | tf_op jit(solution)/shard_map/ppermute | solution.py:43
  314.9 52.8 %all-to-all-start.4 = ((bf16[4,128,2048]{2,1,0:T(8,128)(2,1)}), bf16[4,128,2048]{2,1,0:T(8,128)(2,1)S(1)}, u32[]{:S(2)}, u32[]{:S(2)}) async-start(bf16[4,128,2048]{2,1,0:T(8,128)(2,1)} %fusion), calls=%async_computation.4 | async-start | bytes 4194304 | tf_op jit(solution)/shard_map/all_to_all | solution.py:104
  331.5 25.5 %collective-permute-start.14 = (bf16[512,1024]{1,0:T(8,128)(2,1)}, bf16[512,1024]{1,0:T(8,128)(2,1)S(1)}, u32[]{:S(2)}, u32[]{:S(2)}) collective-permute-start(bf16[512,1024]{1,0:T(8,128)(2,1)} %get-tuple-element.87), channel_id=1, source_target_pairs={{0,8},{8,0},{16,24},{24,16},{1,9},{9,1},{17,25},{25,17},{2,10},{10... | collective-permute-start | bytes 3145736 | tf_op jit(solution)/shard_map/ppermute | solution.py:59
  332.9 25.3 %collective-permute-start.15 = (bf16[512,1024]{1,0:T(8,128)(2,1)}, bf16[512,1024]{1,0:T(8,128)(2,1)}, u32[]{:S(2)}, u32[]{:S(2)}) collective-permute-start(bf16[512,1024]{1,0:T(8,128)(2,1)} %get-tuple-element.88), channel_id=1, source_target_pairs={{0,16},{8,24},{16,0},{24,8},{1,17},{9,25},{17,1},{25,9},{2,18},{10... | collective-permute-start | bytes 3145736 | tf_op jit(solution)/shard_map/ppermute | solution.py:60
  377.5 30.1 %all-to-all-start.5 = ((bf16[128,8,512]{0,2,1:T(8,128)(2,1)}), bf16[128,8,512]{0,2,1:T(8,128)(2,1)S(1)}, u32[]{:S(2)}, u32[]{:S(2)}) async-start(bf16[128,8,512]{0,2,1:T(8,128)(2,1)} %pad_maximum_fusion), calls=%async_computation.5 | async-start | bytes 2097152 | tf_op jit(solution)/shard_map/all_to_all | solution.py:832
  381.1 224.3 %reduce-scatter.3.cloned.1.call-start = ((), (), s32[]{:S(2)}) async-start(), calls=%async_computation.14 | async-start | bytes 4718592 | tf_op jit(solution)/shard_map/reduce_scatter | solution.py:838
  410.6 41.1 %collective-permute-start.20 = (bf16[512,1024]{1,0:T(8,128)(2,1)}, bf16[512,1024]{1,0:T(8,128)(2,1)}, u32[]{:S(2)}, u32[]{:S(2)}) collective-permute-start(bf16[512,1024]{1,0:T(8,128)(2,1)} %get-tuple-element.104), channel_id=1, source_target_pairs={{0,16},{8,24},{16,0},{24,8},{1,17},{9,25},{17,1},{25,9},{2,18},{10... | collective-permute-start | bytes 3145736 | tf_op jit(solution)/shard_map/ppermute | solution.py:60
  412.1 39.6 %collective-permute-start.18 = (bf16[512,1024]{1,0:T(8,128)(2,1)}, bf16[512,1024]{1,0:T(8,128)(2,1)}, u32[]{:S(2)}, u32[]{:S(2)}) collective-permute-start(bf16[512,1024]{1,0:T(8,128)(2,1)} %get-tuple-element.102), channel_id=1, source_target_pairs={{0,8},{8,0},{16,24},{24,16},{1,9},{9,1},{17,25},{25,17},{2,10},{10... | collective-permute-start | bytes 3145736 | tf_op jit(solution)/shard_map/ppermute | solution.py:59
  416.7 41.4 %collective-permute-start.24 = (bf16[512,1024]{1,0:T(8,128)(2,1)}, bf16[512,1024]{1,0:T(8,128)(2,1)}, u32[]{:S(2)}, u32[]{:S(2)}) collective-permute-start(bf16[512,1024]{1,0:T(8,128)(2,1)} %get-tuple-element.108), channel_id=1, source_target_pairs={{0,16},{8,24},{16,0},{24,8},{1,17},{9,25},{17,1},{25,9},{2,18},{10... | collective-permute-start | bytes 3145736 | tf_op jit(solution)/shard_map/ppermute | solution.py:60
  417.3 41.9 %collective-permute-start.22 = (bf16[512,1024]{1,0:T(8,128)(2,1)}, bf16[512,1024]{1,0:T(8,128)(2,1)S(1)}, u32[]{:S(2)}, u32[]{:S(2)}) collective-permute-start(bf16[512,1024]{1,0:T(8,128)(2,1)} %get-tuple-element.106), channel_id=1, source_target_pairs={{0,8},{8,0},{16,24},{24,16},{1,9},{9,1},{17,25},{25,17},{2,10},{10... | collective-permute-start | bytes 3145736 | tf_op jit(solution)/shard_map/ppermute | solution.py:59
  418.2 47.5 %all-to-all-start.6 = ((bf16[8,64,1024]{2,1,0:T(8,128)(2,1)}), bf16[8,64,1024]{2,1,0:T(8,128)(2,1)S(1)}, u32[]{:S(2)}, u32[]{:S(2)}) async-start(bf16[8,64,1024]{2,1,0:T(8,128)(2,1)} %bitcast.27), calls=%async_computation.7 | async-start | bytes 2097152 | tf_op jit(solution)/shard_map/all_to_all | solution.py:731
  421.8 183.6 %reduce-scatter.5.cloned.1.call-start = ((), (), s32[]{:S(2)}) async-start(), calls=%async_computation.15 | async-start | bytes 4718592 | tf_op jit(solution)/shard_map/reduce_scatter | solution.py:851
  510.7 65.5 %all-to-all-start.7 = ((bf16[8,64,2048]{2,1,0:T(8,128)(2,1)}), bf16[8,64,2048]{2,1,0:T(8,128)(2,1)S(1)}, u32[]{:S(2)}, u32[]{:S(2)}) async-start(bf16[8,64,2048]{2,1,0:T(8,128)(2,1)} %bitcast.88), calls=%async_computation.8 | async-start | bytes 4194304 | tf_op jit(solution)/shard_map/all_to_all | solution.py:731
  523.8 28.7 %collective-permute-start.30 = (bf16[512,768]{1,0:T(8,128)(2,1)}, bf16[512,768]{1,0:T(8,128)(2,1)S(1)}, u32[]{:S(2)}, u32[]{:S(2)}) collective-permute-start(bf16[512,768]{1,0:T(8,128)(2,1)} %get-tuple-element.119), channel_id=1, source_target_pairs={{0,16},{8,24},{16,0},{24,8},{1,17},{9,25},{17,1},{25,9},{2,18},{10... | collective-permute-start | bytes 2359304 | tf_op jit(solution)/shard_map/ppermute | solution.py:60
  (55 other events, 740.7 us)
Sparse Core Ops, SparseCore 0:
  9.6 77.6 all-gather.3
  90.3 113.3 all-gather.5
  230.8 46.7 all-gather.7
  410.7 65.7 reduce-scatter.2
  478.6 65.4 reduce-scatter.4

commit v6 on v5

--- a/solution.py
+++ b/solution.py
@@ -878,6 +878,7 @@
         d_first - first_own * jnp.mean(d_first * first_own, axis=-1, keepdims=True)
     )
 
+    rows_qkv = after(rows_qkv, layer_out, grad_tokens)
     (grad_down,), unused = finish(rows_down, gain_m, (), 1)
     (grad_gate, grad_up), grad_gain_mlp = finish(rows_two, gain_m, (w_gate, w_up), 2)
     (grad_query, grad_key, grad_value), grad_gain_attn = finish(

time: 625 us -> 621 us (level)
  transfers between devices with their start and end apart: 47 -> 47, of which waited for: 30 -> 30; matrix products, arithmetic and copies ran while one was open for 9% -> 9% of each run, Pallas kernels for 24% -> 23%
where the time goes in v6:
time: 621 us; the launch traced here: 612 us
  waiting for transfers between devices  264 us (43%)
  Pallas kernels  174 us (28%)
  starting transfers between devices  80.6 us (13%)
  other arithmetic  46.1 us (7%)
  local copies, waits for them, and re-layouts  24.1 us (4%)
  between operations  14.5 us (2%)
  matrix products  8.26 us (1%)
    all_to_all x3, waiting for transfers between devices, to_columns(): landed = lax.all_to_all(pieces, 'ctx', 0, 0, tiled=True)  81.6 us
    pallas_call x4, Pallas kernels, weight_grad(): pl.pallas_call(functools.partial(weight_grad_kernel, outs, len(pairs)), g...  39 us
    pallas_call x3, Pallas kernels, times_rows(): pl.pallas_call(functools.partial(times_rows_kernel, units, chips), grid_s...  37.5 us
    ppermute x3, waiting for transfers between devices, near(): lax.ppermute(block, 'fsdp', flip('fsdp', 4, 1))  33.8 us
    ppermute x4, waiting for transfers between devices, reduce_far(): lax.ppermute(send_y, 'fsdp', flip('fsdp', 4, 2))  23.5 us
    pallas_call x1, Pallas kernels, attend_back(): pl.pallas_call(functools.partial(attend_back_kernel, heads), grid_spec=pl...  19.9 us
    ppermute x3, waiting for transfers between devices, far(): lax.ppermute(from_x[:half], 'fsdp', flip('fsdp', 4, 2))  19.9 us
    ppermute x4, waiting for transfers between devices, reduce_near(): lax.ppermute(part[0], 'fsdp', flip('fsdp', 4, 1))  19 us
  transfers between devices with their start and end apart: 47, of which 30 were waited for; matrix products, arithmetic and copies ran while one was open for 9% of the time, Pallas kernels for 23%

profile of v6, /device:TPU:0, one launch (start us, length us, event | category | flops | bytes accessed | tf_op | source)
XLA Modules:
  0.0 612.1 jit_solution(11442320697469203835)
XLA Ops:
  21.4 37.5 %all-to-all-done = bf16[8,64,768]{2,1,0:T(8,128)(2,1)S(1)} async-done(((bf16[8,64,768]{2,1,0:T(8,128)(2,1)}), bf16[8,64,768]{2,1,0:T(8,128)(2,1)S(1)}, u32[]{:S(2)}, u32[]{:S(2)}) %all-to-all-start) | async-done | bytes 786464 | tf_op jit(solution)/shard_map/all_to_all | solution.py:125
  66.9 16.6 %collective-permute-done.refs_1_ = bf16[512,768]{1,0:T(8,128)(2,1)} collective-permute-done((bf16[512,768]{1,0:T(8,128)(2,1)S(1)}, bf16[512,768]{1,0:T(8,128)(2,1)}, u32[]{:S(2)}, u32[]{:S(2)}) %collective-permute-start) | collective-permute-done | bytes 786464 | tf_op jit(solution)/shard_map/ppermute | solution.py:43
  98.4 10.2 %project.1 = (bf16[1024,2048]{1,0:T(8,128)(2,1)}, bf16[1024,768]{1,0:T(8,128)(2,1)}) custom-call(s32[8]{0:T(128)} %stack.46.places_ref, bf16[1024,2048]{1,0:T(8,128)(2,1)} %all-gather.4.cloned.1.call-done.x_ref, f32[1024,256]{1,0:T(8,128)} %bitcast.106, f32[1024,256]{1,0:T(8,128)} %bitcast.104, bf16[512,768]{1,0:T(8,128)(2,1)} %bitcast.122, ...), custom_call_target="tpu_custom_call" | custom-call | flops 8999999488 | tf_op jit(solution)/shard_map/project/pallas_call | solution.py:177
  108.7 10.6 %attend.1 = bf16[4,1024,256]{2,1,0:T(8,128)(2,1)} custom-call(s32[4]{0:T(128)} %and_select_fusion.2.lo_ref, s32[1,1024]{1,0:T(1,128)} %bitcast.124, bf16[1024,768]{1,0:T(8,128)(2,1)} %get-tuple-element.73.q_ref.k_ref.v_ref, bf16[1024,768]{1,0:T(8,128)(2,1)} %get-tuple-element.73.q_ref.k_ref.v_ref, bf16[1024,768]{1,0:T(8,128)(2,1)} %get-tuple-element.73.q_ref.k_ref.v_ref), custom_call_target="tpu_custom_call" | custom-call | flops 10000000000 | tf_op jit(solution)/shard_map/attend/pallas_call | solution.py:450
  132.2 38.0 %all-to-all-done.2 = bf16[8,64,1024]{2,1,0:T(8,128)(2,1)S(1)} async-done(((bf16[8,64,1024]{2,1,0:T(8,128)(2,1)}), bf16[8,64,1024]{2,1,0:T(8,128)(2,1)S(1)}, u32[]{:S(2)}, u32[]{:S(2)}) %all-to-all-start.2) | async-done | bytes 1048608 | tf_op jit(solution)/shard_map/all_to_all | solution.py:125
  174.7 17.1 %collective-permute-done.4.refs_1_.refs_6_ = bf16[512,2048]{1,0:T(8,128)(2,1)} collective-permute-done((bf16[512,2048]{1,0:T(8,128)(2,1)S(1)}, bf16[512,2048]{1,0:T(8,128)(2,1)}, u32[]{:S(2)}, u32[]{:S(2)}) %collective-permute-start.4) | collective-permute-done | bytes 2097184 | tf_op jit(solution)/shard_map/ppermute | solution.py:43
  198.0 19.9 %collective-permute-done.5.refs_3_.refs_8_ = bf16[256,2048]{1,0:T(8,128)(2,1)S(1)} collective-permute-done((bf16[256,2048]{1,0:T(8,128)(2,1)S(1)}, bf16[256,2048]{1,0:T(8,128)(2,1)S(1)}, u32[]{:S(2)}, u32[]{:S(2)}) %collective-permute-start.5) | collective-permute-done | bytes 1048608 | tf_op jit(solution)/shard_map/ppermute | solution.py:52
  220.7 10.4 %all-to-all-done.3.own_ref = bf16[4,1024,256]{2,1,0:T(8,128)(2,1)} async-done(((bf16[4,1024,256]{2,1,0:T(8,128)(2,1)}), bf16[4,1024,256]{2,1,0:T(8,128)(2,1)}, u32[]{:S(2)}, u32[]{:S(2)}) %all-to-all-start.3) | async-done | bytes 2097184 | tf_op jit(solution)/shard_map/all_to_all | solution.py:84
  235.7 17.4 %blend.1 = (bf16[1024,2048]{1,0:T(8,128)(2,1)}, f32[1024,2048]{1,0:T(8,128)}, bf16[1024,2048]{1,0:T(8,128)(2,1)}) custom-call(s32[1]{0:T(128)} %bitcast.core_ref, bf16[1024,2048]{1,0:T(8,128)(2,1)} %all-gather.4.cloned.1.call-done.x_ref, bf16[4,1024,256]{2,1,0:T(8,128)(2,1)} %all-to-all-done.3.own_ref, ...), custom_call_target="tpu_custom_call" | custom-call | flops 15000000512 | tf_op jit(solution)/shard_map/blend/pallas_call | solution.py:613
  260.1 15.6 %open_units.1 = (f32[1024,1024]{1,0:T(8,128)}, f32[1024,1024]{1,0:T(8,128)}, bf16[1024,1024]{1,0:T(8,128)(2,1)}) custom-call(s32[8]{0:T(128)} %stack.46.places_ref, bf16[1024,2048]{1,0:T(8,128)(2,1)} %get-tuple-element.92.left_ref.refs_0_.refs_1_, bf16[512,2048]{1,0:T(8,128)(2,1)} %bitcast.97, bf16[512,2048]{1,0:T(8,128)(2,1)} %collective-permute-done.4.refs_1_.refs_6_, ...), custom_call_target="tpu_custom_call" | custom-call | flops 12000000000 | tf_op jit(solution)/shard_map/open_units/pallas_call | solution.py:224
  277.7 12.7 %close_units.1.left_ref = bf16[2,1024,1024]{2,1,0:T(8,128)(2,1)} custom-call(s32[8]{0:T(128)} %stack.46.places_ref, bf16[1024,2048]{1,0:T(8,128)(2,1)} %all-gather.8.cloned.1.call-done.back_ref.refs_0_.refs_1_, f32[1024,1024]{1,0:T(8,128)} %get-tuple-element.82.gate_ref, f32[1024,1024]{1,0:T(8,128)} %get-tuple-element.83.up_ref, ...), custom_call_target="tpu_custom_call" | custom-call | flops 7000000000 | tf_op jit(solution)/shard_map/close_units/pallas_call | solution.py:264
  290.4 16.3 %times_rows.3 = bf16[2,4,128,2048]{3,2,1,0:T(8,128)(2,1)} custom-call(s32[8]{0:T(128)} %stack.46.places_ref, s32[1]{0:T(128)} %bitcast.core_ref, bf16[2,1024,1024]{2,1,0:T(8,128)(2,1)} %close_units.1.left_ref, bf16[512,2048]{1,0:T(8,128)(2,1)} %bitcast.99, bf16[512,2048]{1,0:T(8,128)(2,1)} %collective-permute-done.4.refs_1_.refs_6_, ...), custom_call_target="tpu_custom_call" | custom-call | flops 8589934592 | tf_op jit(solution)/shard_map/times_rows/pallas_call | solution.py:329
  321.0 10.5 %weight_grad.4 = (bf16[512,1024]{1,0:T(8,128)(2,1)}, bf16[512,1024]{1,0:T(8,128)(2,1)}, bf16[1024,1024]{1,0:T(8,128)(2,1)}) custom-call(s32[8]{0:T(128)} %stack.47.order_ref, bf16[1024,2048]{1,0:T(8,128)(2,1)} %all-gather.8.cloned.1.call-done.back_ref.refs_0_.refs_1_, bf16[1024,2048]{1,0:T(8,128)(2,1)} %all-gather.8.cloned.1.call-done.back_ref.refs_0_.refs_1_, ...), custom_call_target="tpu_custom_call" | custom-call | flops 4294967296 | tf_op jit(solution)/shard_map/weight_grad/pallas_call | solution.py:377
  336.9 10.0 %weight_grad.5 = (bf16[512,1024]{1,0:T(8,128)(2,1)}, bf16[512,1024]{1,0:T(8,128)(2,1)}, bf16[1024,1024]{1,0:T(8,128)(2,1)}) custom-call(s32[8]{0:T(128)} %stack.47.order_ref, bf16[1024,2048]{1,0:T(8,128)(2,1)} %get-tuple-element.92.left_ref.refs_0_.refs_1_, bf16[1024,2048]{1,0:T(8,128)(2,1)} %get-tuple-element.92.left_ref.refs_0_.refs_1_, ...), custom_call_target="tpu_custom_call" | custom-call | flops 4294967296 | tf_op jit(solution)/shard_map/weight_grad/pallas_call | solution.py:377
  346.9 10.0 %weight_grad.6 = (bf16[512,1024]{1,0:T(8,128)(2,1)}, bf16[512,1024]{1,0:T(8,128)(2,1)}, bf16[1024,1024]{1,0:T(8,128)(2,1)}) custom-call(s32[8]{0:T(128)} %stack.47.order_ref, bf16[1024,2048]{1,0:T(8,128)(2,1)} %get-tuple-element.92.left_ref.refs_0_.refs_1_, bf16[1024,2048]{1,0:T(8,128)(2,1)} %get-tuple-element.92.left_ref.refs_0_.refs_1_, ...), custom_call_target="tpu_custom_call" | custom-call | flops 4294967296 | tf_op jit(solution)/shard_map/weight_grad/pallas_call | solution.py:377
  358.3 9.5 %all-to-all-done.4 = bf16[4,128,2048]{2,1,0:T(8,128)(2,1)S(1)} async-done(((bf16[4,128,2048]{2,1,0:T(8,128)(2,1)}), bf16[4,128,2048]{2,1,0:T(8,128)(2,1)S(1)}, u32[]{:S(2)}, u32[]{:S(2)}) %all-to-all-start.4) | async-done | bytes 2097184 | tf_op jit(solution)/shard_map/all_to_all | solution.py:104
  386.8 11.2 %times_rows.4 = bf16[1024,2048]{1,0:T(8,128)(2,1)} custom-call(s32[8]{0:T(128)} %stack.46.places_ref, s32[1]{0:T(128)} %bitcast.core_ref, bf16[1,1024,1024]{2,1,0:T(8,128)(2,1)} %bitcast.127, bf16[512,1024]{1,0:T(8,128)(2,1)} %bitcast.111, bf16[512,1024]{1,0:T(8,128)(2,1)} %copy-done.20, bf16[512,1024]{1,0:T(8,128)(2,1)} %copy-done.19, ...), custom_call_target="tpu_custom_call" | custom-call | flops 4294967296 | tf_op jit(solution)/shard_map/times_rows/pallas_call | solution.py:329
  398.1 9.6 %all-to-all-done.5 = bf16[128,8,512]{0,2,1:T(8,128)(2,1)S(1)} async-done(((bf16[128,8,512]{0,2,1:T(8,128)(2,1)}), bf16[128,8,512]{0,2,1:T(8,128)(2,1)S(1)}, u32[]{:S(2)}, u32[]{:S(2)}) %all-to-all-start.5) | async-done | bytes 1048608 | tf_op jit(solution)/shard_map/all_to_all | solution.py:832
  421.9 19.9 %attend_back.1 = bf16[1024,768]{1,0:T(8,128)(2,1)} custom-call(s32[4]{0:T(128)} %and_select_fusion.2.lo_ref, s32[1,1024]{1,0:T(1,128)} %bitcast.125, bf16[1024,768]{1,0:T(8,128)(2,1)} %get-tuple-element.73.q_ref.k_ref.v_ref, bf16[1024,768]{1,0:T(8,128)(2,1)} %get-tuple-element.73.q_ref.k_ref.v_ref, bf16[1024,768]{1,0:T(8,128)(2,1)} %get-tuple-element.73.q_ref.k_ref.v_ref, ...), custom_call_target="tpu_custom_call" | custom-call | flops 20000000000 | tf_op jit(solution)/shard_map/attend_back/pallas_call | solution.py:566
  441.7 10.0 %times_rows.5 = bf16[1024,2048]{1,0:T(8,128)(2,1)} custom-call(s32[8]{0:T(128)} %stack.46.places_ref, s32[1]{0:T(128)} %bitcast.core_ref, bf16[1,1024,768]{2,1,0:T(8,128)(2,1)} %bitcast.128, bf16[512,768]{1,0:T(8,128)(2,1)} %bitcast.123, bf16[512,768]{1,0:T(8,128)(2,1)} %collective-permute-done.refs_1_, bf16[512,768]{1,0:T(8,128)(2,1)} %collective-permute-done.1.refs_2_, ...), custom_call_target="tpu_custom_call" | custom-call | flops 3221225472 | tf_op jit(solution)/shard_map/times_rows/pallas_call | solution.py:329
  471.7 11.5 %collective-permute-done.19 = bf16[256,1024]{1,0:T(8,128)(2,1)S(1)} collective-permute-done((bf16[256,1024]{1,0:T(8,128)(2,1)S(1)}, bf16[256,1024]{1,0:T(8,128)(2,1)S(1)}, u32[]{:S(2)}, u32[]{:S(2)}) %collective-permute-start.19) | collective-permute-done | bytes 524320 | tf_op jit(solution)/shard_map/ppermute | solution.py:70
  498.1 9.8 %collective-permute-done.25 = bf16[256,1024]{1,0:T(8,128)(2,1)S(1)} collective-permute-done((bf16[256,1024]{1,0:T(8,128)(2,1)S(1)}, bf16[256,1024]{1,0:T(8,128)(2,1)S(1)}, u32[]{:S(2)}, u32[]{:S(2)}) %collective-permute-start.25) | collective-permute-done | bytes 524320 | tf_op jit(solution)/shard_map/ppermute | solution.py:71
  514.3 8.5 %weight_grad.7 = (bf16[512,768]{1,0:T(8,128)(2,1)}, bf16[512,768]{1,0:T(8,128)(2,1)}, bf16[1024,768]{1,0:T(8,128)(2,1)}) custom-call(s32[8]{0:T(128)} %stack.47.order_ref, bf16[1024,2048]{1,0:T(8,128)(2,1)} %get-tuple-element.112.refs_0_.refs_1_, bf16[1024,2048]{1,0:T(8,128)(2,1)} %get-tuple-element.112.refs_0_.refs_1_, bf16[1,1024,768]{2,1,0:T(8,128)(2,1)} %bitcast.129), custom_call_target="tpu_custom_call" | custom-call | flops 3221225472 | tf_op jit(solution)/shard_map/weight_grad/pallas_call | solution.py:377
  525.3 17.7 %collective-permute-done.29 = bf16[512,768]{1,0:T(8,128)(2,1)} collective-permute-done((bf16[512,768]{1,0:T(8,128)(2,1)}, bf16[512,768]{1,0:T(8,128)(2,1)}, u32[]{:S(2)}, u32[]{:S(2)}) %collective-permute-start.29) | collective-permute-done | bytes 786464 | tf_op jit(solution)/shard_map/ppermute | solution.py:59
  (222 shorter events, 237.2 us)
Async XLA Ops:
  7.2 90.5 %all-gather.4.cloned.1.call-start = ((), (), s32[]{:S(2)}) async-start(), calls=%async_computation.11 | async-start | bytes 4718592 | tf_op jit(solution)/shard_map/all_gather | solution.py:758
  7.9 227.8 %all-gather.6.cloned.1.call-start = ((), (), s32[]{:S(2)}) async-start(), calls=%async_computation.12 | async-start | bytes 8650752 | tf_op jit(solution)/shard_map/all_gather | solution.py:766
  12.3 46.6 %all-to-all-start = ((bf16[8,64,768]{2,1,0:T(8,128)(2,1)}), bf16[8,64,768]{2,1,0:T(8,128)(2,1)S(1)}, u32[]{:S(2)}, u32[]{:S(2)}) async-start(bf16[8,64,768]{2,1,0:T(8,128)(2,1)} %maximum_bitcast_fusion.1), calls=%async_computation | async-start | bytes 1572864 | tf_op jit(solution)/shard_map/all_to_all | solution.py:125
  58.9 66.4 %all-to-all-start.1 = ((bf16[8,64,2048]{2,1,0:T(8,128)(2,1)}), bf16[8,64,2048]{2,1,0:T(8,128)(2,1)S(1)}, u32[]{:S(2)}, u32[]{:S(2)}) async-start(bf16[8,64,2048]{2,1,0:T(8,128)(2,1)} %maximum_bitcast_fusion), calls=%async_computation.1 | async-start | bytes 4194304 | tf_op jit(solution)/shard_map/all_to_all | solution.py:125
  125.3 44.9 %all-to-all-start.2 = ((bf16[8,64,1024]{2,1,0:T(8,128)(2,1)}), bf16[8,64,1024]{2,1,0:T(8,128)(2,1)S(1)}, u32[]{:S(2)}, u32[]{:S(2)}) async-start(bf16[8,64,1024]{2,1,0:T(8,128)(2,1)} %bitcast.86), calls=%async_computation.2 | async-start | bytes 2097152 | tf_op jit(solution)/shard_map/all_to_all | solution.py:125
  128.9 63.0 %collective-permute-start.4 = (bf16[512,2048]{1,0:T(8,128)(2,1)S(1)}, bf16[512,2048]{1,0:T(8,128)(2,1)}, u32[]{:S(2)}, u32[]{:S(2)}) collective-permute-start(bf16[512,2048]{1,0:T(8,128)(2,1)S(1)} %bitcast.95), channel_id=1, source_target_pairs={{0,8},{8,0},{16,24},{24,16},{1,9},{9,1},{17,25},{25,17},{2,10},{10... | collective-permute-start | bytes 6291464 | tf_op jit(solution)/shard_map/ppermute | solution.py:43
  130.5 64.4 %collective-permute-start.6 = (bf16[512,2048]{1,0:T(8,128)(2,1)S(1)}, bf16[512,2048]{1,0:T(8,128)(2,1)}, u32[]{:S(2)}, u32[]{:S(2)}) collective-permute-start(bf16[512,2048]{1,0:T(8,128)(2,1)S(1)} %bitcast.96), channel_id=1, source_target_pairs={{0,16},{8,24},{16,0},{24,8},{1,17},{9,25},{17,1},{25,9},{2,18},{10... | collective-permute-start | bytes 6291464 | tf_op jit(solution)/shard_map/ppermute | solution.py:44
  170.2 60.8 %all-to-all-start.3 = ((bf16[4,1024,256]{2,1,0:T(8,128)(2,1)}), bf16[4,1024,256]{2,1,0:T(8,128)(2,1)}, u32[]{:S(2)}, u32[]{:S(2)}) async-start(bf16[4,1024,256]{2,1,0:T(8,128)(2,1)} %attend.1), calls=%async_computation.3 | async-start | bytes 4194304 | tf_op jit(solution)/shard_map/all_to_all | solution.py:84
  174.7 103.0 %all-gather.8.cloned.1.call-start = ((), (), s32[]{:S(2)}) async-start(), calls=%async_computation.13 | async-start | bytes 4718592 | tf_op jit(solution)/shard_map/all_gather | solution.py:800
  231.2 25.6 %collective-permute-start.10 = (bf16[512,1024]{1,0:T(8,128)(2,1)S(1)}, bf16[512,1024]{1,0:T(8,128)(2,1)S(1)}, u32[]{:S(2)}, u32[]{:S(2)}) collective-permute-start(bf16[512,1024]{1,0:T(8,128)(2,1)S(1)} %bitcast.108), channel_id=1, source_target_pairs={{0,16},{8,24},{16,0},{24,8},{1,17},{9,25},{17,1},{25,9},{2,18},{10... | collective-permute-start | bytes 3145736 | tf_op jit(solution)/shard_map/ppermute | solution.py:44
  232.8 25.5 %collective-permute-start.9 = (bf16[512,1024]{1,0:T(8,128)(2,1)S(1)}, bf16[512,1024]{1,0:T(8,128)(2,1)S(1)}, u32[]{:S(2)}, u32[]{:S(2)}) collective-permute-start(bf16[512,1024]{1,0:T(8,128)(2,1)S(1)} %bitcast.109), channel_id=1, source_target_pairs={{0,8},{8,0},{16,24},{24,16},{1,9},{9,1},{17,25},{25,17},{2,10},{10... | collective-permute-start | bytes 3145736 | tf_op jit(solution)/shard_map/ppermute | solution.py:43
  315.0 52.9 %all-to-all-start.4 = ((bf16[4,128,2048]{2,1,0:T(8,128)(2,1)}), bf16[4,128,2048]{2,1,0:T(8,128)(2,1)S(1)}, u32[]{:S(2)}, u32[]{:S(2)}) async-start(bf16[4,128,2048]{2,1,0:T(8,128)(2,1)} %fusion), calls=%async_computation.4 | async-start | bytes 4194304 | tf_op jit(solution)/shard_map/all_to_all | solution.py:104
  331.5 25.5 %collective-permute-start.14 = (bf16[512,1024]{1,0:T(8,128)(2,1)}, bf16[512,1024]{1,0:T(8,128)(2,1)S(1)}, u32[]{:S(2)}, u32[]{:S(2)}) collective-permute-start(bf16[512,1024]{1,0:T(8,128)(2,1)} %get-tuple-element.88), channel_id=1, source_target_pairs={{0,8},{8,0},{16,24},{24,16},{1,9},{9,1},{17,25},{25,17},{2,10},{10... | collective-permute-start | bytes 3145736 | tf_op jit(solution)/shard_map/ppermute | solution.py:59
  333.0 25.4 %collective-permute-start.15 = (bf16[512,1024]{1,0:T(8,128)(2,1)}, bf16[512,1024]{1,0:T(8,128)(2,1)}, u32[]{:S(2)}, u32[]{:S(2)}) collective-permute-start(bf16[512,1024]{1,0:T(8,128)(2,1)} %get-tuple-element.89), channel_id=1, source_target_pairs={{0,16},{8,24},{16,0},{24,8},{1,17},{9,25},{17,1},{25,9},{2,18},{10... | collective-permute-start | bytes 3145736 | tf_op jit(solution)/shard_map/ppermute | solution.py:60
  377.6 30.1 %all-to-all-start.5 = ((bf16[128,8,512]{0,2,1:T(8,128)(2,1)}), bf16[128,8,512]{0,2,1:T(8,128)(2,1)S(1)}, u32[]{:S(2)}, u32[]{:S(2)}) async-start(bf16[128,8,512]{0,2,1:T(8,128)(2,1)} %pad_maximum_fusion), calls=%async_computation.5 | async-start | bytes 2097152 | tf_op jit(solution)/shard_map/all_to_all | solution.py:832
  381.1 212.0 %reduce-scatter.3.cloned.1.call-start = ((), (), s32[]{:S(2)}) async-start(), calls=%async_computation.14 | async-start | bytes 4718592 | tf_op jit(solution)/shard_map/reduce_scatter | solution.py:838
  410.6 41.1 %collective-permute-start.20 = (bf16[512,1024]{1,0:T(8,128)(2,1)}, bf16[512,1024]{1,0:T(8,128)(2,1)}, u32[]{:S(2)}, u32[]{:S(2)}) collective-permute-start(bf16[512,1024]{1,0:T(8,128)(2,1)} %get-tuple-element.105), channel_id=1, source_target_pairs={{0,16},{8,24},{16,0},{24,8},{1,17},{9,25},{17,1},{25,9},{2,18},{10... | collective-permute-start | bytes 3145736 | tf_op jit(solution)/shard_map/ppermute | solution.py:60
  412.1 39.6 %collective-permute-start.18 = (bf16[512,1024]{1,0:T(8,128)(2,1)}, bf16[512,1024]{1,0:T(8,128)(2,1)}, u32[]{:S(2)}, u32[]{:S(2)}) collective-permute-start(bf16[512,1024]{1,0:T(8,128)(2,1)} %get-tuple-element.103), channel_id=1, source_target_pairs={{0,8},{8,0},{16,24},{24,16},{1,9},{9,1},{17,25},{25,17},{2,10},{10... | collective-permute-start | bytes 3145736 | tf_op jit(solution)/shard_map/ppermute | solution.py:59
  416.8 41.4 %collective-permute-start.24 = (bf16[512,1024]{1,0:T(8,128)(2,1)}, bf16[512,1024]{1,0:T(8,128)(2,1)}, u32[]{:S(2)}, u32[]{:S(2)}) collective-permute-start(bf16[512,1024]{1,0:T(8,128)(2,1)} %get-tuple-element.109), channel_id=1, source_target_pairs={{0,16},{8,24},{16,0},{24,8},{1,17},{9,25},{17,1},{25,9},{2,18},{10... | collective-permute-start | bytes 3145736 | tf_op jit(solution)/shard_map/ppermute | solution.py:60
  417.3 41.9 %collective-permute-start.22 = (bf16[512,1024]{1,0:T(8,128)(2,1)}, bf16[512,1024]{1,0:T(8,128)(2,1)S(1)}, u32[]{:S(2)}, u32[]{:S(2)}) collective-permute-start(bf16[512,1024]{1,0:T(8,128)(2,1)} %get-tuple-element.107), channel_id=1, source_target_pairs={{0,8},{8,0},{16,24},{24,16},{1,9},{9,1},{17,25},{25,17},{2,10},{10... | collective-permute-start | bytes 3145736 | tf_op jit(solution)/shard_map/ppermute | solution.py:59
  418.3 47.5 %all-to-all-start.6 = ((bf16[8,64,1024]{2,1,0:T(8,128)(2,1)}), bf16[8,64,1024]{2,1,0:T(8,128)(2,1)S(1)}, u32[]{:S(2)}, u32[]{:S(2)}) async-start(bf16[8,64,1024]{2,1,0:T(8,128)(2,1)} %bitcast.27), calls=%async_computation.7 | async-start | bytes 2097152 | tf_op jit(solution)/shard_map/all_to_all | solution.py:731
  421.8 171.3 %reduce-scatter.5.cloned.1.call-start = ((), (), s32[]{:S(2)}) async-start(), calls=%async_computation.15 | async-start | bytes 4718592 | tf_op jit(solution)/shard_map/reduce_scatter | solution.py:851
  510.7 65.5 %all-to-all-start.7 = ((bf16[8,64,2048]{2,1,0:T(8,128)(2,1)}), bf16[8,64,2048]{2,1,0:T(8,128)(2,1)S(1)}, u32[]{:S(2)}, u32[]{:S(2)}) async-start(bf16[8,64,2048]{2,1,0:T(8,128)(2,1)} %bitcast.88), calls=%async_computation.8 | async-start | bytes 4194304 | tf_op jit(solution)/shard_map/all_to_all | solution.py:731
  523.9 28.7 %collective-permute-start.30 = (bf16[512,768]{1,0:T(8,128)(2,1)}, bf16[512,768]{1,0:T(8,128)(2,1)S(1)}, u32[]{:S(2)}, u32[]{:S(2)}) collective-permute-start(bf16[512,768]{1,0:T(8,128)(2,1)} %get-tuple-element.120), channel_id=1, source_target_pairs={{0,16},{8,24},{16,0},{24,8},{1,17},{9,25},{17,1},{25,9},{2,18},{10... | collective-permute-start | bytes 2359304 | tf_op jit(solution)/shard_map/ppermute | solution.py:60
  (53 other events, 708.8 us)
Sparse Core Ops, SparseCore 0:
  9.6 77.7 all-gather.3
  90.4 113.8 all-gather.5
  231.2 46.3 all-gather.7
  410.7 65.7 reduce-scatter.2
  478.6 65.4 reduce-scatter.4
